TPU v7x, 128 devices: a whole 4x4x4 slice. The times are simulated.
128 devices in a mesh: section: 2 (over x_hi), mp: 4 (over x_lo, core), dp: 16 (over z, y).
Axes of the slice: x: 4 (x_hi: 2, x_lo: 2; x = x_hi * 2 + x_lo), y: 4, z: 4, core: 2. Of those that a mesh axis runs over, the one named last changes fastest.
Arguments:
- embeds: bfloat16 [2, 256, 8192], P('section', 'mp', 'dp'), may hold values from -6 to 6
- cotangent: bfloat16 [2, 256, 8192], P('section', 'mp', 'dp'), may hold values from -6 to 6
- norm_gain: float32 [1, 2, 8192], P(None, 'section', 'dp'), may hold values from 0.25 to 1.75
- w_query: bfloat16 [1, 2, 8192, 8192], P(None, 'section', 'dp', 'mp')
- w_keyval: bfloat16 [1, 2, 8192, 2, 1024], P(None, 'section', 'dp', None, 'mp')
- w_out: bfloat16 [1, 2, 8192, 8192], P(None, 'section', 'mp', 'dp'), may hold values from -0.0625 to 0.0625
- seq_lengths: int32 [2, 3], replicated, may hold values from 1 to 128, 256 in all within a row
- image_mask: int32 [2, 32], P('section'), may hold values from 0 to 1
- block_owner: int32 [2, 32], P('section'), may hold values from 0 to 31, as said below
- merger_weight: bfloat16 [5120, 8192], P('mp', 'dp'), may hold values from -0.078125 to 0.078125
- merger_pre: bfloat16 [32, 2, 2, 8, 5120], P(('section', 'dp'), None, None, None, 'mp'), may hold values from -5 to 5
Outputs:
- input_grad: bfloat16 [2, 256, 8192], P('section', 'mp', 'dp')
- merger_pre_grad: float32 [32, 2, 2, 8, 5120], P(('section', 'dp'), None, None, None, 'mp')
Inputs may be any that keep to these rules, and one draw needn't show every extreme that they name: `block_owner`: within one micro-batch at most 2 image blocks have the same owner; some owner has exactly 2 image blocks in every micro-batch.
All inputs are finite; a program needn't handle non-finite values.
Results may differ from a plain program's by a relative error of at most 0.029.
Values may be sent and summed in bfloat16 or wider, within the bound.
No kernel may reach another device: no remote copies, remote signals or barrier semaphores. Data moves between devices by JAX's collectives and lax.ppermute only.
A program may use at most 128 MiB of HBM per device.

v0:
```python
import math

import jax
import jax.numpy as jnp
from jax import lax
from jax.sharding import PartitionSpec as P

MODEL_WIDTH = 8192
HEAD_SIZE = 128
CAP = 2
VB = 8


EPSILON = 1e-06
MASKED = -1e30


def passed_along(shard, axis, by):
    size = lax.axis_size(axis)
    return lax.ppermute(shard, axis, [(i, (i + by) % size) for i in range(size)])


def build_masks(seq_lengths, tokens):
    bounds = jnp.cumsum(seq_lengths, axis=1)
    places = jnp.arange(tokens, dtype=jnp.int32)
    segment = jnp.sum((places[None, :, None] >= bounds[:, None, :]).astype(jnp.int32), axis=2)
    causal = places[None, :] <= places[:, None]
    return (segment[:, :, None] == segment[:, None, :]) & causal[None]


def split_heads(query, keys, values):
    tokens = query.shape[0]
    groups = keys.shape[1] // HEAD_SIZE
    group_size = query.shape[1] // keys.shape[1]
    return (
        query.reshape(tokens, groups, group_size, HEAD_SIZE),
        keys.reshape(tokens, groups, HEAD_SIZE),
        values.reshape(tokens, groups, HEAD_SIZE),
    )


def head_weights(query_heads, key_heads, allowed):
    scores = jnp.einsum(
        "qhgd,khd->hgqk", query_heads, key_heads, preferred_element_type=jnp.float32
    )
    scores = jnp.where(allowed[None, None], scores * (1.0 / math.sqrt(HEAD_SIZE)), MASKED)
    largest = jnp.max(scores, axis=-1, keepdims=True)
    raised = jnp.exp(scores - largest)
    return raised / jnp.sum(raised, axis=-1, keepdims=True)


def attend(query, keys, values, allowed):
    query_heads, key_heads, value_heads = split_heads(query, keys, values)
    weights = head_weights(query_heads, key_heads, allowed)
    mixture = jnp.einsum(
        "hgqk,khd->qhgd",
        weights.astype(jnp.bfloat16),
        value_heads,
        preferred_element_type=jnp.float32,
    )
    return mixture.reshape(query.shape[0], -1).astype(jnp.bfloat16)


def attend_back(query, keys, values, head_grad, allowed):
    query_heads, key_heads, value_heads = split_heads(query, keys, values)
    weights = head_weights(query_heads, key_heads, allowed)
    grad_heads = head_grad.reshape(query_heads.shape)
    value_grad = jnp.einsum(
        "hgqk,qhgd->khd",
        weights.astype(jnp.bfloat16),
        grad_heads,
        preferred_element_type=jnp.float32,
    )
    weight_grad = jnp.einsum(
        "qhgd,khd->hgqk", grad_heads, value_heads, preferred_element_type=jnp.float32
    )
    centred = weight_grad - jnp.sum(weight_grad * weights, axis=-1, keepdims=True)
    score_grad = (weights * centred * (1.0 / math.sqrt(HEAD_SIZE))).astype(jnp.bfloat16)
    query_grad = jnp.einsum(
        "hgqk,khd->qhgd", score_grad, key_heads, preferred_element_type=jnp.float32
    )
    key_grad = jnp.einsum(
        "hgqk,qhgd->khd", score_grad, query_heads, preferred_element_type=jnp.float32
    )
    tokens = query.shape[0]
    return jnp.concatenate(
        [
            query_grad.reshape(tokens, -1),
            key_grad.reshape(tokens, -1),
            value_grad.reshape(tokens, -1),
        ],
        axis=1,
    )


def gelu_slope(values):
    cumulative = 0.5 * (1.0 + lax.erf(values * (1.0 / math.sqrt(2.0))))
    return cumulative + values * jnp.exp(-0.5 * values * values) * (1.0 / math.sqrt(2.0 * math.pi))


def store(buffer, entry_value, layer_slot, micro_batch, active):
    previous = buffer[layer_slot, micro_batch]
    return buffer.at[layer_slot, micro_batch].set(jnp.where(active, entry_value, previous))


def contract_last(left, right):
    return lax.dot_general(
        left, right, (((1,), (1,)), ((), ())), preferred_element_type=jnp.float32
    )


def local(
    embeds,
    cotangent,
    norm_gain,
    w_query,
    w_keyval,
    w_out,
    seq_lengths,
    image_mask,
    block_owner,
    merger_weight,
    merger_pre,
):
    sections = lax.axis_size("section")
    section_index = lax.axis_index("section")
    rows = embeds.shape[1]
    width = embeds.shape[2]
    tokens = rows * lax.axis_size("mp")
    layer_slots = w_query.shape[0]
    q_cols = w_query.shape[3]
    keyvalue_columns = w_keyval.shape[4]
    w_joined = jnp.concatenate(
        [w_query[:, 0], w_keyval[:, 0].reshape(layer_slots, width, 2 * keyvalue_columns)], axis=2
    )
    joined_cols = w_joined.shape[2]
    gains = norm_gain[:, 0]
    out_weights = w_out[:, 0]
    allowed_all = build_masks(seq_lengths, tokens)
    steps = (layer_slots + 1) * sections - 1

    def forward_step(step_index, carry):
        resident, stash_qkv, stash_scale = carry
        micro_batch = (section_index - step_index) % sections
        entry = (sections - micro_batch) % sections
        progress = step_index - entry
        active = (progress >= 0) & (progress < layer_slots * sections)
        layer_slot = jnp.clip(progress // sections, 0, layer_slots - 1)
        gathered = lax.all_gather(resident, "mp", axis=0, tiled=True)
        gathered_f = gathered.astype(jnp.float32)
        normed = (gathered_f * gains[layer_slot]).astype(jnp.bfloat16)
        partial_proj = jnp.dot(normed, w_joined[layer_slot], preferred_element_type=jnp.float32)
        squares = jnp.sum(gathered_f * gathered_f, axis=1)
        projected, square_sum = lax.psum((partial_proj, squares), "dp")
        scale_rows = lax.rsqrt(square_sum / MODEL_WIDTH + EPSILON)
        qkv = (projected * scale_rows[:, None]).astype(jnp.bfloat16)
        attended = attend(
            qkv[:, :q_cols],
            qkv[:, q_cols : q_cols + keyvalue_columns],
            qkv[:, q_cols + keyvalue_columns :],
            allowed_all[micro_batch],
        )
        out_matrix = out_weights[layer_slot]
        added = lax.psum_scatter(
            jnp.dot(attended, out_matrix, preferred_element_type=jnp.float32),
            "mp",
            scatter_dimension=0,
            tiled=True,
        )
        updated = (resident.astype(jnp.float32) + added).astype(jnp.bfloat16)
        kept = jnp.where(active, updated, resident)
        stash_qkv = store(stash_qkv, qkv, layer_slot, micro_batch, active)
        stash_scale = store(stash_scale, scale_rows, layer_slot, micro_batch, active)
        moved = passed_along(kept, "section", 1)
        return (moved, stash_qkv, stash_scale)

    start_carry = (
        embeds[0],
        jnp.zeros((layer_slots, sections, tokens, joined_cols), jnp.bfloat16),
        jnp.zeros((layer_slots, sections, tokens), jnp.float32),
    )
    finished = lax.fori_loop(0, steps, forward_step, start_carry)
    stash_qkv, stash_scale = (finished[1], finished[2])

    def backward_step(step_index, grad_rows):
        micro_batch = (section_index + step_index) % sections
        entry = (micro_batch + 1) % sections
        progress = step_index - entry
        active = (progress >= 0) & (progress < layer_slots * sections)
        layer_slot = layer_slots - 1 - jnp.clip(progress // sections, 0, layer_slots - 1)
        out_matrix = out_weights[layer_slot]
        partial_heads = contract_last(
            lax.all_gather(grad_rows, "mp", axis=0, tiled=True), out_matrix
        )
        head_grad = lax.psum(partial_heads.astype(jnp.bfloat16), "dp")
        qkv = stash_qkv[layer_slot, micro_batch]
        scale_rows = stash_scale[layer_slot, micro_batch]
        grads = attend_back(
            qkv[:, :q_cols],
            qkv[:, q_cols : q_cols + keyvalue_columns],
            qkv[:, q_cols + keyvalue_columns :],
            head_grad,
            allowed_all[micro_batch],
        )
        scaled = (grads * scale_rows[:, None]).astype(jnp.bfloat16)
        joined = w_joined[layer_slot]
        through = lax.psum_scatter(
            contract_last(scaled, joined).astype(jnp.bfloat16),
            "mp",
            scatter_dimension=0,
            tiled=True,
        ).astype(jnp.float32)
        updated = (grad_rows.astype(jnp.float32) + gains[layer_slot] * through).astype(jnp.bfloat16)
        kept = jnp.where(active, updated, grad_rows)
        return passed_along(kept, "section", -1)

    grad_rows = lax.fori_loop(0, steps, backward_step, cotangent[0])
    landing = steps % sections
    grad_rows = passed_along(grad_rows, "section", landing)
    hidden_part = contract_last(lax.all_gather(grad_rows, "mp", axis=0, tiled=True), merger_weight)
    hidden_cols = merger_weight.shape[0]
    block_count = tokens // VB
    hidden_blocks = hidden_part.reshape(block_count, VB * hidden_cols)
    owners = block_owner[0]
    marks = image_mask[0]
    positions = jnp.arange(block_count, dtype=jnp.int32)
    earlier = (
        (owners[:, None] == owners[None, :])
        & (marks[None, :] == 1)
        & (positions[None, :] < positions[:, None])
    )
    slots = jnp.sum(earlier.astype(jnp.int32), axis=1)
    dp_count = lax.axis_size("dp")
    owner_count = sections * dp_count
    target = owners * CAP + slots
    targets_all = jnp.arange(owner_count * CAP, dtype=jnp.int32)
    selector = ((targets_all[:, None] == target[None, :]) & (marks[None, :] == 1)).astype(
        jnp.float32
    )
    outgoing = jnp.dot(selector, hidden_blocks, precision=lax.Precision.HIGHEST)
    outgoing = outgoing.reshape(owner_count, CAP, VB, hidden_cols)
    arrived = lax.all_to_all(
        outgoing.astype(jnp.bfloat16), ("section", "dp"), split_axis=0, concat_axis=0, tiled=True
    ).astype(outgoing.dtype)
    hidden_grad = jnp.sum(arrived.reshape(sections, dp_count, CAP, VB, hidden_cols), axis=1)
    merger_grad = gelu_slope(merger_pre[0].astype(jnp.float32)) * hidden_grad
    return (grad_rows[None], merger_grad[None])


def solution(mesh):
    placed = (
        P("section", "mp", "dp"),
        P("section", "mp", "dp"),
        P(None, "section", "dp"),
        P(None, "section", "dp", "mp"),
        P(None, "section", "dp", None, "mp"),
        P(None, "section", "mp", "dp"),
        P(),
        P("section", None),
        P("section", None),
        P("mp", "dp"),
        P(("section", "dp"), None, None, None, "mp"),
    )
    return jax.shard_map(
        local,
        mesh=mesh,
        in_specs=placed,
        out_specs=(P("section", "mp", "dp"), P(("section", "dp"), None, None, None, "mp")),
        check_vma=False,
    )
```

profile of v0, /device:TPU:6, one launch (start us, length us, event | category | flops | bytes accessed | tf_op | source)
XLA Modules:
  0.0 932.0 jit_solution(12699139617132982599)
XLA Ops:
  17.2 416.9 %while.36 = (s32[]{:T(128)}, bf16[64,512]{1,0:T(8,128)(2,1)S(1)}, bf16[1,2,256,2560]{3,2,1,0:T(8,128)(2,1)}, f32[1,2,256]{2,1,0:T(2,128)S(1)}, s32[]{:T(128)}, /...) while((s32[]{:T(128)}, bf16[64,512]{1,0:T(8,128)(2,1)S(1)}, ...), condition=%wide.region_11.12_spmd, body=%wide.region_2.11_spmd.sunk | while | flops 1757938944 | bytes 71224312 | solution.py:182
  17.2 5.8 all_gather.26
  27.4 42.4 %psum.46 = f32[256]{0:T(256)S(1)} all-reduce(f32[256]{0:T(256)S(1)} %fusion.142), channel_id=1, replica_groups=mesh['section'=2,'mp'=4,'dp'=16] {'dp'}, use_global_device_ids=true, to_apply=%region_5.5 | all-reduce | flops 256 | bytes 2048 | tf_op jit(solution)/shard_map/while/body/eval_jaxpr/psum | solution.py:154
  73.4 49.2 %all-reduce.3.cloned.1.call-done = f32[256,2560]{1,0:T(8,128)} async-done(((f32[256,2560]{1,0:T(8,128)}), f32[256,2560]{1,0:T(8,128)}) %all-reduce.3.cloned.1.call-update) | async-done | bytes 2621456 | tf_op jit(solution)/shard_map/while/body/eval_jaxpr/psum | solution.py:154
  133.8 15.9 %reduce-scatter.3.cloned.1.call-done = f32[64,512]{1,0:T(8,128)} async-done(((f32[256,512]{1,0:T(8,128)}), f32[64,512]{1,0:T(8,128)}) %reduce-scatter.3.cloned.1.call-update) | async-done | bytes 131088 | tf_op jit(solution)/shard_map/while/body/eval_jaxpr/reduce_scatter | solution.py:164
  156.7 5.8 all_gather.26
  166.9 41.0 %psum.46 = f32[256]{0:T(256)S(1)} all-reduce(f32[256]{0:T(256)S(1)} %fusion.142), channel_id=1, replica_groups=mesh['section'=2,'mp'=4,'dp'=16] {'dp'}, use_global_device_ids=true, to_apply=%region_5.5 | all-reduce | flops 256 | bytes 2048 | tf_op jit(solution)/shard_map/while/body/eval_jaxpr/psum | solution.py:154
  211.4 49.9 %all-reduce.3.cloned.1.call-done = f32[256,2560]{1,0:T(8,128)} async-done(((f32[256,2560]{1,0:T(8,128)}), f32[256,2560]{1,0:T(8,128)}) %all-reduce.3.cloned.1.call-update) | async-done | bytes 2621456 | tf_op jit(solution)/shard_map/while/body/eval_jaxpr/psum | solution.py:154
  272.4 15.9 %reduce-scatter.3.cloned.1.call-done = f32[64,512]{1,0:T(8,128)} async-done(((f32[256,512]{1,0:T(8,128)}), f32[64,512]{1,0:T(8,128)}) %reduce-scatter.3.cloned.1.call-update) | async-done | bytes 131088 | tf_op jit(solution)/shard_map/while/body/eval_jaxpr/reduce_scatter | solution.py:164
  295.3 5.8 all_gather.26
  305.5 41.0 %psum.46 = f32[256]{0:T(256)S(1)} all-reduce(f32[256]{0:T(256)S(1)} %fusion.142), channel_id=1, replica_groups=mesh['section'=2,'mp'=4,'dp'=16] {'dp'}, use_global_device_ids=true, to_apply=%region_5.5 | all-reduce | flops 256 | bytes 2048 | tf_op jit(solution)/shard_map/while/body/eval_jaxpr/psum | solution.py:154
  350.1 49.9 %all-reduce.3.cloned.1.call-done = f32[256,2560]{1,0:T(8,128)} async-done(((f32[256,2560]{1,0:T(8,128)}), f32[256,2560]{1,0:T(8,128)}) %all-reduce.3.cloned.1.call-update) | async-done | bytes 2621456 | tf_op jit(solution)/shard_map/while/body/eval_jaxpr/psum | solution.py:154
  411.1 15.9 %reduce-scatter.3.cloned.1.call-done = f32[64,512]{1,0:T(8,128)} async-done(((f32[256,512]{1,0:T(8,128)}), f32[64,512]{1,0:T(8,128)}) %reduce-scatter.3.cloned.1.call-update) | async-done | bytes 131088 | tf_op jit(solution)/shard_map/while/body/eval_jaxpr/reduce_scatter | solution.py:164
  434.0 441.9 %while.37 = (s32[]{:T(128)}, bf16[64,512]{1,0:T(8,128)(2,1)}, s32[]{:T(128)}, f32[1,512]{1,0:T(1,128)S(1)}, bf16[1,2,256,2560]{3,2,1,0:T(8,128)(2,1)}, /*index=5...) while((s32[]{:T(128)}, bf16[64,512]{1,0:T(8,128)(2,1)}, ...), condition=%wide.region_18.19_spmd, body=%wide.region_12.18_spmd.sunk | while | flops 2575115008 | bytes 93656784 | solution.py:217
  434.0 6.0 all_gather.27
  454.6 78.2 %all-reduce.5.cloned.1.call-done = bf16[256,2,8,128]{3,0,2,1:T(8,128)(2,1)} async-done(((bf16[256,2,8,128]{3,0,2,1:T(8,128)(2,1)}), bf16[256,2,8,128]{3,0,2,1:T(8,128)(2,1)}) %all-reduce.5.cloned.1.call-update) | async-done | bytes 1048592 | tf_op jit(solution)/shard_map/while/body/eval_jaxpr/psum | solution.py:195
  536.9 7.2 fusion.167
  544.1 8.7 fusion.168
  558.1 15.8 %reduce-scatter.5.cloned.1.call-done = bf16[64,512]{1,0:T(8,128)(2,1)} async-done(((bf16[256,512]{1,0:T(8,128)(2,1)}), bf16[64,512]{1,0:T(8,128)(2,1)}) %reduce-scatter.5.cloned.1.call-update) | async-done | bytes 65552 | tf_op jit(solution)/shard_map/while/body/eval_jaxpr/reduce_scatter | solution.py:207
  581.4 6.0 all_gather.27
  601.9 78.2 %all-reduce.5.cloned.1.call-done = bf16[256,2,8,128]{3,0,2,1:T(8,128)(2,1)} async-done(((bf16[256,2,8,128]{3,0,2,1:T(8,128)(2,1)}), bf16[256,2,8,128]{3,0,2,1:T(8,128)(2,1)}) %all-reduce.5.cloned.1.call-update) | async-done | bytes 1048592 | tf_op jit(solution)/shard_map/while/body/eval_jaxpr/psum | solution.py:195
  684.1 7.2 fusion.167
  691.4 8.7 fusion.168
  705.4 15.8 %reduce-scatter.5.cloned.1.call-done = bf16[64,512]{1,0:T(8,128)(2,1)} async-done(((bf16[256,512]{1,0:T(8,128)(2,1)}), bf16[64,512]{1,0:T(8,128)(2,1)}) %reduce-scatter.5.cloned.1.call-update) | async-done | bytes 65552 | tf_op jit(solution)/shard_map/while/body/eval_jaxpr/reduce_scatter | solution.py:207
  728.6 6.0 all_gather.27
  749.2 78.2 %all-reduce.5.cloned.1.call-done = bf16[256,2,8,128]{3,0,2,1:T(8,128)(2,1)} async-done(((bf16[256,2,8,128]{3,0,2,1:T(8,128)(2,1)}), bf16[256,2,8,128]{3,0,2,1:T(8,128)(2,1)}) %all-reduce.5.cloned.1.call-update) | async-done | bytes 1048592 | tf_op jit(solution)/shard_map/while/body/eval_jaxpr/psum | solution.py:195
  831.4 7.2 fusion.167
  838.7 8.7 fusion.168
  852.6 15.8 %reduce-scatter.5.cloned.1.call-done = bf16[64,512]{1,0:T(8,128)(2,1)} async-done(((bf16[256,512]{1,0:T(8,128)(2,1)}), bf16[64,512]{1,0:T(8,128)(2,1)}) %reduce-scatter.5.cloned.1.call-update) | async-done | bytes 65552 | tf_op jit(solution)/shard_map/while/body/eval_jaxpr/reduce_scatter | solution.py:207
  881.9 5.8 all_gather.23
  893.8 10.2 %all-to-all-start = ((bf16[32,2,8,1280]{3,2,1,0:T(8,128)(2,1)}), bf16[32,2,8,1280]{3,2,1,0:T(8,128)(2,1)S(1)}, u32[]{:S(2)}, u32[]{:S(2)}) async-start(bf16[32,2,8,1280]{3,2,1,0:T(8,128)(2,1)} %copy.90), calls=%async_computation.2 | async-start | bytes 2621440 | tf_op jit(solution)/shard_map/all_to_all | solution.py:242
  904.0 19.6 %all-to-all-done = bf16[32,2,8,1280]{3,2,1,0:T(8,128)(2,1)S(1)} async-done(((bf16[32,2,8,1280]{3,2,1,0:T(8,128)(2,1)}), bf16[32,2,8,1280]{3,2,1,0:T(8,128)(2,1)S(1)}, u32[]{:S(2)}, u32[]{:S(2)}) %all-to-all-start) | async-done | bytes 1310752 | tf_op jit(solution)/shard_map/all_to_all | solution.py:242
  (244 shorter events, 195.3 us)
Async XLA Ops:
  7.2 880.5 %copy-start = (bf16[1280,512]{1,0:T(8,128)(2,1)S(1)}, bf16[1280,512]{1,0:T(8,128)(2,1)}, u32[]{:S(2)}) copy-start(bf16[1280,512]{1,0:T(8,128)(2,1)} %param.28) | copy-start | bytes 3932164
  17.2 10.0 %copy-start.7 = (bf16[64,512]{1,0:T(8,128)(2,1)}, bf16[64,512]{1,0:T(8,128)(2,1)S(1)}, u32[]{:S(2)}) copy-start(bf16[64,512]{1,0:T(8,128)(2,1)S(1)} %get-tuple-element.733) | copy-start | bytes 196612 | tf_op jit(solution)/shard_map/while
  17.2 105.4 %all-reduce.3.cloned.1.call-start = ((), (), s32[]{:S(2)}) async-start(), calls=%async_computation.3 | async-start | bytes 5242880 | tf_op jit(solution)/shard_map/while/body/eval_jaxpr/psum | solution.py:154
  27.2 122.5 %reduce-scatter.3.cloned.1.call-start = ((), (), s32[]{:S(2)}) async-start(), calls=%async_computation.4 | async-start | bytes 655360 | tf_op jit(solution)/shard_map/while/body/eval_jaxpr/reduce_scatter | solution.py:164
  150.7 6.0 collective-permute-start
  156.7 9.9 %copy-start.7 = (bf16[64,512]{1,0:T(8,128)(2,1)}, bf16[64,512]{1,0:T(8,128)(2,1)S(1)}, u32[]{:S(2)}) copy-start(bf16[64,512]{1,0:T(8,128)(2,1)S(1)} %get-tuple-element.733) | copy-start | bytes 196612 | tf_op jit(solution)/shard_map/while
  156.7 104.6 %all-reduce.3.cloned.1.call-start = ((), (), s32[]{:S(2)}) async-start(), calls=%async_computation.3 | async-start | bytes 5242880 | tf_op jit(solution)/shard_map/while/body/eval_jaxpr/psum | solution.py:154
  166.6 121.7 %reduce-scatter.3.cloned.1.call-start = ((), (), s32[]{:S(2)}) async-start(), calls=%async_computation.4 | async-start | bytes 655360 | tf_op jit(solution)/shard_map/while/body/eval_jaxpr/reduce_scatter | solution.py:164
  289.3 6.0 collective-permute-start
  295.3 9.9 %copy-start.7 = (bf16[64,512]{1,0:T(8,128)(2,1)}, bf16[64,512]{1,0:T(8,128)(2,1)S(1)}, u32[]{:S(2)}) copy-start(bf16[64,512]{1,0:T(8,128)(2,1)S(1)} %get-tuple-element.733) | copy-start | bytes 196612 | tf_op jit(solution)/shard_map/while
  295.3 104.6 %all-reduce.3.cloned.1.call-start = ((), (), s32[]{:S(2)}) async-start(), calls=%async_computation.3 | async-start | bytes 5242880 | tf_op jit(solution)/shard_map/while/body/eval_jaxpr/psum | solution.py:154
  305.2 121.8 %reduce-scatter.3.cloned.1.call-start = ((), (), s32[]{:S(2)}) async-start(), calls=%async_computation.4 | async-start | bytes 655360 | tf_op jit(solution)/shard_map/while/body/eval_jaxpr/reduce_scatter | solution.py:164
  428.0 6.0 collective-permute-start
  434.0 442.8 %copy-start.16 = (s32[1,32]{1,0:T(1,128)S(1)}, s32[1,32]{1,0:T(1,128)}, u32[]{:S(2)}) copy-start(s32[1,32]{1,0:T(1,128)} %param.26) | copy-start | bytes 388
  434.0 442.8 %copy-start.15 = (s32[1,32]{1,0:T(1,128)S(1)}, s32[1,32]{1,0:T(1,128)}, u32[]{:S(2)}) copy-start(s32[1,32]{1,0:T(1,128)} %param.27) | copy-start | bytes 388
  434.0 98.8 %all-reduce.5.cloned.1.call-start = ((), (), s32[]{:S(2)}) async-start(), calls=%async_computation.5 | async-start | bytes 2097152 | tf_op jit(solution)/shard_map/while/body/eval_jaxpr/psum | solution.py:195
  443.9 130.0 %reduce-scatter.5.cloned.1.call-start = ((), (), s32[]{:S(2)}) async-start(), calls=%async_computation.6 | async-start | bytes 327680 | tf_op jit(solution)/shard_map/while/body/eval_jaxpr/reduce_scatter | solution.py:207
  556.4 17.5 %copy-start.5 = (bf16[64,512]{1,0:T(8,128)(2,1)S(1)}, bf16[64,512]{1,0:T(8,128)(2,1)}, u32[]{:S(2)}) copy-start(bf16[64,512]{1,0:T(8,128)(2,1)} %get-tuple-element.777) | copy-start | bytes 196612 | tf_op jit(solution)/shard_map/while
  574.8 6.0 collective-permute-start.1
  581.4 98.8 %all-reduce.5.cloned.1.call-start = ((), (), s32[]{:S(2)}) async-start(), calls=%async_computation.5 | async-start | bytes 2097152 | tf_op jit(solution)/shard_map/while/body/eval_jaxpr/psum | solution.py:195
  591.2 130.0 %reduce-scatter.5.cloned.1.call-start = ((), (), s32[]{:S(2)}) async-start(), calls=%async_computation.6 | async-start | bytes 327680 | tf_op jit(solution)/shard_map/while/body/eval_jaxpr/reduce_scatter | solution.py:207
  691.4 8.7 copy-start.4
  703.7 17.5 %copy-start.5 = (bf16[64,512]{1,0:T(8,128)(2,1)S(1)}, bf16[64,512]{1,0:T(8,128)(2,1)}, u32[]{:S(2)}) copy-start(bf16[64,512]{1,0:T(8,128)(2,1)} %get-tuple-element.777) | copy-start | bytes 196612 | tf_op jit(solution)/shard_map/while
  722.0 5.9 collective-permute-start.1
  728.6 98.8 %all-reduce.5.cloned.1.call-start = ((), (), s32[]{:S(2)}) async-start(), calls=%async_computation.5 | async-start | bytes 2097152 | tf_op jit(solution)/shard_map/while/body/eval_jaxpr/psum | solution.py:195
  738.5 130.0 %reduce-scatter.5.cloned.1.call-start = ((), (), s32[]{:S(2)}) async-start(), calls=%async_computation.6 | async-start | bytes 327680 | tf_op jit(solution)/shard_map/while/body/eval_jaxpr/reduce_scatter | solution.py:207
  838.7 8.7 copy-start.4
  851.0 17.4 %copy-start.5 = (bf16[64,512]{1,0:T(8,128)(2,1)S(1)}, bf16[64,512]{1,0:T(8,128)(2,1)}, u32[]{:S(2)}) copy-start(bf16[64,512]{1,0:T(8,128)(2,1)} %get-tuple-element.777) | copy-start | bytes 196612 | tf_op jit(solution)/shard_map/while
  869.3 5.9 collective-permute-start.1
  875.9 6.0 collective-permute-start.2
  893.8 30.0 %copy-start.12 = (bf16[1,2,2,8,1280]{4,3,2,1,0:T(8,128)(2,1)S(1)}, bf16[1,2,2,8,1280]{4,3,2,1,0:T(8,128)(2,1)}, u32[]{:S(2)}) copy-start(bf16[1,2,2,8,1280]{4,3,2,1,0:T(8,128)(2,1)} %param.29) | copy-start | bytes 245764
  893.8 29.8 %all-to-all-start = ((bf16[32,2,8,1280]{3,2,1,0:T(8,128)(2,1)}), bf16[32,2,8,1280]{3,2,1,0:T(8,128)(2,1)S(1)}, u32[]{:S(2)}, u32[]{:S(2)}) async-start(bf16[32,2,8,1280]{3,2,1,0:T(8,128)(2,1)} %copy.90), calls=%async_computation.2 | async-start | bytes 2621440 | tf_op jit(solution)/shard_map/all_to_all | solution.py:242
  (28 other events, 69.9 us)
Sparse Core Ops, SparseCore 0:
  27.3 95.2 all-reduce.2
  133.2 16.4 reduce-scatter.2
  166.8 94.4 all-reduce.2
  271.8 16.4 reduce-scatter.2
  305.4 94.4 all-reduce.2
  410.5 16.4 reduce-scatter.2
  444.0 88.7 all-reduce.4
  558.2 15.6 reduce-scatter.4
  591.3 88.7 all-reduce.4
  705.5 15.6 reduce-scatter.4
  738.6 88.7 all-reduce.4
  852.8 15.6 reduce-scatter.4
where the time goes:
time: 935 us; the launch traced here: 932 us
  waiting for transfers between devices  531 us (57%)
  blocking collectives  165 us (18%)
  matrix products  118 us (13%)
  local copies, waits for them, and re-layouts  50.2 us (5%)
  other arithmetic  34.1 us (4%)
  starting transfers between devices  17.4 us (2%)
  between operations  14.1 us (2%)
    psum x3, waiting for transfers between devices, backward_step(): head_grad = lax.psum(partial_heads.astype(jnp.bfloat16), 'dp')  235 us
    psum x3, waiting for transfers between devices, forward_step(): projected, square_sum = lax.psum((partial_proj, squares), 'dp')  149 us
    psum x3, blocking collectives, forward_step(): projected, square_sum = lax.psum((partial_proj, squares), 'dp')  124 us
    reduce_scatter x3, waiting for transfers between devices, forward_step(): lax.psum_scatter(jnp.dot(attended, out_matrix, preferred_element_type=jnp...  47.7 us
    reduce_scatter x3, waiting for transfers between devices, backward_step(): lax.psum_scatter(contract_last(scaled, joined).astype(jnp.bfloat16), 'mp'...  47.4 us
    ppermute x7, waiting for transfers between devices, passed_along(): lax.ppermute(shard, axis, [(i, (i + by) % size) for i in range(size)])  32.8 us
    dot_general x3, matrix products, attend_back(): jnp.einsum('hgqk,khd->qhgd', score_grad, key_heads, preferred_element_typ...  26 us
    dot_general x3, matrix products, attend_back(): jnp.einsum('hgqk,qhgd->khd', score_grad, query_heads, preferred_element_t...  21.7 us
  transfers between devices with their start and end apart: 20, of which 20 were waited for; matrix products, arithmetic and copies ran while one was open for 5% of the time, Pallas kernels for 0%

commit v1 on v0

v1 whole, which is shorter than its diff:
```python
import functools
import math

import jax
import jax.numpy as jnp
from jax import lax
from jax.experimental import pallas as pl
from jax.experimental.pallas import tpu as pltpu
from jax.sharding import PartitionSpec as P

MODEL_WIDTH = 8192
HEAD_SIZE = 128
GROUP_HEADS = 8
CAP = 2
VB = 8
NSEQ = 3

EPSILON = 1e-06
MASKED = -1e30
SOFT = 1.0 / math.sqrt(HEAD_SIZE)
LOG2E = math.log2(math.e)
QB = 128

BF = jnp.bfloat16
F32 = jnp.float32

VMEM = pl.BlockSpec(memory_space=pltpu.VMEM)
SMEM = pl.BlockSpec(memory_space=pltpu.SMEM)
ANY = pl.BlockSpec(memory_space=pl.ANY)
HBM = pl.BlockSpec(memory_space=pltpu.HBM)


def shape_of(shape, dtype):
    return jax.ShapeDtypeStruct(shape, dtype)


def in_hbm(*arrays):
    return [pltpu.with_memory_space_constraint(array, pltpu.HBM) for array in arrays]


def params(mebibytes):
    return pltpu.CompilerParams(vmem_limit_bytes=mebibytes << 20)


def cost(flops, bytes_accessed):
    return pl.CostEstimate(flops=flops, bytes_accessed=bytes_accessed, transcendentals=0)


def dot_nn(left, right):
    return jnp.dot(left, right, preferred_element_type=F32)


def dot_nt(left, right):
    return lax.dot_general(left, right, (((1,), (1,)), ((), ())), preferred_element_type=F32)


def two_lanes(column):
    high = column.astype(BF).astype(F32)
    lane = lax.broadcasted_iota(jnp.int32, (column.shape[0], 128), 1)
    return jnp.where(lane == 0, high, jnp.where(lane == 1, column - high, 0.0)).astype(BF)


def start_columns(sources, chunks, sems):
    width, index = chunks.shape[2], 0
    for source in sources:
        for start in range(0, source.shape[1], width):
            block = source.at[:, start : start + width]
            pltpu.make_async_copy(block, chunks.at[index], sems.at[index]).start()
            index += 1


def start_rows(sources, chunks, sems):
    rows, at = chunks.shape[1], 0
    for source in sources:
        start = 0
        while start < source.shape[0]:
            index, within = at // rows, at % rows
            count = min(rows - within, source.shape[0] - start)
            block = source.at[start : start + count, :]
            place = chunks.at[index, within : within + count, :]
            pltpu.make_async_copy(block, place, sems.at[index]).start()
            start, at = start + count, at + count


def start_joined(wqs, wkv_ref, chunks, sems):
    start_columns(wqs, chunks, sems)
    last = chunks.shape[0] - 1
    pltpu.make_async_copy(wkv_ref, chunks.at[last], sems.at[last]).start()


def landed(chunks, sems, index):
    pltpu.make_async_copy(chunks.at[index], chunks.at[index], sems.at[index]).wait()
    return chunks.at[index]


def by_section(first, second):
    section = lax.axis_index("section")
    pl.when(section == 0)(first)
    pl.when(section != 0)(second)


def spans(cols):
    return [slice(start, min(start + 512, cols)) for start in range(0, cols, 512)]


def start_spans(source, target, sems):
    for index, span in enumerate(spans(target.shape[-1])):
        at = (slice(None),) * (len(target.shape) - 1) + (span,)
        pltpu.make_async_copy(source.at[at], target.at[at], sems.at[index]).start()


def wait_span(target, sems, index):
    at = (slice(None),) * (len(target.shape) - 1) + (spans(target.shape[-1])[index],)
    pltpu.make_async_copy(target.at[at], target.at[at], sems.at[index]).wait()


def sender(staged, out_ref, sems):
    owners, share, cols = staged.shape

    def put(start, tile):
        span = slice(start, start + tile.shape[1])
        staged[:, :, span] = tile.reshape(owners, share, tile.shape[1])
        index = spans(cols).index(span)
        at = (slice(None), slice(None), span)
        pltpu.make_async_copy(staged.at[at], out_ref.at[at], sems.at[index]).start()

    def finish():
        for index in range(len(spans(cols))):
            wait_span(staged, sems, index)

    return put, finish


def repeat_out(tile, out_ref, sems):
    for place in range(out_ref.shape[0]):
        pltpu.make_async_copy(tile, out_ref.at[place], sems.at[place]).start()


def repeat_wait(tile, out_ref, sems):
    for place in range(out_ref.shape[0]):
        pltpu.make_async_copy(tile, out_ref.at[place], sems.at[place]).wait()


def project_rows(rows, gain, chunks, chunk_at, put):
    rows_f = rows.astype(F32)
    normed = (rows_f * gain).astype(BF)
    count, _, width = chunks.shape
    put(count * width, two_lanes(jnp.sum(rows_f * rows_f, axis=1, keepdims=True)))
    for index in range(count):
        put(index * width, dot_nn(normed, chunk_at(index)[...]).astype(BF))


def load_kernel(joined, pieces, *refs):
    *sources, out_ref, sems = refs

    def load(refs):
        if joined:
            start_joined(refs[:-1], refs[-1], out_ref, sems)
        else:
            start_rows(refs, out_ref, sems)

    by_section(lambda: load(sources[:pieces]), lambda: load(sources[pieces:]))
    for index in range(out_ref.shape[0]):
        landed(out_ref, sems, index)


def first_kernel(
    x_ref, gain_ref, wq_ref, wkv_ref, wout_ref, out_ref, chunks, staged, sems, out_sems
):
    put, finish = sender(staged, out_ref, out_sems)
    tokens = x_ref.shape[0]

    def rows():
        return jnp.concatenate([x_ref[tokens // 2 :, :], x_ref[: tokens // 2, :]], axis=0)

    def first():
        start_joined([wq_ref], wkv_ref, chunks, sems)
        project_rows(rows(), gain_ref[...], chunks, lambda at: landed(chunks, sems, at), put)

    def second():
        start_rows([wout_ref], chunks, sems)
        count, width, _ = chunks.shape
        put(count * width, jnp.zeros((tokens, 128), BF))
        put((count - 1) * width, jnp.zeros((tokens, width), BF))
        x = rows()
        for index in range(count - 1):
            put(index * width, dot_nt(x, landed(chunks, sems, index)[...]).astype(BF))

    by_section(first, second)
    finish()


def first_load_kernel(wq_ref, wkv_ref, wout_ref, out_ref, sems):
    def wait(count):
        for index in range(count):
            landed(out_ref, sems, index)

    def first():
        start_joined([wq_ref], wkv_ref, out_ref, sems)
        wait(out_ref.shape[0])

    def second():
        start_rows([wout_ref], out_ref, sems)
        wait(out_ref.shape[0] - 1)

    by_section(first, second)


def first_own_kernel(
    mine_ref, near_ref, far_ref, cross_ref, gain_ref, chunks, out_ref, x_ref, x, staged, out_sems
):
    rank = lax.axis_index("mp")
    share = mine_ref.shape[0]
    for distance, ref in enumerate((mine_ref, near_ref, far_ref, cross_ref)):
        at = pl.multiple_of(jnp.bitwise_xor(rank, distance) * share, share)
        x[pl.ds(at, share), :] = ref[...].astype(F32)
    x_ref[...] = x[...].astype(BF)
    put, finish = sender(staged, out_ref, out_sems)
    tokens = x_ref.shape[0]
    count, width, _ = chunks.shape

    def first():
        project_rows(x_ref[...], gain_ref[...], chunks, lambda at: chunks.at[at], put)

    def second():
        put(count * width, jnp.zeros((tokens, 128), BF))
        put((count - 1) * width, jnp.zeros((tokens, width), BF))
        for index in range(count - 1):
            put(index * width, dot_nt(x_ref[...], chunks[index]).astype(BF))

    by_section(first, second)
    finish()


def chosen(first_ref, second_ref):
    return jnp.where(lax.axis_index("section") == 0, first_ref[...], second_ref[...])


def summed(pair_ref, across_ref, beside_ref):
    even = lax.axis_index("mp") % 2 == 0
    lower = jnp.where(even, across_ref[...], beside_ref[...])
    upper = jnp.where(even, beside_ref[...], across_ref[...])
    return pair_ref[...].astype(F32) + jnp.concatenate([lower, upper], axis=0).astype(F32)


def project_kernel(
    r0_ref, r1_ref, pair_ref, across_ref, beside_ref, g0_ref, g1_ref, chunks, out_ref,
    staged, out_sems,
):
    added = summed(pair_ref, across_ref, beside_ref)
    rows = (chosen(r0_ref, r1_ref).astype(F32) + added).astype(BF)
    put, finish = sender(staged, out_ref, out_sems)
    project_rows(rows, chosen(g0_ref, g1_ref), chunks, lambda at: chunks.at[at], put)
    finish()


def head_grad_kernel(
    r0_ref, r1_ref, pair_ref, across_ref, beside_ref, g0_ref, g1_ref, chunks, out_ref, rows_ref,
    staged, out_sems,
):
    added = summed(pair_ref, across_ref, beside_ref)
    rows = chosen(r0_ref, r1_ref).astype(F32) + chosen(g0_ref, g1_ref) * added
    rows_ref[...] = rows.astype(BF)
    count, width, _ = chunks.shape
    put, finish = sender(staged, out_ref, out_sems)
    for index in range(count):
        put(index * width, dot_nt(rows_ref[...], chunks[index]).astype(BF))
    finish()


def add_parts(load, count):
    total = load(0).astype(F32)
    for index in range(1, count):
        total = total + load(index).astype(F32)
    return total


def part_sums(parts, sems):
    def total(index):
        wait_span(parts, sems, index)
        span = spans(parts.shape[2])[index]
        return add_parts(lambda source: parts[source, :, span], parts.shape[0])

    return total


def scaled_sum(total, tile):
    ranges = spans(tile.shape[1])
    squares = jnp.sum(total(len(ranges) - 1), axis=1, keepdims=True)
    scale = lax.rsqrt(squares / MODEL_WIDTH + EPSILON)
    for index, span in enumerate(ranges[:-1]):
        tile[:, span] = (total(index) * scale).astype(BF)
    tile[:, ranges[-1]] = two_lanes(scale)


def plain_sum(total, tile):
    for index, span in enumerate(spans(tile.shape[1])):
        tile[:, span] = total(index).astype(BF)


def first_sum_kernel(parts_ref, out_ref, parts, sems):
    start_spans(parts_ref, parts, sems)
    total = part_sums(parts, sems)
    by_section(lambda: scaled_sum(total, out_ref), lambda: plain_sum(total, out_ref))


def sum_kernel(adder, parts_ref, out_ref, parts, tile, sems, out_sems):
    start_spans(parts_ref, parts, sems)
    adder(part_sums(parts, sems), tile)
    repeat_out(tile, out_ref, out_sems)
    repeat_wait(tile, out_ref, out_sems)


def choose_kernel(first_ref, second_ref, out_ref, sems):
    first = first_ref.at[:, : out_ref.shape[2]]
    second = second_ref.at[:, : out_ref.shape[2]]
    by_section(
        lambda: repeat_out(first, out_ref, sems), lambda: repeat_out(second, out_ref, sems)
    )
    repeat_wait(first, out_ref, sems)


def fill_bias(seq_ref, bias):
    section = lax.axis_index("section")
    tokens = bias.shape[0]
    keys = lax.broadcasted_iota(jnp.int32, (tokens, tokens), 0)
    queries = lax.broadcasted_iota(jnp.int32, (tokens, tokens), 1)
    key_segment = jnp.zeros((tokens, tokens), jnp.int32)
    query_segment = jnp.zeros((tokens, tokens), jnp.int32)
    bound = 0
    for index in range(NSEQ):
        bound = bound + seq_ref[section, index]
        key_segment = key_segment + (keys >= bound).astype(jnp.int32)
        query_segment = query_segment + (queries >= bound).astype(jnp.int32)
    allowed = (keys <= queries) & (key_segment == query_segment)
    bias[...] = jnp.where(allowed, 0.0, MASKED)


def head_columns(head):
    return slice(head * HEAD_SIZE, (head + 1) * HEAD_SIZE)


def softmax_blocks(tokens, body):
    def one_head(head, carry):
        for at in range(0, tokens, QB):
            lanes = pl.ds(pl.multiple_of(head * tokens + at, QB), QB)
            body(slice(at, at + QB), lanes, at + QB)
        return carry

    lax.fori_loop(0, GROUP_HEADS, one_head, 0, unroll=2)


def clear_unreached(target, tokens):
    for head in range(GROUP_HEADS):
        for at in range(0, tokens - QB, QB):
            lanes = slice(head * tokens + at, head * tokens + at + QB)
            target[at + QB :, lanes] = jnp.zeros((tokens - at - QB, QB), target.dtype)


def weights_of(scores, bias):
    scores = scores * (SOFT * LOG2E) + bias
    raised = jnp.exp2(scores - jnp.max(scores, axis=0, keepdims=True))
    return raised * (1.0 / jnp.sum(raised, axis=0, keepdims=True))


def start_qkv(qkv_ref, qkv, q_cols, sems):
    pltpu.make_async_copy(qkv_ref.at[:, q_cols:], qkv.at[:, q_cols:], sems.at[0]).start()
    start_groups(qkv_ref, qkv, q_cols, sems, 1)


def start_groups(source, target, q_cols, sems, first):
    width = GROUP_HEADS * HEAD_SIZE
    for group in range(q_cols // width):
        at = (slice(None), slice(group * width, (group + 1) * width))
        pltpu.make_async_copy(source.at[at], target.at[at], sems.at[first + group]).start()


def wait_group(target, sems, first, group):
    width = GROUP_HEADS * HEAD_SIZE
    at = (slice(None), slice(group * width, (group + 1) * width))
    pltpu.make_async_copy(target.at[at], target.at[at], sems.at[first + group]).wait()


def forward_kernel(seq_ref, qkv_ref, wout0_ref, *refs):
    *wout1_refs, out_ref, qkv, chunks, bias, scores, weights, attended, sems, in_sems = refs
    tokens, q_cols = attended.shape
    start_qkv(qkv_ref, qkv, q_cols, in_sems)
    by_section(
        lambda: start_rows([wout0_ref], chunks, sems),
        lambda: start_rows(wout1_refs, chunks, sems),
    )
    fill_bias(seq_ref, bias)
    clear_unreached(weights, tokens)
    groups = q_cols // (GROUP_HEADS * HEAD_SIZE)
    pltpu.make_async_copy(qkv.at[:, q_cols:], qkv.at[:, q_cols:], in_sems.at[0]).wait()
    for group in range(groups):
        at = q_cols + group * HEAD_SIZE
        keys = qkv[:, at : at + HEAD_SIZE]
        at = at + groups * HEAD_SIZE
        values_t = qkv[:, at : at + HEAD_SIZE].astype(F32).T.astype(BF)
        wait_group(qkv, in_sems, 1, group)
        for index in range(GROUP_HEADS):
            columns = head_columns(group * GROUP_HEADS + index)
            scores[:, index * tokens : (index + 1) * tokens] = dot_nt(keys, qkv[:, columns])

        def block(queries, lanes, reach):
            weights[:reach, lanes] = weights_of(
                scores[:reach, lanes], bias[:reach, queries]
            ).astype(BF)

        softmax_blocks(tokens, block)
        for index in range(GROUP_HEADS):
            columns = head_columns(group * GROUP_HEADS + index)
            mixed = dot_nn(values_t, weights[:, index * tokens : (index + 1) * tokens])
            attended[:, columns] = mixed.T.astype(BF)
    count, width, _ = chunks.shape
    out = dot_nn(attended[:, :width], landed(chunks, sems, 0)[...])
    for index in range(1, count):
        columns = slice(index * width, (index + 1) * width)
        out = out + dot_nn(attended[:, columns], landed(chunks, sems, index)[...])
    out_ref[...] = out.astype(BF)


def softmax_kernel(seq_ref, qkv_ref, out_ref, qkv, bias, scores, in_sems, out_sems):
    tokens = bias.shape[0]
    groups = out_ref.shape[0]
    q_cols = groups * GROUP_HEADS * HEAD_SIZE
    start_qkv(qkv_ref, qkv, q_cols, in_sems)
    fill_bias(seq_ref, bias)
    pltpu.make_async_copy(qkv.at[:, q_cols:], qkv.at[:, q_cols:], in_sems.at[0]).wait()
    for group in range(groups):
        at = q_cols + group * HEAD_SIZE
        keys = qkv[:, at : at + HEAD_SIZE]
        wait_group(qkv, in_sems, 1, group)
        for index in range(GROUP_HEADS):
            columns = head_columns(group * GROUP_HEADS + index)
            lanes = slice(index * tokens, (index + 1) * tokens)
            scores[group, :, lanes] = dot_nt(keys, qkv[:, columns])

        def block(queries, lanes, reach):
            scores[group, :reach, lanes] = weights_of(
                scores[group, :reach, lanes], bias[:reach, queries]
            )

        softmax_blocks(tokens, block)
        pltpu.make_async_copy(scores.at[group], out_ref.at[group], out_sems.at[group]).start()
    for group in range(groups):
        pltpu.make_async_copy(scores.at[group], out_ref.at[group], out_sems.at[group]).wait()


def backward_kernel(known, pieces, seq_ref, qkv_ref, grads_ref, *refs):
    wq0_refs, (wq1_ref, wkv0_ref, wkv1_ref, *refs) = refs[:pieces], refs[pieces:]
    known_ref, refs = (refs[0], refs[1:]) if known else (None, refs)
    (
        out_ref, qkv, grads, chunks, bias, scores, weight_grads, weights, score_grads, scaled_q,
        scaled_kv, sems, in_sems,
    ) = refs
    tokens, q_cols = grads.shape
    start_qkv(qkv_ref, qkv, q_cols, in_sems)
    groups = q_cols // (GROUP_HEADS * HEAD_SIZE)
    start_groups(grads_ref, grads, q_cols, in_sems, 1 + groups)
    stored = [
        pltpu.make_async_copy(known_ref.at[group], scores.at[group], in_sems.at[5 + group])
        for group in range(groups if known else 0)
    ]
    for copy in stored:
        copy.start()
    by_section(
        lambda: start_joined(wq0_refs, wkv0_ref, chunks, sems),
        lambda: start_joined([wq1_ref], wkv1_ref, chunks, sems),
    )
    if not known:
        fill_bias(seq_ref, bias)
    clear_unreached(weights, tokens)
    clear_unreached(score_grads, tokens)
    kv_cols = groups * HEAD_SIZE
    pltpu.make_async_copy(qkv.at[:, q_cols:], qkv.at[:, q_cols:], in_sems.at[0]).wait()
    scale_lanes = qkv[:, q_cols + 2 * kv_cols :].astype(F32)
    scale_column = jnp.sum(scale_lanes, axis=1, keepdims=True)
    scale_row = jnp.sum(scale_lanes.T, axis=0, keepdims=True) * SOFT
    for group in range(groups):
        at = q_cols + group * HEAD_SIZE
        keys = qkv[:, at : at + HEAD_SIZE]
        keys_t = keys.astype(F32).T.astype(BF)
        at = at + kv_cols
        values = qkv[:, at : at + HEAD_SIZE]
        wait_group(qkv, in_sems, 1, group)
        wait_group(grads, in_sems, 1 + groups, group)
        for index in range(GROUP_HEADS):
            columns = head_columns(group * GROUP_HEADS + index)
            lanes = slice(index * tokens, (index + 1) * tokens)
            if not known:
                scores[group, :, lanes] = dot_nt(keys, qkv[:, columns])
            weight_grads[:, lanes] = dot_nt(values, grads[:, columns])
        if known:
            stored[group].wait()
        def block(queries, lanes, reach):
            weight = scores[group, :reach, lanes]
            if not known:
                weight = weights_of(weight, bias[:reach, queries])
            weights[:reach, lanes] = weight.astype(BF)
            weight_grad = weight_grads[:reach, lanes]
            mean = jnp.sum(weight_grad * weight, axis=0, keepdims=True)
            score_grads[:reach, lanes] = (weight * (weight_grad - mean)).astype(BF)

        softmax_blocks(tokens, block)
        key_grad = jnp.zeros((tokens, HEAD_SIZE), F32)
        value_grad = jnp.zeros((tokens, HEAD_SIZE), F32)
        for index in range(GROUP_HEADS):
            columns = head_columns(group * GROUP_HEADS + index)
            lanes = slice(index * tokens, (index + 1) * tokens)
            score_grad = score_grads[:, lanes]
            scaled_q[columns, :] = (dot_nn(keys_t, score_grad) * scale_row).astype(BF)
            key_grad = key_grad + dot_nn(score_grad, qkv[:, columns])
            value_grad = value_grad + dot_nn(weights[:, lanes], grads[:, columns])
        at = group * HEAD_SIZE
        scaled_kv[:, at : at + HEAD_SIZE] = (key_grad * (scale_column * SOFT)).astype(BF)
        at = at + kv_cols
        scaled_kv[:, at : at + HEAD_SIZE] = (value_grad * scale_column).astype(BF)
    count, width, _ = chunks.shape
    through = dot_nt(landed(chunks, sems, count - 1)[...], scaled_kv[...])
    for index in range(count - 1):
        rows = slice(index * width, (index + 1) * width)
        through = through + dot_nn(landed(chunks, sems, index)[...], scaled_q[rows, :])
    out_ref[...] = through.T.astype(BF)


def merger_kernel(
    marks_ref, owners_ref, last_ref, pair_ref, across_ref, beside_ref, g0_ref, g1_ref, weight_ref,
    out_ref, grad_ref, rows, hidden, counts, places,
):
    added = summed(pair_ref, across_ref, beside_ref)
    rows[...] = last_ref[...].astype(F32) + chosen(g0_ref, g1_ref) * added
    share = grad_ref.shape[0]
    at = pl.multiple_of(lax.axis_index("mp") * share, share)
    grad_ref[...] = rows[pl.ds(at, share), :].astype(BF)
    x = rows[...].astype(BF)
    cols = weight_ref.shape[0]
    for start in range(0, cols, 256):
        hidden[:, start : start + 256] = dot_nt(x, weight_ref[start : start + 256, :])
    dp_count, sections = out_ref.shape[:2]
    owner_count = dp_count * sections

    def clear(owner, carry):
        counts[owner] = 0
        for slot in range(CAP):
            places[owner * CAP + slot] = -1
        return carry

    lax.fori_loop(0, owner_count, clear, 0)

    def place(block, carry):
        owner = owners_ref[0, block]

        @pl.when(marks_ref[0, block] == 1)
        def _():
            slot = counts[owner]
            places[owner * CAP + slot] = block
            counts[owner] = slot + 1

        return carry

    lax.fori_loop(0, marks_ref.shape[1], place, 0)

    def send(owner, carry):
        pieces = []
        for slot in range(CAP):
            block = places[owner * CAP + slot]
            at = pl.multiple_of(jnp.maximum(block, 0) * VB, VB)
            pieces.append(jnp.where(block >= 0, hidden[pl.ds(at, VB), :], 0.0))
        out_ref[lax.rem(owner, dp_count), lax.div(owner, dp_count)] = jnp.concatenate(
            pieces, axis=0
        ).astype(BF)
        return carry

    lax.fori_loop(0, owner_count, send, 0)


def merger_sum_kernel(parts_ref, own_ref, other_ref):
    section = lax.axis_index("section")
    sources = parts_ref.shape[0]

    def total(index):
        return add_parts(lambda source: parts_ref[source, index], sources)

    first, second = total(0), total(1)
    own_ref[...] = jnp.where(section == 0, first, second)
    other_ref[...] = jnp.where(section == 0, second, first).astype(BF)


def gelu_slope(values):
    cumulative = 0.5 * (1.0 + lax.erf(values * (1.0 / math.sqrt(2.0))))
    return cumulative + values * jnp.exp(-0.5 * values * values) * (1.0 / math.sqrt(2.0 * math.pi))


def local(
    embeds,
    cotangent,
    norm_gain,
    w_query,
    w_keyval,
    w_out,
    seq_lengths,
    image_mask,
    block_owner,
    merger_weight,
    merger_pre,
):
    section = lax.axis_index("section")
    mp_count = lax.axis_size("mp")
    dp_count = lax.axis_size("dp")
    rows, width = embeds.shape[1:]
    tokens = rows * mp_count
    share = tokens // dp_count
    q_cols = w_query.shape[3]
    kv_cols = w_keyval.shape[4]
    joined = q_cols + 2 * kv_cols + 128
    emb, cot = embeds[0], cotangent[0]
    wq, wout = w_query[0, 0], w_out[0, 0]
    wkv = w_keyval[0, 0].reshape(width, 2 * kv_cols)
    gain = norm_gain[0]

    def partner(index):
        other, rank = 1 - index // mp_count, (index % mp_count + mp_count // 2) % mp_count
        return other * mp_count + rank

    everyone = range(2 * mp_count)
    from_first = [(i, partner(i)) for i in everyone if i < mp_count]
    from_second = [(i, partner(i)) for i in everyone if i >= mp_count]

    def swap(array, pairs):
        return lax.ppermute(array, ("section", "mp"), pairs)

    def scatter(array, axis):
        return lax.all_to_all(array, axis, split_axis=0, concat_axis=0, tiled=True)

    def spread(copies):
        return scatter(copies, "dp").reshape(tokens, copies.shape[2])

    def gather(array, axis):
        return lax.all_gather(array, axis, axis=0, tiled=True)

    def chunks_of(count):
        return pltpu.VMEM((count, width, width), BF)

    own_x, other_x = jnp.where(section == 0, emb, cot), jnp.where(section == 0, cot, emb)
    received_x = swap(other_x, from_first + from_second)
    gain_x = swap(gain, from_first + from_second)
    def vmem(*shape):
        return pltpu.VMEM(shape, BF)

    def dma(count):
        return pltpu.SemaphoreType.DMA((count,))

    def other_rows_parts(x):
        return pl.pallas_call(
            first_kernel,
            out_shape=pltpu.HBM((dp_count, share, joined), BF),
            in_specs=[VMEM] * 2 + [HBM] * 3,
            out_specs=HBM,
            scratch_shapes=[chunks_of(5), vmem(dp_count, share, joined), dma(5), dma(6)],
            compiler_params=params(24),
            cost_estimate=cost(2 * tokens * width * joined, 6 << 20),
        )(x, gain, *in_hbm(wq, wkv, wout))

    def first_sum(parts):
        return pl.pallas_call(
            first_sum_kernel,
            out_shape=shape_of((share, joined), BF),
            in_specs=[ANY],
            out_specs=VMEM,
            scratch_shapes=[vmem(dp_count, share, joined), dma(6)],
            compiler_params=params(24),
            cost_estimate=cost(parts.size, 2 << 20),
        )(parts)

    def summed_copies(adder, parts):
        cols = parts.shape[2]
        return pl.pallas_call(
            functools.partial(sum_kernel, adder),
            out_shape=pltpu.HBM((dp_count, share, cols), BF),
            in_specs=[ANY],
            out_specs=HBM,
            scratch_shapes=[vmem(dp_count, share, cols), vmem(share, cols), dma(6), dma(dp_count)],
            compiler_params=params(24),
            cost_estimate=cost(parts.size, 4 << 20),
        )(parts)

    def chosen_copies(first, second, cols):
        return pl.pallas_call(
            choose_kernel,
            out_shape=pltpu.HBM((dp_count, share, cols), BF),
            in_specs=[VMEM] * 2,
            out_specs=HBM,
            scratch_shapes=[dma(dp_count)],
            compiler_params=params(24),
            cost_estimate=cost(0, 2 << 20),
        )(first, second)

    def loaded(joins, firsts, seconds):
        count = 5 if joins else 4
        return pl.pallas_call(
            functools.partial(load_kernel, joins, len(firsts)),
            out_shape=pltpu.VMEM((count, width, width), BF),
            in_specs=[HBM] * (len(firsts) + len(seconds)),
            out_specs=VMEM,
            scratch_shapes=[dma(count)],
            compiler_params=params(16),
            cost_estimate=cost(0, 5 << 20),
        )(*in_hbm(*firsts, *seconds))

    def beside(array, distance):
        return lax.ppermute(array, "mp", [(i, i ^ distance) for i in range(mp_count)])

    def sum_over_mp(part, *later):
        mate = beside(part, 1)
        at = lax.axis_index("mp") % 2 * (tokens // 2)

        def half(array):
            return lax.dynamic_slice_in_dim(array, at, tokens // 2).astype(F32)

        pair_half = (half(part) + half(mate)).astype(BF)
        across = beside(pair_half, 2)
        pair_half, part, mate, *later = lax.optimization_barrier((pair_half, part, mate, *later))
        pair = (part.astype(F32) + mate.astype(F32)).astype(BF)
        return (pair, across, beside(across, 1)), later

    around = [beside(own_x, distance) for distance in (1, 2, 3)]
    first_chunks = pl.pallas_call(
        first_load_kernel,
        out_shape=pltpu.VMEM((5, width, width), BF),
        in_specs=[HBM] * 3,
        out_specs=VMEM,
        scratch_shapes=[dma(5)],
        compiler_params=params(16),
        cost_estimate=cost(0, 5 << 20),
    )(*in_hbm(wq, wkv, wout))
    own_parts, own_all = pl.pallas_call(
        first_own_kernel,
        out_shape=[pltpu.HBM((dp_count, share, joined), BF), shape_of((tokens, width), BF)],
        in_specs=[VMEM] * 6,
        out_specs=[HBM, VMEM],
        scratch_shapes=[
            pltpu.VMEM((tokens, width), F32),
            vmem(dp_count, share, joined),
            dma(6),
        ],
        compiler_params=params(24),
        cost_estimate=cost(2 * tokens * width * joined, 6 << 20),
    )(own_x, *around, gain, first_chunks)
    own_parts, received_x, gain_x, wq_s, wout_s = lax.optimization_barrier(
        (own_parts, received_x, gain_x, wq, wout)
    )
    own_parts = scatter(own_parts, "dp")
    wq_b = swap(wq_s, from_second)
    cuts = (5 * q_cols // 16, 5 * q_cols // 8)
    wout_a0 = swap(wout_s[: cuts[0]], from_first)
    wout_a1, wout_a2 = wout_s[cuts[0] : cuts[1]], wout_s[cuts[1] :]
    other_parts = other_rows_parts(gather(received_x, "mp"))
    own_parts, other_parts, wout_a0, wout_a1, wout_a2 = lax.optimization_barrier(
        (own_parts, other_parts, wout_a0, wout_a1, wout_a2)
    )
    wout_a1 = swap(wout_a1, from_first)
    own = first_sum(own_parts)
    mine_all = gather(other_x, "mp")
    other_parts, own, mine_all, wout_a1 = lax.optimization_barrier(
        (scatter(other_parts, "dp"), own, mine_all, wout_a1)
    )
    other = first_sum(other_parts)
    received = swap(other, from_first)
    received_grad, wkv_s = lax.optimization_barrier((swap(other, from_second), wkv))
    wkv_b = swap(wkv_s, from_second)
    copies, wout_a2 = lax.optimization_barrier((chosen_copies(own, received, joined), wout_a2))
    wout_a2 = swap(wout_a2, from_first)
    grad_copies = chosen_copies(received_grad, own, q_cols)
    qkv_first, grad_copies, wout_a2, wq_b, wq_s, wkv_s = lax.optimization_barrier(
        (spread(copies), grad_copies, wout_a2, wq_b, wq, wkv)
    )
    wout_a = (wout_a0, wout_a1, wout_a2)
    wq_a, wkv_a = swap(wq_s, from_first), swap(wkv_s, from_first)
    head_grad_last = spread(grad_copies)

    def layer_forward(qkv, wouts):
        out = pl.pallas_call(
            forward_kernel,
            out_shape=shape_of((tokens, width), BF),
            in_specs=[SMEM, ANY] + [HBM] * (1 + len(wouts[1])),
            out_specs=VMEM,
            scratch_shapes=[
                vmem(tokens, joined),
                chunks_of(4),
                pltpu.VMEM((tokens, tokens), F32),
                pltpu.VMEM((tokens, GROUP_HEADS * tokens), F32),
                vmem(tokens, GROUP_HEADS * tokens),
                vmem(tokens, q_cols),
                dma(4),
                dma(3),
            ],
            compiler_params=params(32),
            cost_estimate=cost(6 * tokens * tokens * q_cols, 4 << 20),
        )(seq_lengths, qkv, *in_hbm(wouts[0], *wouts[1]))
        return out

    def rows_after(resident, sums):
        even = lax.axis_index("mp") % 2 == 0
        lower, upper = jnp.where(even, *sums[1:]), jnp.where(even, *sums[:0:-1])
        added = sums[0].astype(F32) + jnp.concatenate([lower, upper], axis=0).astype(F32)
        return (resident.astype(F32) + added).astype(BF)

    out, wkv_b = lax.optimization_barrier((layer_forward(qkv_first, (wout, wout_a)), wkv_b))
    sums, pieces = sum_over_mp(out, wq_b, wkv_b, wq, wkv)
    joined_last = loaded(True, pieces[:2], pieces[2:])
    parts = pl.pallas_call(
        project_kernel,
        out_shape=pltpu.HBM((dp_count, share, joined), BF),
        in_specs=[VMEM] * 8,
        out_specs=HBM,
        scratch_shapes=[vmem(dp_count, share, joined), dma(6)],
        compiler_params=params(24),
        cost_estimate=cost(2 * tokens * width * joined, 6 << 20),
    )(own_all, mine_all, *sums, gain_x, gain, joined_last)
    parts, head_grad_last = lax.optimization_barrier((parts, head_grad_last))
    qkv_last = spread(summed_copies(scaled_sum, scatter(parts, "dp")))
    wout_b = swap(wout, from_second)
    wout_last = jnp.where(section == 0, wout_b, wout)
    h_one = rows_after(jnp.where(section == 0, own_all, mine_all), sums)
    rows_after(h_one, sum_over_mp(layer_forward(qkv_last, (wout_last, (wout_last,))))[0])

    def layer_backward(qkv, head_grads, wqs, wkvs, *known, later=()):
        through = pl.pallas_call(
            functools.partial(backward_kernel, len(known), len(wqs[0])),
            out_shape=shape_of((tokens, width), BF),
            in_specs=[SMEM, ANY, ANY] + [HBM] * (3 + len(wqs[0]) + len(known)),
            out_specs=VMEM,
            scratch_shapes=[
                vmem(tokens, joined),
                vmem(tokens, q_cols),
                chunks_of(5),
                pltpu.VMEM((tokens, tokens), F32),
                pltpu.VMEM((groups, tokens, GROUP_HEADS * tokens), F32),
                pltpu.VMEM((tokens, GROUP_HEADS * tokens), F32),
                vmem(tokens, GROUP_HEADS * tokens),
                vmem(tokens, GROUP_HEADS * tokens),
                vmem(q_cols, tokens),
                vmem(tokens, 2 * kv_cols),
                dma(5),
                dma(7),
            ],
            compiler_params=params(32),
            cost_estimate=cost(12 * tokens * tokens * q_cols, 6 << 20),
        )(seq_lengths, qkv, head_grads, *in_hbm(*wqs[0], *wqs[1], *wkvs, *known))
        return sum_over_mp(through, *later)

    groups = kv_cols // HEAD_SIZE
    sums, pieces = layer_backward(
        qkv_last,
        *in_hbm(head_grad_last),
        ((wq_b,), (wq,)),
        (wkv_b, wkv),
        later=(wout, *wout_a),
    )
    parts, grad_one = pl.pallas_call(
        head_grad_kernel,
        out_shape=[pltpu.HBM((dp_count, share, q_cols), BF), shape_of((tokens, width), BF)],
        in_specs=[VMEM] * 8,
        out_specs=[HBM, VMEM],
        scratch_shapes=[vmem(dp_count, share, q_cols), dma(4)],
        compiler_params=params(24),
        cost_estimate=cost(2 * tokens * width * q_cols, 4 << 20),
    )(mine_all, own_all, *sums, gain_x, gain, loaded(False, pieces[:1], pieces[1:]))
    parts, qkv_late = lax.optimization_barrier((parts, qkv_first))
    softmax_first = pl.pallas_call(
        softmax_kernel,
        out_shape=pltpu.HBM((groups, tokens, GROUP_HEADS * tokens), F32),
        in_specs=[SMEM, ANY],
        out_specs=HBM,
        scratch_shapes=[
            vmem(tokens, joined),
            pltpu.VMEM((tokens, tokens), F32),
            pltpu.VMEM((groups, tokens, GROUP_HEADS * tokens), F32),
            dma(3),
            dma(2),
        ],
        compiler_params=params(32),
        cost_estimate=cost(4 * tokens * tokens * q_cols, 6 << 20),
    )(seq_lengths, *in_hbm(qkv_late))
    parts, softmax_first, wq_a, wkv_a = lax.optimization_barrier(
        (scatter(parts, "dp"), softmax_first, wq_a, wkv_a)
    )
    head_grad_first = spread(summed_copies(plain_sum, parts))
    sums, _ = layer_backward(
        *in_hbm(qkv_late), head_grad_first, ((wq,), (wq_a,)), (wkv, wkv_a), softmax_first
    )

    hidden_cols = merger_weight.shape[0]
    outgoing, input_grad = pl.pallas_call(
        merger_kernel,
        out_shape=[
            shape_of((dp_count, 2, CAP * VB, hidden_cols), BF),
            shape_of((rows, width), BF),
        ],
        in_specs=[SMEM, SMEM] + [VMEM] * 7,
        out_specs=[VMEM] * 2,
        scratch_shapes=[
            pltpu.VMEM((tokens, width), F32),
            pltpu.VMEM((tokens, hidden_cols), F32),
            pltpu.SMEM((2 * dp_count,), jnp.int32),
            pltpu.SMEM((2 * dp_count * CAP,), jnp.int32),
        ],
        compiler_params=params(24),
    )(image_mask, block_owner, grad_one, *sums, gain, gain_x, merger_weight)
    kept, passed = pl.pallas_call(
        merger_sum_kernel,
        out_shape=[
            shape_of((CAP * VB, hidden_cols), F32),
            shape_of((CAP * VB, hidden_cols), BF),
        ],
        in_specs=[VMEM],
        out_specs=[VMEM] * 2,
        compiler_params=params(24),
    )(scatter(outgoing, "dp"))
    crossed = lax.ppermute(passed, "section", [(0, 1), (1, 0)]).astype(F32)
    first = jnp.where(section == 0, kept, crossed)
    second = jnp.where(section == 0, crossed, kept)
    hidden_grad = jnp.stack([first, second]).reshape(2, CAP, VB, hidden_cols)
    merger_grad = gelu_slope(merger_pre[0].astype(F32)) * hidden_grad
    return (input_grad[None], merger_grad[None])


def solution(mesh):
    placed = (
        P("section", "mp", "dp"),
        P("section", "mp", "dp"),
        P(None, "section", "dp"),
        P(None, "section", "dp", "mp"),
        P(None, "section", "dp", None, "mp"),
        P(None, "section", "mp", "dp"),
        P(),
        P("section", None),
        P("section", None),
        P("mp", "dp"),
        P(("section", "dp"), None, None, None, "mp"),
    )
    return jax.shard_map(
        local,
        mesh=mesh,
        in_specs=placed,
        out_specs=(P("section", "mp", "dp"), P(("section", "dp"), None, None, None, "mp")),
        check_vma=False,
    )
```

time: 935 us -> 299 us (0.32)
  waiting for transfers between devices: 531 us -> 85.4 us
  matrix products: 118 us -> 0 us
  blocking collectives: 165 us -> 84.9 us
  Pallas kernels: 0 us -> 53 us
  starting transfers between devices: 17.4 us -> 65.2 us
  local copies, waits for them, and re-layouts: 50.2 us -> 6.28 us
  other arithmetic: 34.1 us -> 1.95 us
  between operations: 14.1 us -> 1.16 us
    psum x6 -> x0, waiting for transfers between devices: 384 us -> none  [the longest x3 235 us: backward_step(): head_grad = lax.psum(partial_heads.astype(jnp.bfloat16), 'dp')]
    psum x3 -> x0, blocking collectives: 124 us -> none  [forward_step(): projected, square_sum = lax.psum((partial_proj, squares), 'dp')]
    dot_general x32 -> x0, matrix products: 104 us -> none  [the longest x3 26 us: attend_back(): jnp.einsum('hgqk,khd->qhgd', score_grad, key_heads, preferred_element_typ...]
    reduce_scatter x6 -> x0, waiting for transfers between devices: 95.2 us -> none  [the longest x3 47.7 us: forward_step(): lax.psum_scatter(jnp.dot(attended, out_matrix, preferred_element_type=jnp...]
    all_to_all x0 -> x3, blocking collectives: none -> 73.3 us  [scatter(): return lax.all_to_all(array, axis, split_axis=0, concat_axis=0, tiled=True)]
    pallas_call x0 -> x19, Pallas kernels: none -> 53 us  [the longest x2 18.6 us: layer_backward(): pl.pallas_call(functools.partial(backward_kernel, len(known), len(wqs[0])...]
    ppermute x7 -> x24, waiting for transfers between devices: 32.8 us -> 64.4 us  [the longest x11 37.5 us: swap(): return lax.ppermute(array, ('section', 'mp'), pairs)]
    all_gather x7 -> x2, blocking collectives: 41.1 us -> 11.6 us  [gather(): return lax.all_gather(array, axis, axis=0, tiled=True)]
  transfers between devices with their start and end apart: 20 -> 30, of which waited for: 20 -> 19; matrix products, arithmetic and copies ran while one was open for 5% -> 2% of each run, Pallas kernels for 0% -> 13%
where the time goes in v1:
time: 299 us; the launch traced here: 298 us
  waiting for transfers between devices  85.4 us (29%)
  blocking collectives  84.9 us (28%)
  starting transfers between devices  65.2 us (22%)
  Pallas kernels  53 us (18%)
  local copies, waits for them, and re-layouts  6.28 us (2%)
    all_to_all x3, blocking collectives, scatter(): return lax.all_to_all(array, axis, split_axis=0, concat_axis=0, tiled=True)  73.3 us
    ppermute x11, waiting for transfers between devices, swap(): return lax.ppermute(array, ('section', 'mp'), pairs)  37.5 us
    all_to_all x6, starting transfers between devices, scatter(): return lax.all_to_all(array, axis, split_axis=0, concat_axis=0, tiled=True)  36.5 us
    ppermute x11, starting transfers between devices, swap(): return lax.ppermute(array, ('section', 'mp'), pairs)  25.8 us
    ppermute x12, waiting for transfers between devices, beside(): lax.ppermute(array, 'mp', [(i, i ^ distance) for i in range(mp_count)])  21.4 us
    all_to_all x6, waiting for transfers between devices, scatter(): return lax.all_to_all(array, axis, split_axis=0, concat_axis=0, tiled=True)  21 us
    pallas_call x2, Pallas kernels, layer_backward(): pl.pallas_call(functools.partial(backward_kernel, len(known), len(wqs[0])...  18.6 us
    all_gather x2, blocking collectives, gather(): return lax.all_gather(array, axis, axis=0, tiled=True)  11.6 us
  transfers between devices with their start and end apart: 30, of which 19 were waited for; matrix products, arithmetic and copies ran while one was open for 2% of the time, Pallas kernels for 13%

profile of v1, /device:TPU:6, one launch (start us, length us, event | category | flops | bytes accessed | tf_op | source)
XLA Modules:
  0.0 297.8 jit_solution(12740495269112292783)
XLA Ops:
  3.9 2.8 collective-permute-start.3
  11.9 8.1 %all-to-all-start = ((bf16[16,16,2688]{2,1,0:T(8,128)(2,1)}), bf16[16,16,2688]{2,1,0:T(8,128)(2,1)S(1)}, u32[]{:S(2)}, u32[]{:S(2)}) async-start(bf16[16,16,2688]{2,1,0:T(8,128)(2,1)} %get-tuple-element.59), calls=%async_computation | async-start | bytes 2752512 | tf_op jit(solution)/shard_map/all_to_all | solution.py:635
  20.0 2.2 fusion.9
  25.6 5.8 %all_gather.6.x_ref = bf16[256,512]{1,0:T(8,128)(2,1)S(1)} all-gather(bf16[64,512]{1,0:T(8,128)(2,1)S(1)} %collective-permute-done.3), channel_id=1, replica_groups=mesh['section'=2,'mp'=4,'dp'=16] {'mp'}, dimensions={0}, use_global_device_ids=true | all-gather | bytes 327680 | tf_op jit(solution)/shard_map/all_gather | solution.py:641
  31.3 3.4 %shard_map.124 = bf16[16,16,2688]{2,1,0:T(8,128)(2,1)} custom-call(bf16[256,512]{1,0:T(8,128)(2,1)S(1)} %all_gather.6.x_ref, f32[1,512]{1,0:T(1,128)S(1)} %bitcast.28, bf16[512,2048]{1,0:T(8,128)(2,1)} %bitcast.39, bf16[512,512]{1,0:T(8,128)(2,1)} %bitcast.46, bf16[2048,512]{1,0:T(8,128)(2,1)} %bitcast.35), custom_call_target="tpu_custom_call" | custom-call | flops 704643072 | bytes 6291456 | tf_op jit(solution)/shard_map/pallas_call | solution.py:656
  34.7 6.8 %collective-permute-done.5.refs_0_.refs_1_ = bf16[640,512]{1,0:T(8,128)(2,1)} collective-permute-done((bf16[640,512]{1,0:T(8,128)(2,1)S(1)}, bf16[640,512]{1,0:T(8,128)(2,1)}, u32[]{:S(2)}, u32[]{:S(2)}) %collective-permute-start.5) | collective-permute-done | bytes 655392 | tf_op jit(solution)/shard_map/ppermute | solution.py:632
  41.6 6.9 %all-to-all-start.1 = ((bf16[16,16,2688]{2,1,0:T(8,128)(2,1)}), bf16[16,16,2688]{2,1,0:T(8,128)(2,1)S(1)}, u32[]{:S(2)}, u32[]{:S(2)}) async-start(bf16[16,16,2688]{2,1,0:T(8,128)(2,1)} %shard_map.124), calls=%async_computation.1 | async-start | bytes 2752512 | tf_op jit(solution)/shard_map/all_to_all | solution.py:635
  48.5 2.7 collective-permute-start.10
  52.4 5.8 %all-gather = bf16[1,256,512]{2,1,0:T(8,128)(2,1)S(1)} all-gather(bf16[1,64,512]{2,1,0:T(8,128)(2,1)S(1)} %get-tuple-element.116), channel_id=2, replica_groups=mesh['section'=2,'mp'=4,'dp'=16] {'mp'}, dimensions={1}, use_global_device_ids=true | all-gather | bytes 327680 | tf_op jit(solution)/shard_map/all_gather | solution.py:641
  58.6 11.1 %collective-permute-done.6.refs_1_.refs_2_ = bf16[640,512]{1,0:T(8,128)(2,1)} collective-permute-done((bf16[640,512]{1,0:T(8,128)(2,1)}, bf16[640,512]{1,0:T(8,128)(2,1)}, u32[]{:S(2)}, u32[]{:S(2)}) %collective-permute-start.6) | collective-permute-done | bytes 655392 | tf_op jit(solution)/shard_map/ppermute | solution.py:632
  71.5 6.3 %collective-permute-done.7.second_ref = bf16[16,2688]{1,0:T(8,128)(2,1)S(1)} collective-permute-done((bf16[16,2688]{1,0:T(8,128)(2,1)S(1)}, bf16[16,2688]{1,0:T(8,128)(2,1)S(1)}, u32[]{:S(2)}, u32[]{:S(2)}) %collective-permute-start.7) | collective-permute-done | bytes 86048 | tf_op jit(solution)/shard_map/ppermute | solution.py:632
  79.0 7.1 %all-to-all-start.2 = ((bf16[16,16,2688]{2,1,0:T(8,128)(2,1)}), bf16[16,16,2688]{2,1,0:T(8,128)(2,1)S(1)}, u32[]{:S(2)}, u32[]{:S(2)}) async-start(bf16[16,16,2688]{2,1,0:T(8,128)(2,1)} %shard_map.127), calls=%async_computation.2 | async-start | bytes 2752512 | tf_op jit(solution)/shard_map/all_to_all | solution.py:635
  87.4 6.6 %collective-permute-start.8 = (bf16[16,2688]{1,0:T(8,128)(2,1)S(1)}, bf16[16,2688]{1,0:T(8,128)(2,1)S(1)}, u32[]{:S(2)}, u32[]{:S(2)}) collective-permute-start(bf16[16,2688]{1,0:T(8,128)(2,1)S(1)} %shard_map.126), channel_id=1, source_target_pairs={{64,32},{80,48},{96,0},{112,16},{65,33},{81,49},{97,1},{113,17},{6... | collective-permute-start | bytes 258056 | tf_op jit(solution)/shard_map/ppermute | solution.py:632
  96.1 5.5 %collective-permute-start.11 = (bf16[512,512]{1,0:T(8,128)(2,1)S(1)}, bf16[512,512]{1,0:T(8,128)(2,1)S(1)}, u32[]{:S(2)}, u32[]{:S(2)}) collective-permute-start(bf16[512,512]{1,0:T(8,128)(2,1)S(1)} %bitcast.50), channel_id=1, source_target_pairs={{64,32},{80,48},{96,0},{112,16},{65,33},{81,49},{97,1},{113,17},{6... | collective-permute-start | bytes 1572872 | tf_op jit(solution)/shard_map/ppermute | solution.py:632
  102.8 2.1 collective-permute-done.9.refs_2_.refs_3_
  104.9 7.0 %all-to-all-start.3 = ((bf16[16,16,2048]{2,1,0:T(8,128)(2,1)}), bf16[16,16,2048]{2,1,0:T(8,128)(2,1)}, u32[]{:S(2)}, u32[]{:S(2)}) async-start(bf16[16,16,2048]{2,1,0:T(8,128)(2,1)} %shard_map.128), calls=%async_computation.3 | async-start | bytes 2097152 | tf_op jit(solution)/shard_map/all_to_all | solution.py:635
  111.9 5.1 %shard_map.129 = bf16[256,512]{1,0:T(8,128)(2,1)S(1)} custom-call(s32[2,3]{1,0:T(2,128)S(1)} %copy-done.3, bf16[256,2688]{1,0:T(8,128)(2,1)S(1)} %bitcast.19, bf16[2048,512]{1,0:T(8,128)(2,1)} %bitcast.36, bf16[640,512]{1,0:T(8,128)(2,1)} %collective-permute-done.5.refs_0_.refs_1_, bf16[640,512]{1,0:T(8,128)(2,1)} %collective-permute-done.6.refs_1_.refs_2_, ...), custom_call_target="tpu_custom_call" | custom-call | flops 805306368 | bytes 4194304 | tf_op jit(solution)/shard_map/pallas_call | solution.py:784
  120.6 3.8 %collective-permute-done.13.across_ref = bf16[128,512]{1,0:T(8,128)(2,1)S(1)} collective-permute-done((bf16[128,512]{1,0:T(8,128)(2,1)S(1)}, bf16[128,512]{1,0:T(8,128)(2,1)S(1)}, u32[]{:S(2)}, u32[]{:S(2)}) %collective-permute-start.13) | collective-permute-done | bytes 131104 | tf_op jit(solution)/shard_map/ppermute | solution.py:713
  127.4 28.2 %all_to_all.45.parts_ref = bf16[16,16,2688]{2,1,0:T(8,128)(2,1)S(1)} all-to-all(bf16[16,16,2688]{2,1,0:T(8,128)(2,1)} %shard_map.131), channel_id=1, replica_groups=mesh['section'=2,'mp'=4,'dp'=16] {'dp'}, dimensions={0} | all-to-all | bytes 2752512 | tf_op jit(solution)/shard_map/all_to_all | solution.py:635
  157.3 3.7 %all-to-all-start.5 = ((bf16[16,16,2688]{2,1,0:T(8,128)(2,1)}), bf16[16,16,2688]{2,1,0:T(8,128)(2,1)S(1)}, u32[]{:S(2)}, u32[]{:S(2)}) async-start(bf16[16,16,2688]{2,1,0:T(8,128)(2,1)} %shard_map.132), calls=%async_computation.5 | async-start | bytes 2752512 | tf_op jit(solution)/shard_map/all_to_all | solution.py:635
  162.3 19.6 %all-to-all-done.5 = bf16[16,16,2688]{2,1,0:T(8,128)(2,1)S(1)} async-done(((bf16[16,16,2688]{2,1,0:T(8,128)(2,1)}), bf16[16,16,2688]{2,1,0:T(8,128)(2,1)S(1)}, u32[]{:S(2)}, u32[]{:S(2)}) %all-to-all-start.5) | async-done | bytes 1376288 | tf_op jit(solution)/shard_map/all_to_all | solution.py:635
  182.0 9.8 %shard_map.133 = bf16[256,512]{1,0:T(8,128)(2,1)S(1)} custom-call(s32[2,3]{1,0:T(2,128)S(1)} %copy-done.3, bf16[256,2688]{1,0:T(8,128)(2,1)S(1)} %bitcast.22, bf16[256,2048]{1,0:T(8,128)(2,1)} %bitcast.7.grads_ref, bf16[512,2048]{1,0:T(8,128)(2,1)} %collective-permute-done.10.refs_0_, bf16[512,2048]{1,0:T(8,128)(2,1)} %bitcast.43, ...), custom_call_target="tpu_custom_call" | custom-call | flops 1610612736 | bytes 6291456 | tf_op jit(solution)/shard_map/pallas_call | solution.py:830
  195.4 3.7 %collective-permute-done.16.across_ref = bf16[128,512]{1,0:T(8,128)(2,1)S(1)} collective-permute-done((bf16[128,512]{1,0:T(8,128)(2,1)S(1)}, bf16[128,512]{1,0:T(8,128)(2,1)S(1)}, u32[]{:S(2)}, u32[]{:S(2)}) %collective-permute-start.16) | collective-permute-done | bytes 131104 | tf_op jit(solution)/shard_map/ppermute | solution.py:713
  202.0 3.8 %all-to-all-start.6 = ((bf16[16,16,2048]{2,1,0:T(8,128)(2,1)}), bf16[16,16,2048]{2,1,0:T(8,128)(2,1)S(1)}, u32[]{:S(2)}, u32[]{:S(2)}) async-start(bf16[16,16,2048]{2,1,0:T(8,128)(2,1)} %get-tuple-element.101), calls=%async_computation.6 | async-start | bytes 2097152 | tf_op jit(solution)/shard_map/all_to_all | solution.py:635
  207.1 6.7 %shard_map.136.refs_4_ = f32[2,256,2048]{2,1,0:T(8,128)} custom-call(s32[2,3]{1,0:T(2,128)S(1)} %copy-done.3, bf16[256,2688]{1,0:T(8,128)(2,1)} %bitcast.20), custom_call_target="tpu_custom_call" | custom-call | flops 536870912 | bytes 6291456 | tf_op jit(solution)/shard_map/pallas_call | solution.py:872
  213.8 9.1 %collective-permute-done.19.refs_3_ = bf16[512,512]{1,0:T(8,128)(2,1)S(1)} collective-permute-done((bf16[512,512]{1,0:T(8,128)(2,1)S(1)}, bf16[512,512]{1,0:T(8,128)(2,1)S(1)}, u32[]{:S(2)}, u32[]{:S(2)}) %collective-permute-start.19) | collective-permute-done | bytes 524320 | tf_op jit(solution)/shard_map/ppermute | solution.py:632
  225.7 22.0 %all_to_all.46 = bf16[16,16,2048]{2,1,0:T(8,128)(2,1)S(1)} all-to-all(bf16[16,16,2048]{2,1,0:T(8,128)(2,1)} %shard_map.137), channel_id=1, replica_groups=mesh['section'=2,'mp'=4,'dp'=16] {'dp'}, dimensions={0} | all-to-all | bytes 2097152 | tf_op jit(solution)/shard_map/all_to_all | solution.py:635
  247.7 8.7 %shard_map.138 = bf16[256,512]{1,0:T(8,128)(2,1)S(1)} custom-call(s32[2,3]{1,0:T(2,128)S(1)} %copy-done.3, bf16[256,2688]{1,0:T(8,128)(2,1)} %bitcast.21, bf16[256,2048]{1,0:T(8,128)(2,1)S(1)} %bitcast.23, bf16[512,2048]{1,0:T(8,128)(2,1)} %bitcast.44, bf16[512,2048]{1,0:T(8,128)(2,1)} %collective-permute-done.18.refs_1_, bf16[512,512]{1,0:T(8,128)(2,1)} %bitcast.49, ...), custom_call_target="tpu_custom_call" | custom-call | flops 1610612736 | bytes 6291456 | tf_op jit(solution)/shard_map/pallas_call | solution.py:830
  258.2 5.5 %collective-permute-done.21.across_ref = bf16[128,512]{1,0:T(8,128)(2,1)S(1)} collective-permute-done((bf16[128,512]{1,0:T(8,128)(2,1)S(1)}, bf16[128,512]{1,0:T(8,128)(2,1)S(1)}, u32[]{:S(2)}, u32[]{:S(2)}) %collective-permute-start.21) | collective-permute-done | bytes 131104 | tf_op jit(solution)/shard_map/ppermute | solution.py:713
  265.1 3.1 %shard_map.139 = (bf16[16,2,16,1280]{3,2,1,0:T(8,128)(2,1)S(1)}, bf16[64,512]{1,0:T(8,128)(2,1)}) custom-call(s32[1,32]{1,0:T(1,128)S(1)} %copy-done.4, s32[1,32]{1,0:T(1,128)S(1)} %copy-done.5, bf16[256,512]{1,0:T(8,128)(2,1)S(1)} %get-tuple-element.98.last_ref, bf16[256,512]{1,0:T(8,128)(2,1)S(1)} %add_convert_fusion.pair_ref, ...), custom_call_target="tpu_custom_call" | custom-call | tf_op jit(solution)/shard_map/pallas_call | solution.py:896
  268.1 23.1 %all_to_all.47.parts_ref = bf16[16,2,16,1280]{3,2,1,0:T(8,128)(2,1)S(1)} all-to-all(bf16[16,2,16,1280]{3,2,1,0:T(8,128)(2,1)S(1)} %get-tuple-element.111), channel_id=1, replica_groups=mesh['section'=2,'mp'=4,'dp'=16] {'dp'}, dimensions={0} | all-to-all | bytes 2621440 | tf_op jit(solution)/shard_map/all_to_all | solution.py:635
  291.6 5.5 %collective-permute-done.23 = bf16[16,1280]{1,0:T(8,128)(2,1)S(1)} collective-permute-done((bf16[16,1280]{1,0:T(8,128)(2,1)S(1)}, bf16[16,1280]{1,0:T(8,128)(2,1)S(1)}, u32[]{:S(2)}, u32[]{:S(2)}) %collective-permute-start.23) | collective-permute-done | bytes 40992 | tf_op jit(solution)/shard_map/ppermute | solution.py:922
  (86 shorter events, 45.1 us)
Async XLA Ops:
  1.5 8.7 %collective-permute-start = (bf16[64,512]{1,0:T(8,128)(2,1)S(1)}, bf16[64,512]{1,0:T(8,128)(2,1)S(1)}, u32[]{:S(2)}, u32[]{:S(2)}) collective-permute-start(bf16[64,512]{1,0:T(8,128)(2,1)S(1)} %get-tuple-element.117.mine_ref), channel_id=1, source_target_pairs={{0,16},{16,0},{32,48},{48,32},{1,17},{17,1},{33,49},{49,33},{2,18}... | collective-permute-start | bytes 196616 | tf_op jit(solution)/shard_map/ppermute | solution.py:713
  1.6 8.6 %collective-permute-start.1 = (bf16[64,512]{1,0:T(8,128)(2,1)S(1)}, bf16[64,512]{1,0:T(8,128)(2,1)S(1)}, u32[]{:S(2)}, u32[]{:S(2)}) collective-permute-start(bf16[64,512]{1,0:T(8,128)(2,1)S(1)} %get-tuple-element.117.mine_ref), channel_id=1, source_target_pairs={{0,32},{16,48},{32,0},{48,16},{1,33},{17,49},{33,1},{49,17},{2,34}... | collective-permute-start | bytes 196616 | tf_op jit(solution)/shard_map/ppermute | solution.py:713
  2.5 7.7 %collective-permute-start.2 = (bf16[64,512]{1,0:T(8,128)(2,1)S(1)}, bf16[64,512]{1,0:T(8,128)(2,1)S(1)}, u32[]{:S(2)}, u32[]{:S(2)}) collective-permute-start(bf16[64,512]{1,0:T(8,128)(2,1)S(1)} %get-tuple-element.117.mine_ref), channel_id=1, source_target_pairs={{0,48},{16,32},{32,16},{48,0},{1,49},{17,33},{33,17},{49,1},{2,50}... | collective-permute-start | bytes 196616 | tf_op jit(solution)/shard_map/ppermute | solution.py:713
  3.5 8.4 %collective-permute-start.4 = (f32[1,512]{1,0:T(1,128)}, f32[1,512]{1,0:T(1,128)S(1)}, u32[]{:S(2)}, u32[]{:S(2)}) collective-permute-start(f32[1,512]{1,0:T(1,128)} %bitcast.26), channel_id=1, source_target_pairs={{0,96},{16,112},{32,64},{48,80},{64,32},{80,48},{96,0},{112,16},{1... | collective-permute-start | bytes 6152 | tf_op jit(solution)/shard_map/ppermute | solution.py:632
  3.9 8.0 %collective-permute-start.3 = (bf16[64,512]{1,0:T(8,128)(2,1)S(1)}, bf16[64,512]{1,0:T(8,128)(2,1)S(1)}, u32[]{:S(2)}, u32[]{:S(2)}) collective-permute-start(bf16[64,512]{1,0:T(8,128)(2,1)S(1)} %bitcast.53), channel_id=1, source_target_pairs={{0,96},{16,112},{32,64},{48,80},{64,32},{80,48},{96,0},{112,16},{1... | collective-permute-start | bytes 196616 | tf_op jit(solution)/shard_map/ppermute | solution.py:632
  11.9 29.7 %all-to-all-start = ((bf16[16,16,2688]{2,1,0:T(8,128)(2,1)}), bf16[16,16,2688]{2,1,0:T(8,128)(2,1)S(1)}, u32[]{:S(2)}, u32[]{:S(2)}) async-start(bf16[16,16,2688]{2,1,0:T(8,128)(2,1)} %get-tuple-element.59), calls=%async_computation | async-start | bytes 2752512 | tf_op jit(solution)/shard_map/all_to_all | solution.py:635
  22.2 19.3 %collective-permute-start.5 = (bf16[640,512]{1,0:T(8,128)(2,1)S(1)}, bf16[640,512]{1,0:T(8,128)(2,1)}, u32[]{:S(2)}, u32[]{:S(2)}) collective-permute-start(bf16[640,512]{1,0:T(8,128)(2,1)S(1)} %get-tuple-element.115), channel_id=1, source_target_pairs={{0,96},{16,112},{32,64},{48,80},{1,97},{17,113},{33,65},{49,81},{2... | collective-permute-start | bytes 1966088 | tf_op jit(solution)/shard_map/ppermute | solution.py:632
  41.6 28.2 %all-to-all-start.1 = ((bf16[16,16,2688]{2,1,0:T(8,128)(2,1)}), bf16[16,16,2688]{2,1,0:T(8,128)(2,1)S(1)}, u32[]{:S(2)}, u32[]{:S(2)}) async-start(bf16[16,16,2688]{2,1,0:T(8,128)(2,1)} %shard_map.124), calls=%async_computation.1 | async-start | bytes 2752512 | tf_op jit(solution)/shard_map/all_to_all | solution.py:635
  48.5 54.3 %collective-permute-start.10 = (bf16[512,2048]{1,0:T(8,128)(2,1)}, bf16[512,2048]{1,0:T(8,128)(2,1)}, u32[]{:S(2)}, u32[]{:S(2)}) collective-permute-start(bf16[512,2048]{1,0:T(8,128)(2,1)} %bitcast.40), channel_id=1, source_target_pairs={{64,32},{80,48},{96,0},{112,16},{65,33},{81,49},{97,1},{113,17},{6... | collective-permute-start | bytes 6291464 | tf_op jit(solution)/shard_map/ppermute | solution.py:632
  51.2 18.6 %collective-permute-start.6 = (bf16[640,512]{1,0:T(8,128)(2,1)}, bf16[640,512]{1,0:T(8,128)(2,1)}, u32[]{:S(2)}, u32[]{:S(2)}) collective-permute-start(bf16[640,512]{1,0:T(8,128)(2,1)} %get-tuple-element.64), channel_id=1, source_target_pairs={{0,96},{16,112},{32,64},{48,80},{1,97},{17,113},{33,65},{49,81},{2... | collective-permute-start | bytes 1966088 | tf_op jit(solution)/shard_map/ppermute | solution.py:632
  70.2 7.6 %collective-permute-start.7 = (bf16[16,2688]{1,0:T(8,128)(2,1)S(1)}, bf16[16,2688]{1,0:T(8,128)(2,1)S(1)}, u32[]{:S(2)}, u32[]{:S(2)}) collective-permute-start(bf16[16,2688]{1,0:T(8,128)(2,1)S(1)} %shard_map.126), channel_id=1, source_target_pairs={{0,96},{16,112},{32,64},{48,80},{1,97},{17,113},{33,65},{49,81},{2... | collective-permute-start | bytes 258056 | tf_op jit(solution)/shard_map/ppermute | solution.py:632
  79.0 25.9 %all-to-all-start.2 = ((bf16[16,16,2688]{2,1,0:T(8,128)(2,1)}), bf16[16,16,2688]{2,1,0:T(8,128)(2,1)S(1)}, u32[]{:S(2)}, u32[]{:S(2)}) async-start(bf16[16,16,2688]{2,1,0:T(8,128)(2,1)} %shard_map.127), calls=%async_computation.2 | async-start | bytes 2752512 | tf_op jit(solution)/shard_map/all_to_all | solution.py:635
  86.1 25.8 %copy-start.3 = (s32[2,3]{1,0:T(2,128)S(1)}, s32[2,3]{1,0:T(2,128)}, u32[]{:S(2)}) copy-start(s32[2,3]{1,0:T(2,128)} %seq_ref.7) | copy-start | bytes 76
  86.1 18.8 %collective-permute-start.9 = (bf16[768,512]{1,0:T(8,128)(2,1)}, bf16[768,512]{1,0:T(8,128)(2,1)}, u32[]{:S(2)}, u32[]{:S(2)}) collective-permute-start(bf16[768,512]{1,0:T(8,128)(2,1)} %slice.11), channel_id=1, source_target_pairs={{0,96},{16,112},{32,64},{48,80},{1,97},{17,113},{33,65},{49,81},{2... | collective-permute-start | bytes 2359304 | tf_op jit(solution)/shard_map/ppermute | solution.py:632
  87.4 8.7 %collective-permute-start.8 = (bf16[16,2688]{1,0:T(8,128)(2,1)S(1)}, bf16[16,2688]{1,0:T(8,128)(2,1)S(1)}, u32[]{:S(2)}, u32[]{:S(2)}) collective-permute-start(bf16[16,2688]{1,0:T(8,128)(2,1)S(1)} %shard_map.126), channel_id=1, source_target_pairs={{64,32},{80,48},{96,0},{112,16},{65,33},{81,49},{97,1},{113,17},{6... | collective-permute-start | bytes 258056 | tf_op jit(solution)/shard_map/ppermute | solution.py:632
  96.1 20.9 %collective-permute-start.11 = (bf16[512,512]{1,0:T(8,128)(2,1)S(1)}, bf16[512,512]{1,0:T(8,128)(2,1)S(1)}, u32[]{:S(2)}, u32[]{:S(2)}) collective-permute-start(bf16[512,512]{1,0:T(8,128)(2,1)S(1)} %bitcast.50), channel_id=1, source_target_pairs={{64,32},{80,48},{96,0},{112,16},{65,33},{81,49},{97,1},{113,17},{6... | collective-permute-start | bytes 1572872 | tf_op jit(solution)/shard_map/ppermute | solution.py:632
  104.9 22.5 %all-to-all-start.3 = ((bf16[16,16,2048]{2,1,0:T(8,128)(2,1)}), bf16[16,16,2048]{2,1,0:T(8,128)(2,1)}, u32[]{:S(2)}, u32[]{:S(2)}) async-start(bf16[16,16,2048]{2,1,0:T(8,128)(2,1)} %shard_map.128), calls=%async_computation.3 | async-start | bytes 2097152 | tf_op jit(solution)/shard_map/all_to_all | solution.py:635
  117.1 1.6 collective-permute-start.12
  118.7 5.6 %collective-permute-start.13 = (bf16[128,512]{1,0:T(8,128)(2,1)S(1)}, bf16[128,512]{1,0:T(8,128)(2,1)S(1)}, u32[]{:S(2)}, u32[]{:S(2)}) collective-permute-start(bf16[128,512]{1,0:T(8,128)(2,1)S(1)} %add_convert_fusion.5), channel_id=1, source_target_pairs={{0,32},{16,48},{32,0},{48,16},{1,33},{17,49},{33,1},{49,17},{2,34}... | collective-permute-start | bytes 393224 | tf_op jit(solution)/shard_map/ppermute | solution.py:713
  124.3 1.3 collective-permute-start.14
  157.3 24.7 %all-to-all-start.5 = ((bf16[16,16,2688]{2,1,0:T(8,128)(2,1)}), bf16[16,16,2688]{2,1,0:T(8,128)(2,1)S(1)}, u32[]{:S(2)}, u32[]{:S(2)}) async-start(bf16[16,16,2688]{2,1,0:T(8,128)(2,1)} %shard_map.132), calls=%async_computation.5 | async-start | bytes 2752512 | tf_op jit(solution)/shard_map/all_to_all | solution.py:635
  161.0 61.9 %collective-permute-start.18 = (bf16[512,2048]{1,0:T(8,128)(2,1)}, bf16[512,2048]{1,0:T(8,128)(2,1)}, u32[]{:S(2)}, u32[]{:S(2)}) collective-permute-start(bf16[512,2048]{1,0:T(8,128)(2,1)} %bitcast.42), channel_id=1, source_target_pairs={{0,96},{16,112},{32,64},{48,80},{1,97},{17,113},{33,65},{49,81},{2... | collective-permute-start | bytes 6291464 | tf_op jit(solution)/shard_map/ppermute | solution.py:632
  191.8 1.6 collective-permute-start.15
  193.5 5.6 %collective-permute-start.16 = (bf16[128,512]{1,0:T(8,128)(2,1)S(1)}, bf16[128,512]{1,0:T(8,128)(2,1)S(1)}, u32[]{:S(2)}, u32[]{:S(2)}) collective-permute-start(bf16[128,512]{1,0:T(8,128)(2,1)S(1)} %add_convert_fusion.4), channel_id=1, source_target_pairs={{0,32},{16,48},{32,0},{48,16},{1,33},{17,49},{33,1},{49,17},{2,34}... | collective-permute-start | bytes 393224 | tf_op jit(solution)/shard_map/ppermute | solution.py:713
  199.1 1.3 collective-permute-start.17
  202.0 22.2 %all-to-all-start.6 = ((bf16[16,16,2048]{2,1,0:T(8,128)(2,1)}), bf16[16,16,2048]{2,1,0:T(8,128)(2,1)S(1)}, u32[]{:S(2)}, u32[]{:S(2)}) async-start(bf16[16,16,2048]{2,1,0:T(8,128)(2,1)} %get-tuple-element.101), calls=%async_computation.6 | async-start | bytes 2097152 | tf_op jit(solution)/shard_map/all_to_all | solution.py:635
  205.8 17.1 %collective-permute-start.19 = (bf16[512,512]{1,0:T(8,128)(2,1)S(1)}, bf16[512,512]{1,0:T(8,128)(2,1)S(1)}, u32[]{:S(2)}, u32[]{:S(2)}) collective-permute-start(bf16[512,512]{1,0:T(8,128)(2,1)S(1)} %bitcast.51), channel_id=1, source_target_pairs={{0,96},{16,112},{32,64},{48,80},{1,97},{17,113},{33,65},{49,81},{2... | collective-permute-start | bytes 1572872 | tf_op jit(solution)/shard_map/ppermute | solution.py:632
  222.9 24.8 %copy-start.9 = (bf16[512,512]{1,0:T(8,128)(2,1)}, bf16[512,512]{1,0:T(8,128)(2,1)S(1)}, u32[]{:S(2)}) copy-start(bf16[512,512]{1,0:T(8,128)(2,1)S(1)} %collective-permute-done.19.refs_3_) | copy-start | bytes 1572868
  256.5 1.6 collective-permute-start.20
  258.1 5.6 %collective-permute-start.21 = (bf16[128,512]{1,0:T(8,128)(2,1)S(1)}, bf16[128,512]{1,0:T(8,128)(2,1)S(1)}, u32[]{:S(2)}, u32[]{:S(2)}) collective-permute-start(bf16[128,512]{1,0:T(8,128)(2,1)S(1)} %add_convert_fusion.3), channel_id=1, source_target_pairs={{0,32},{16,48},{32,0},{48,16},{1,33},{17,49},{33,1},{49,17},{2,34}... | collective-permute-start | bytes 393224 | tf_op jit(solution)/shard_map/ppermute | solution.py:713
  263.7 1.3 collective-permute-start.22
  291.5 5.6 %collective-permute-start.23 = (bf16[16,1280]{1,0:T(8,128)(2,1)S(1)}, bf16[16,1280]{1,0:T(8,128)(2,1)S(1)}, u32[]{:S(2)}, u32[]{:S(2)}) collective-permute-start(bf16[16,1280]{1,0:T(8,128)(2,1)S(1)} %get-tuple-element.113), channel_id=1, source_target_pairs={{0,64},{64,0},{1,65},{65,1},{2,66},{66,2},{3,67},{67,3},{4,68},{68... | collective-permute-start | bytes 122888 | tf_op jit(solution)/shard_map/ppermute | solution.py:922
  (9 other events, 94.4 us)

commit v2 on v1

--- a/solution.py
+++ b/solution.py
@@ -347,7 +347,7 @@
             body(slice(at, at + QB), lanes, at + QB)
         return carry
 
-    lax.fori_loop(0, GROUP_HEADS, one_head, 0, unroll=2)
+    lax.fori_loop(0, GROUP_HEADS, one_head, 0, unroll=4)
 
 
 def clear_unreached(target, tokens):
@@ -365,14 +365,14 @@
 
 def start_qkv(qkv_ref, qkv, q_cols, sems):
     pltpu.make_async_copy(qkv_ref.at[:, q_cols:], qkv.at[:, q_cols:], sems.at[0]).start()
-    start_groups(qkv_ref, qkv, q_cols, sems, 1)
-
-
-def start_groups(source, target, q_cols, sems, first):
+    for group in range(q_cols // (GROUP_HEADS * HEAD_SIZE)):
+        start_group(qkv_ref, qkv, sems, 1, group)
+
+
+def start_group(source, target, sems, first, group):
     width = GROUP_HEADS * HEAD_SIZE
-    for group in range(q_cols // width):
-        at = (slice(None), slice(group * width, (group + 1) * width))
-        pltpu.make_async_copy(source.at[at], target.at[at], sems.at[first + group]).start()
+    at = (slice(None), slice(group * width, (group + 1) * width))
+    pltpu.make_async_copy(source.at[at], target.at[at], sems.at[first + group]).start()
 
 
 def wait_group(target, sems, first, group):
@@ -421,60 +421,30 @@
     out_ref[...] = out.astype(BF)
 
 
-def softmax_kernel(seq_ref, qkv_ref, out_ref, qkv, bias, scores, in_sems, out_sems):
-    tokens = bias.shape[0]
-    groups = out_ref.shape[0]
-    q_cols = groups * GROUP_HEADS * HEAD_SIZE
-    start_qkv(qkv_ref, qkv, q_cols, in_sems)
+def backward_kernel(
+    seq_ref, qkv_ref, grads_ref, wq0_ref, wq1_ref, wkv0_ref, wkv1_ref, out_ref,
+    qkv, grads, chunks, bias, scores, weight_grads, weights, score_grads, scaled_q, scaled_kv,
+    sems, in_sems,
+):
+    tokens, q_cols = grads.shape
+    groups = q_cols // (GROUP_HEADS * HEAD_SIZE)
+    pltpu.make_async_copy(qkv_ref.at[:, q_cols:], qkv.at[:, q_cols:], in_sems.at[0]).start()
+    start_group(qkv_ref, qkv, in_sems, 1, 0)
+    start_group(grads_ref, grads, in_sems, 1 + groups, 0)
     fill_bias(seq_ref, bias)
-    pltpu.make_async_copy(qkv.at[:, q_cols:], qkv.at[:, q_cols:], in_sems.at[0]).wait()
-    for group in range(groups):
-        at = q_cols + group * HEAD_SIZE
-        keys = qkv[:, at : at + HEAD_SIZE]
-        wait_group(qkv, in_sems, 1, group)
-        for index in range(GROUP_HEADS):
-            columns = head_columns(group * GROUP_HEADS + index)
-            lanes = slice(index * tokens, (index + 1) * tokens)
-            scores[group, :, lanes] = dot_nt(keys, qkv[:, columns])
-
-        def block(queries, lanes, reach):
-            scores[group, :reach, lanes] = weights_of(
-                scores[group, :reach, lanes], bias[:reach, queries]
-            )
-
-        softmax_blocks(tokens, block)
-        pltpu.make_async_copy(scores.at[group], out_ref.at[group], out_sems.at[group]).start()
-    for group in range(groups):
-        pltpu.make_async_copy(scores.at[group], out_ref.at[group], out_sems.at[group]).wait()
-
-
-def backward_kernel(known, pieces, seq_ref, qkv_ref, grads_ref, *refs):
-    wq0_refs, (wq1_ref, wkv0_ref, wkv1_ref, *refs) = refs[:pieces], refs[pieces:]
-    known_ref, refs = (refs[0], refs[1:]) if known else (None, refs)
-    (
-        out_ref, qkv, grads, chunks, bias, scores, weight_grads, weights, score_grads, scaled_q,
-        scaled_kv, sems, in_sems,
-    ) = refs
-    tokens, q_cols = grads.shape
-    start_qkv(qkv_ref, qkv, q_cols, in_sems)
-    groups = q_cols // (GROUP_HEADS * HEAD_SIZE)
-    start_groups(grads_ref, grads, q_cols, in_sems, 1 + groups)
-    stored = [
-        pltpu.make_async_copy(known_ref.at[group], scores.at[group], in_sems.at[5 + group])
-        for group in range(groups if known else 0)
-    ]
-    for copy in stored:
-        copy.start()
-    by_section(
-        lambda: start_joined(wq0_refs, wkv0_ref, chunks, sems),
-        lambda: start_joined([wq1_ref], wkv1_ref, chunks, sems),
-    )
-    if not known:
-        fill_bias(seq_ref, bias)
     clear_unreached(weights, tokens)
     clear_unreached(score_grads, tokens)
     kv_cols = groups * HEAD_SIZE
     pltpu.make_async_copy(qkv.at[:, q_cols:], qkv.at[:, q_cols:], in_sems.at[0]).wait()
+    wait_group(qkv, in_sems, 1, 0)
+    wait_group(grads, in_sems, 1 + groups, 0)
+    for group in range(1, groups):
+        start_group(qkv_ref, qkv, in_sems, 1, group)
+        start_group(grads_ref, grads, in_sems, 1 + groups, group)
+    by_section(
+        lambda: start_joined([wq0_ref], wkv0_ref, chunks, sems),
+        lambda: start_joined([wq1_ref], wkv1_ref, chunks, sems),
+    )
     scale_lanes = qkv[:, q_cols + 2 * kv_cols :].astype(F32)
     scale_column = jnp.sum(scale_lanes, axis=1, keepdims=True)
     scale_row = jnp.sum(scale_lanes.T, axis=0, keepdims=True) * SOFT
@@ -484,20 +454,16 @@
         keys_t = keys.astype(F32).T.astype(BF)
         at = at + kv_cols
         values = qkv[:, at : at + HEAD_SIZE]
-        wait_group(qkv, in_sems, 1, group)
-        wait_group(grads, in_sems, 1 + groups, group)
+        if group > 0:
+            wait_group(qkv, in_sems, 1, group)
+            wait_group(grads, in_sems, 1 + groups, group)
         for index in range(GROUP_HEADS):
             columns = head_columns(group * GROUP_HEADS + index)
             lanes = slice(index * tokens, (index + 1) * tokens)
-            if not known:
-                scores[group, :, lanes] = dot_nt(keys, qkv[:, columns])
+            scores[:, lanes] = dot_nt(keys, qkv[:, columns])
             weight_grads[:, lanes] = dot_nt(values, grads[:, columns])
-        if known:
-            stored[group].wait()
         def block(queries, lanes, reach):
-            weight = scores[group, :reach, lanes]
-            if not known:
-                weight = weights_of(weight, bias[:reach, queries])
+            weight = weights_of(scores[:reach, lanes], bias[:reach, queries])
             weights[:reach, lanes] = weight.astype(BF)
             weight_grad = weight_grads[:reach, lanes]
             mean = jnp.sum(weight_grad * weight, axis=0, keepdims=True)
@@ -725,7 +691,7 @@
         pair = (part.astype(F32) + mate.astype(F32)).astype(BF)
         return (pair, across, beside(across, 1)), later
 
-    around = [beside(own_x, distance) for distance in (1, 2, 3)]
+    others = [beside(own_x, distance) for distance in (1, 2, 3)]
     first_chunks = pl.pallas_call(
         first_load_kernel,
         out_shape=pltpu.VMEM((5, width, width), BF),
@@ -747,7 +713,7 @@
         ],
         compiler_params=params(24),
         cost_estimate=cost(2 * tokens * width * joined, 6 << 20),
-    )(own_x, *around, gain, first_chunks)
+    )(own_x, *others, gain, first_chunks)
     own_parts, received_x, gain_x, wq_s, wout_s = lax.optimization_barrier(
         (own_parts, received_x, gain_x, wq, wout)
     )
@@ -826,36 +792,35 @@
     h_one = rows_after(jnp.where(section == 0, own_all, mine_all), sums)
     rows_after(h_one, sum_over_mp(layer_forward(qkv_last, (wout_last, (wout_last,))))[0])
 
-    def layer_backward(qkv, head_grads, wqs, wkvs, *known, later=()):
+    def layer_backward(qkv, head_grads, wqs, wkvs, later=()):
         through = pl.pallas_call(
-            functools.partial(backward_kernel, len(known), len(wqs[0])),
+            backward_kernel,
             out_shape=shape_of((tokens, width), BF),
-            in_specs=[SMEM, ANY, ANY] + [HBM] * (3 + len(wqs[0]) + len(known)),
+            in_specs=[SMEM, ANY, ANY] + [HBM] * 4,
             out_specs=VMEM,
             scratch_shapes=[
                 vmem(tokens, joined),
                 vmem(tokens, q_cols),
                 chunks_of(5),
                 pltpu.VMEM((tokens, tokens), F32),
-                pltpu.VMEM((groups, tokens, GROUP_HEADS * tokens), F32),
+                pltpu.VMEM((tokens, GROUP_HEADS * tokens), F32),
                 pltpu.VMEM((tokens, GROUP_HEADS * tokens), F32),
                 vmem(tokens, GROUP_HEADS * tokens),
                 vmem(tokens, GROUP_HEADS * tokens),
                 vmem(q_cols, tokens),
                 vmem(tokens, 2 * kv_cols),
                 dma(5),
-                dma(7),
+                dma(5),
             ],
             compiler_params=params(32),
             cost_estimate=cost(12 * tokens * tokens * q_cols, 6 << 20),
-        )(seq_lengths, qkv, head_grads, *in_hbm(*wqs[0], *wqs[1], *wkvs, *known))
+        )(seq_lengths, qkv, head_grads, *in_hbm(*wqs, *wkvs))
         return sum_over_mp(through, *later)
 
-    groups = kv_cols // HEAD_SIZE
     sums, pieces = layer_backward(
         qkv_last,
         *in_hbm(head_grad_last),
-        ((wq_b,), (wq,)),
+        (wq_b, wq),
         (wkv_b, wkv),
         later=(wout, *wout_a),
     )
@@ -868,29 +833,9 @@
         compiler_params=params(24),
         cost_estimate=cost(2 * tokens * width * q_cols, 4 << 20),
     )(mine_all, own_all, *sums, gain_x, gain, loaded(False, pieces[:1], pieces[1:]))
-    parts, qkv_late = lax.optimization_barrier((parts, qkv_first))
-    softmax_first = pl.pallas_call(
-        softmax_kernel,
-        out_shape=pltpu.HBM((groups, tokens, GROUP_HEADS * tokens), F32),
-        in_specs=[SMEM, ANY],
-        out_specs=HBM,
-        scratch_shapes=[
-            vmem(tokens, joined),
-            pltpu.VMEM((tokens, tokens), F32),
-            pltpu.VMEM((groups, tokens, GROUP_HEADS * tokens), F32),
-            dma(3),
-            dma(2),
-        ],
-        compiler_params=params(32),
-        cost_estimate=cost(4 * tokens * tokens * q_cols, 6 << 20),
-    )(seq_lengths, *in_hbm(qkv_late))
-    parts, softmax_first, wq_a, wkv_a = lax.optimization_barrier(
-        (scatter(parts, "dp"), softmax_first, wq_a, wkv_a)
-    )
+    parts, wq_a, wkv_a = lax.optimization_barrier((scatter(parts, "dp"), wq_a, wkv_a))
     head_grad_first = spread(summed_copies(plain_sum, parts))
-    sums, _ = layer_backward(
-        *in_hbm(qkv_late), head_grad_first, ((wq,), (wq_a,)), (wkv, wkv_a), softmax_first
-    )
+    sums, _ = layer_backward(qkv_first, head_grad_first, (wq, wq_a), (wkv, wkv_a))
 
     hidden_cols = merger_weight.shape[0]
     outgoing, input_grad = pl.pallas_call(

time: 299 us -> 299 us (level)
  Pallas kernels: 53 us -> 44.9 us
  waiting for transfers between devices: 85.4 us -> 91.3 us
    pallas_call x3 -> x2, Pallas kernels: 25.3 us -> 17.4 us  [layer_backward(): pl.pallas_call(backward_kernel, out_shape=shape_of((tokens, width), BF),...]
    ppermute x11, waiting for transfers between devices: 37.5 us -> 44.4 us  [swap(): return lax.ppermute(array, ('section', 'mp'), pairs)]
  transfers between devices with their start and end apart: 30 -> 30, of which waited for: 19 -> 19; matrix products, arithmetic and copies ran while one was open for 2% -> 2% of each run, Pallas kernels for 13% -> 10%
where the time goes in v2:
time: 299 us; the launch traced here: 297 us
  waiting for transfers between devices  91.3 us (31%)
  blocking collectives  85.9 us (29%)
  starting transfers between devices  65.1 us (22%)
  Pallas kernels  44.9 us (15%)
  local copies, waits for them, and re-layouts  7.09 us (2%)
    all_to_all x3, blocking collectives, scatter(): return lax.all_to_all(array, axis, split_axis=0, concat_axis=0, tiled=True)  74.3 us
    ppermute x11, waiting for transfers between devices, swap(): return lax.ppermute(array, ('section', 'mp'), pairs)  44.4 us
    all_to_all x6, starting transfers between devices, scatter(): return lax.all_to_all(array, axis, split_axis=0, concat_axis=0, tiled=True)  36.4 us
    ppermute x11, starting transfers between devices, swap(): return lax.ppermute(array, ('section', 'mp'), pairs)  25.9 us
    ppermute x12, waiting for transfers between devices, beside(): lax.ppermute(array, 'mp', [(i, i ^ distance) for i in range(mp_count)])  21.4 us
    all_to_all x6, waiting for transfers between devices, scatter(): return lax.all_to_all(array, axis, split_axis=0, concat_axis=0, tiled=True)  20 us
    pallas_call x2, Pallas kernels, layer_backward(): pl.pallas_call(backward_kernel, out_shape=shape_of((tokens, width), BF),...  17.4 us
    all_gather x2, blocking collectives, gather(): return lax.all_gather(array, axis, axis=0, tiled=True)  11.6 us
  transfers between devices with their start and end apart: 30, of which 19 were waited for; matrix products, arithmetic and copies ran while one was open for 2% of the time, Pallas kernels for 10%

profile of v2, /device:TPU:6, one launch (start us, length us, event | category | flops | bytes accessed | tf_op | source)
XLA Modules:
  0.0 297.3 jit_solution(9706475858566193150)
XLA Ops:
  3.9 2.8 collective-permute-start.3
  11.9 8.1 %all-to-all-start = ((bf16[16,16,2688]{2,1,0:T(8,128)(2,1)}), bf16[16,16,2688]{2,1,0:T(8,128)(2,1)S(1)}, u32[]{:S(2)}, u32[]{:S(2)}) async-start(bf16[16,16,2688]{2,1,0:T(8,128)(2,1)} %get-tuple-element.56), calls=%async_computation | async-start | bytes 2752512 | tf_op jit(solution)/shard_map/all_to_all | solution.py:601
  20.0 2.2 fusion.9
  23.5 2.1 slice.11
  25.5 5.8 %all_gather.6.x_ref = bf16[256,512]{1,0:T(8,128)(2,1)S(1)} all-gather(bf16[64,512]{1,0:T(8,128)(2,1)S(1)} %collective-permute-done.3), channel_id=1, replica_groups=mesh['section'=2,'mp'=4,'dp'=16] {'mp'}, dimensions={0}, use_global_device_ids=true | all-gather | bytes 327680 | tf_op jit(solution)/shard_map/all_gather | solution.py:607
  31.3 3.3 %shard_map.124 = bf16[16,16,2688]{2,1,0:T(8,128)(2,1)} custom-call(bf16[256,512]{1,0:T(8,128)(2,1)S(1)} %all_gather.6.x_ref, f32[1,512]{1,0:T(1,128)S(1)} %bitcast.27, bf16[512,2048]{1,0:T(8,128)(2,1)} %bitcast.38, bf16[512,512]{1,0:T(8,128)(2,1)} %bitcast.45, bf16[2048,512]{1,0:T(8,128)(2,1)} %bitcast.34), custom_call_target="tpu_custom_call" | custom-call | flops 704643072 | bytes 6291456 | tf_op jit(solution)/shard_map/pallas_call | solution.py:622
  34.6 6.9 %collective-permute-done.5.refs_0_.refs_1_ = bf16[640,512]{1,0:T(8,128)(2,1)} collective-permute-done((bf16[640,512]{1,0:T(8,128)(2,1)S(1)}, bf16[640,512]{1,0:T(8,128)(2,1)}, u32[]{:S(2)}, u32[]{:S(2)}) %collective-permute-start.5) | collective-permute-done | bytes 655392 | tf_op jit(solution)/shard_map/ppermute | solution.py:598
  41.6 6.9 %all-to-all-start.1 = ((bf16[16,16,2688]{2,1,0:T(8,128)(2,1)}), bf16[16,16,2688]{2,1,0:T(8,128)(2,1)S(1)}, u32[]{:S(2)}, u32[]{:S(2)}) async-start(bf16[16,16,2688]{2,1,0:T(8,128)(2,1)} %shard_map.124), calls=%async_computation.1 | async-start | bytes 2752512 | tf_op jit(solution)/shard_map/all_to_all | solution.py:601
  48.5 2.7 collective-permute-start.10
  52.4 5.8 %all-gather = bf16[1,256,512]{2,1,0:T(8,128)(2,1)S(1)} all-gather(bf16[1,64,512]{2,1,0:T(8,128)(2,1)S(1)} %get-tuple-element.110), channel_id=2, replica_groups=mesh['section'=2,'mp'=4,'dp'=16] {'mp'}, dimensions={1}, use_global_device_ids=true | all-gather | bytes 327680 | tf_op jit(solution)/shard_map/all_gather | solution.py:607
  58.6 11.2 %collective-permute-done.6.refs_1_.refs_2_ = bf16[640,512]{1,0:T(8,128)(2,1)} collective-permute-done((bf16[640,512]{1,0:T(8,128)(2,1)}, bf16[640,512]{1,0:T(8,128)(2,1)}, u32[]{:S(2)}, u32[]{:S(2)}) %collective-permute-start.6) | collective-permute-done | bytes 655392 | tf_op jit(solution)/shard_map/ppermute | solution.py:598
  71.5 6.3 %collective-permute-done.7.second_ref = bf16[16,2688]{1,0:T(8,128)(2,1)S(1)} collective-permute-done((bf16[16,2688]{1,0:T(8,128)(2,1)S(1)}, bf16[16,2688]{1,0:T(8,128)(2,1)S(1)}, u32[]{:S(2)}, u32[]{:S(2)}) %collective-permute-start.7) | collective-permute-done | bytes 86048 | tf_op jit(solution)/shard_map/ppermute | solution.py:598
  79.0 7.1 %all-to-all-start.2 = ((bf16[16,16,2688]{2,1,0:T(8,128)(2,1)}), bf16[16,16,2688]{2,1,0:T(8,128)(2,1)S(1)}, u32[]{:S(2)}, u32[]{:S(2)}) async-start(bf16[16,16,2688]{2,1,0:T(8,128)(2,1)} %shard_map.127), calls=%async_computation.2 | async-start | bytes 2752512 | tf_op jit(solution)/shard_map/all_to_all | solution.py:601
  87.4 5.8 %collective-permute-start.8 = (bf16[16,2688]{1,0:T(8,128)(2,1)S(1)}, bf16[16,2688]{1,0:T(8,128)(2,1)S(1)}, u32[]{:S(2)}, u32[]{:S(2)}) collective-permute-start(bf16[16,2688]{1,0:T(8,128)(2,1)S(1)} %shard_map.126), channel_id=1, source_target_pairs={{64,32},{80,48},{96,0},{112,16},{65,33},{81,49},{97,1},{113,17},{6... | collective-permute-start | bytes 258056 | tf_op jit(solution)/shard_map/ppermute | solution.py:598
  93.2 2.5 collective-permute-done.8.first_ref
  95.8 6.4 %collective-permute-start.11 = (bf16[512,512]{1,0:T(8,128)(2,1)S(1)}, bf16[512,512]{1,0:T(8,128)(2,1)}, u32[]{:S(2)}, u32[]{:S(2)}) collective-permute-start(bf16[512,512]{1,0:T(8,128)(2,1)S(1)} %bitcast.50), channel_id=1, source_target_pairs={{64,32},{80,48},{96,0},{112,16},{65,33},{81,49},{97,1},{113,17},{6... | collective-permute-start | bytes 1572872 | tf_op jit(solution)/shard_map/ppermute | solution.py:598
  104.9 7.0 %all-to-all-start.3 = ((bf16[16,16,2048]{2,1,0:T(8,128)(2,1)}), bf16[16,16,2048]{2,1,0:T(8,128)(2,1)}, u32[]{:S(2)}, u32[]{:S(2)}) async-start(bf16[16,16,2048]{2,1,0:T(8,128)(2,1)} %shard_map.128), calls=%async_computation.3 | async-start | bytes 2097152 | tf_op jit(solution)/shard_map/all_to_all | solution.py:601
  111.9 5.0 %shard_map.129 = bf16[256,512]{1,0:T(8,128)(2,1)S(1)} custom-call(s32[2,3]{1,0:T(2,128)S(1)} %copy-done.2, bf16[256,2688]{1,0:T(8,128)(2,1)S(1)} %bitcast.19, bf16[2048,512]{1,0:T(8,128)(2,1)} %bitcast.35, bf16[640,512]{1,0:T(8,128)(2,1)} %collective-permute-done.5.refs_0_.refs_1_, bf16[640,512]{1,0:T(8,128)(2,1)} %collective-permute-done.6.refs_1_.refs_2_, ...), custom_call_target="tpu_custom_call" | custom-call | flops 805306368 | bytes 4194304 | tf_op jit(solution)/shard_map/pallas_call | solution.py:750
  120.4 3.8 %collective-permute-done.13.across_ref = bf16[128,512]{1,0:T(8,128)(2,1)S(1)} collective-permute-done((bf16[128,512]{1,0:T(8,128)(2,1)S(1)}, bf16[128,512]{1,0:T(8,128)(2,1)S(1)}, u32[]{:S(2)}, u32[]{:S(2)}) %collective-permute-start.13) | collective-permute-done | bytes 131104 | tf_op jit(solution)/shard_map/ppermute | solution.py:679
  127.2 28.2 %all_to_all.45.parts_ref = bf16[16,16,2688]{2,1,0:T(8,128)(2,1)S(1)} all-to-all(bf16[16,16,2688]{2,1,0:T(8,128)(2,1)} %shard_map.131), channel_id=1, replica_groups=mesh['section'=2,'mp'=4,'dp'=16] {'dp'}, dimensions={0} | all-to-all | bytes 2752512 | tf_op jit(solution)/shard_map/all_to_all | solution.py:601
  157.1 3.7 %all-to-all-start.5 = ((bf16[16,16,2688]{2,1,0:T(8,128)(2,1)}), bf16[16,16,2688]{2,1,0:T(8,128)(2,1)S(1)}, u32[]{:S(2)}, u32[]{:S(2)}) async-start(bf16[16,16,2688]{2,1,0:T(8,128)(2,1)} %shard_map.132), calls=%async_computation.5 | async-start | bytes 2752512 | tf_op jit(solution)/shard_map/all_to_all | solution.py:601
  162.1 19.6 %all-to-all-done.5 = bf16[16,16,2688]{2,1,0:T(8,128)(2,1)S(1)} async-done(((bf16[16,16,2688]{2,1,0:T(8,128)(2,1)}), bf16[16,16,2688]{2,1,0:T(8,128)(2,1)S(1)}, u32[]{:S(2)}, u32[]{:S(2)}) %all-to-all-start.5) | async-done | bytes 1376288 | tf_op jit(solution)/shard_map/all_to_all | solution.py:601
  181.7 9.1 %shard_map.133 = bf16[256,512]{1,0:T(8,128)(2,1)S(1)} custom-call(s32[2,3]{1,0:T(2,128)S(1)} %copy-done.2, bf16[256,2688]{1,0:T(8,128)(2,1)S(1)} %bitcast.21, bf16[256,2048]{1,0:T(8,128)(2,1)} %bitcast.7.grads_ref, bf16[512,2048]{1,0:T(8,128)(2,1)} %collective-permute-done.10.refs_0_.wq0_ref, bf16[512,2048]{1,0:T(8,128)(2,1)} %bitcast.42, ...), custom_call_target="tpu_custom_call" | custom-call | flops 1610612736 | bytes 6291456 | tf_op jit(solution)/shard_map/pallas_call | solution.py:796
  194.4 3.7 %collective-permute-done.16.across_ref = bf16[128,512]{1,0:T(8,128)(2,1)S(1)} collective-permute-done((bf16[128,512]{1,0:T(8,128)(2,1)S(1)}, bf16[128,512]{1,0:T(8,128)(2,1)S(1)}, u32[]{:S(2)}, u32[]{:S(2)}) %collective-permute-start.16) | collective-permute-done | bytes 131104 | tf_op jit(solution)/shard_map/ppermute | solution.py:679
  201.0 3.7 %all-to-all-start.6 = ((bf16[16,16,2048]{2,1,0:T(8,128)(2,1)}), bf16[16,16,2048]{2,1,0:T(8,128)(2,1)S(1)}, u32[]{:S(2)}, u32[]{:S(2)}) async-start(bf16[16,16,2048]{2,1,0:T(8,128)(2,1)} %get-tuple-element.96), calls=%async_computation.6 | async-start | bytes 2097152 | tf_op jit(solution)/shard_map/all_to_all | solution.py:601
  206.0 16.0 %collective-permute-done.19.wkv1_ref = bf16[512,512]{1,0:T(8,128)(2,1)S(1)} collective-permute-done((bf16[512,512]{1,0:T(8,128)(2,1)}, bf16[512,512]{1,0:T(8,128)(2,1)S(1)}, u32[]{:S(2)}, u32[]{:S(2)}) %collective-permute-start.19) | collective-permute-done | bytes 524320 | tf_op jit(solution)/shard_map/ppermute | solution.py:598
  224.6 23.0 %all_to_all.46 = bf16[16,16,2048]{2,1,0:T(8,128)(2,1)S(1)} all-to-all(bf16[16,16,2048]{2,1,0:T(8,128)(2,1)} %shard_map.136), channel_id=1, replica_groups=mesh['section'=2,'mp'=4,'dp'=16] {'dp'}, dimensions={0} | all-to-all | bytes 2097152 | tf_op jit(solution)/shard_map/all_to_all | solution.py:601
  247.6 8.3 %shard_map.137 = bf16[256,512]{1,0:T(8,128)(2,1)S(1)} custom-call(s32[2,3]{1,0:T(2,128)S(1)} %copy-done.2, bf16[256,2688]{1,0:T(8,128)(2,1)S(1)} %bitcast.20, bf16[256,2048]{1,0:T(8,128)(2,1)S(1)} %bitcast.22, bf16[512,2048]{1,0:T(8,128)(2,1)} %bitcast.43, bf16[512,2048]{1,0:T(8,128)(2,1)} %collective-permute-done.18.wq1_ref, bf16[512,512]{1,0:T(8,128)(2,1)} %bitcast.49, ...), custom_call_target="tpu_custom_call" | custom-call | flops 1610612736 | bytes 6291456 | tf_op jit(solution)/shard_map/pallas_call | solution.py:796
  257.6 5.5 %collective-permute-done.21.across_ref = bf16[128,512]{1,0:T(8,128)(2,1)S(1)} collective-permute-done((bf16[128,512]{1,0:T(8,128)(2,1)S(1)}, bf16[128,512]{1,0:T(8,128)(2,1)S(1)}, u32[]{:S(2)}, u32[]{:S(2)}) %collective-permute-start.21) | collective-permute-done | bytes 131104 | tf_op jit(solution)/shard_map/ppermute | solution.py:679
  264.5 3.1 %shard_map.138 = (bf16[16,2,16,1280]{3,2,1,0:T(8,128)(2,1)S(1)}, bf16[64,512]{1,0:T(8,128)(2,1)}) custom-call(s32[1,32]{1,0:T(1,128)S(1)} %copy-done.3, s32[1,32]{1,0:T(1,128)S(1)} %copy-done.4, bf16[256,512]{1,0:T(8,128)(2,1)S(1)} %get-tuple-element.95.last_ref, bf16[256,512]{1,0:T(8,128)(2,1)S(1)} %add_convert_fusion.pair_ref, ...), custom_call_target="tpu_custom_call" | custom-call | tf_op jit(solution)/shard_map/pallas_call | solution.py:841
  267.6 23.2 %all_to_all.47.parts_ref = bf16[16,2,16,1280]{3,2,1,0:T(8,128)(2,1)S(1)} all-to-all(bf16[16,2,16,1280]{3,2,1,0:T(8,128)(2,1)S(1)} %get-tuple-element.105), channel_id=1, replica_groups=mesh['section'=2,'mp'=4,'dp'=16] {'dp'}, dimensions={0} | all-to-all | bytes 2621440 | tf_op jit(solution)/shard_map/all_to_all | solution.py:601
  291.0 5.5 %collective-permute-done.23 = bf16[16,1280]{1,0:T(8,128)(2,1)S(1)} collective-permute-done((bf16[16,1280]{1,0:T(8,128)(2,1)S(1)}, bf16[16,1280]{1,0:T(8,128)(2,1)S(1)}, u32[]{:S(2)}, u32[]{:S(2)}) %collective-permute-start.23) | collective-permute-done | bytes 40992 | tf_op jit(solution)/shard_map/ppermute | solution.py:867
  (81 shorter events, 42.2 us)
Async XLA Ops:
  1.5 8.7 %collective-permute-start = (bf16[64,512]{1,0:T(8,128)(2,1)S(1)}, bf16[64,512]{1,0:T(8,128)(2,1)S(1)}, u32[]{:S(2)}, u32[]{:S(2)}) collective-permute-start(bf16[64,512]{1,0:T(8,128)(2,1)S(1)} %get-tuple-element.111.mine_ref), channel_id=1, source_target_pairs={{0,16},{16,0},{32,48},{48,32},{1,17},{17,1},{33,49},{49,33},{2,18}... | collective-permute-start | bytes 196616 | tf_op jit(solution)/shard_map/ppermute | solution.py:679
  1.6 8.6 %collective-permute-start.1 = (bf16[64,512]{1,0:T(8,128)(2,1)S(1)}, bf16[64,512]{1,0:T(8,128)(2,1)S(1)}, u32[]{:S(2)}, u32[]{:S(2)}) collective-permute-start(bf16[64,512]{1,0:T(8,128)(2,1)S(1)} %get-tuple-element.111.mine_ref), channel_id=1, source_target_pairs={{0,32},{16,48},{32,0},{48,16},{1,33},{17,49},{33,1},{49,17},{2,34}... | collective-permute-start | bytes 196616 | tf_op jit(solution)/shard_map/ppermute | solution.py:679
  2.5 7.7 %collective-permute-start.2 = (bf16[64,512]{1,0:T(8,128)(2,1)S(1)}, bf16[64,512]{1,0:T(8,128)(2,1)S(1)}, u32[]{:S(2)}, u32[]{:S(2)}) collective-permute-start(bf16[64,512]{1,0:T(8,128)(2,1)S(1)} %get-tuple-element.111.mine_ref), channel_id=1, source_target_pairs={{0,48},{16,32},{32,16},{48,0},{1,49},{17,33},{33,17},{49,1},{2,50}... | collective-permute-start | bytes 196616 | tf_op jit(solution)/shard_map/ppermute | solution.py:679
  3.5 8.4 %collective-permute-start.4 = (f32[1,512]{1,0:T(1,128)}, f32[1,512]{1,0:T(1,128)S(1)}, u32[]{:S(2)}, u32[]{:S(2)}) collective-permute-start(f32[1,512]{1,0:T(1,128)} %bitcast.25), channel_id=1, source_target_pairs={{0,96},{16,112},{32,64},{48,80},{64,32},{80,48},{96,0},{112,16},{1... | collective-permute-start | bytes 6152 | tf_op jit(solution)/shard_map/ppermute | solution.py:598
  3.9 8.0 %collective-permute-start.3 = (bf16[64,512]{1,0:T(8,128)(2,1)S(1)}, bf16[64,512]{1,0:T(8,128)(2,1)S(1)}, u32[]{:S(2)}, u32[]{:S(2)}) collective-permute-start(bf16[64,512]{1,0:T(8,128)(2,1)S(1)} %bitcast.52), channel_id=1, source_target_pairs={{0,96},{16,112},{32,64},{48,80},{64,32},{80,48},{96,0},{112,16},{1... | collective-permute-start | bytes 196616 | tf_op jit(solution)/shard_map/ppermute | solution.py:598
  11.9 29.7 %all-to-all-start = ((bf16[16,16,2688]{2,1,0:T(8,128)(2,1)}), bf16[16,16,2688]{2,1,0:T(8,128)(2,1)S(1)}, u32[]{:S(2)}, u32[]{:S(2)}) async-start(bf16[16,16,2688]{2,1,0:T(8,128)(2,1)} %get-tuple-element.56), calls=%async_computation | async-start | bytes 2752512 | tf_op jit(solution)/shard_map/all_to_all | solution.py:601
  22.2 19.3 %collective-permute-start.5 = (bf16[640,512]{1,0:T(8,128)(2,1)S(1)}, bf16[640,512]{1,0:T(8,128)(2,1)}, u32[]{:S(2)}, u32[]{:S(2)}) collective-permute-start(bf16[640,512]{1,0:T(8,128)(2,1)S(1)} %get-tuple-element.109), channel_id=1, source_target_pairs={{0,96},{16,112},{32,64},{48,80},{1,97},{17,113},{33,65},{49,81},{2... | collective-permute-start | bytes 1966088 | tf_op jit(solution)/shard_map/ppermute | solution.py:598
  41.6 28.2 %all-to-all-start.1 = ((bf16[16,16,2688]{2,1,0:T(8,128)(2,1)}), bf16[16,16,2688]{2,1,0:T(8,128)(2,1)S(1)}, u32[]{:S(2)}, u32[]{:S(2)}) async-start(bf16[16,16,2688]{2,1,0:T(8,128)(2,1)} %shard_map.124), calls=%async_computation.1 | async-start | bytes 2752512 | tf_op jit(solution)/shard_map/all_to_all | solution.py:601
  48.5 54.8 %collective-permute-start.10 = (bf16[512,2048]{1,0:T(8,128)(2,1)}, bf16[512,2048]{1,0:T(8,128)(2,1)}, u32[]{:S(2)}, u32[]{:S(2)}) collective-permute-start(bf16[512,2048]{1,0:T(8,128)(2,1)} %bitcast.39), channel_id=1, source_target_pairs={{64,32},{80,48},{96,0},{112,16},{65,33},{81,49},{97,1},{113,17},{6... | collective-permute-start | bytes 6291464 | tf_op jit(solution)/shard_map/ppermute | solution.py:598
  51.1 18.6 %collective-permute-start.6 = (bf16[640,512]{1,0:T(8,128)(2,1)}, bf16[640,512]{1,0:T(8,128)(2,1)}, u32[]{:S(2)}, u32[]{:S(2)}) collective-permute-start(bf16[640,512]{1,0:T(8,128)(2,1)} %get-tuple-element.61), channel_id=1, source_target_pairs={{0,96},{16,112},{32,64},{48,80},{1,97},{17,113},{33,65},{49,81},{2... | collective-permute-start | bytes 1966088 | tf_op jit(solution)/shard_map/ppermute | solution.py:598
  70.2 7.6 %collective-permute-start.7 = (bf16[16,2688]{1,0:T(8,128)(2,1)S(1)}, bf16[16,2688]{1,0:T(8,128)(2,1)S(1)}, u32[]{:S(2)}, u32[]{:S(2)}) collective-permute-start(bf16[16,2688]{1,0:T(8,128)(2,1)S(1)} %shard_map.126), channel_id=1, source_target_pairs={{0,96},{16,112},{32,64},{48,80},{1,97},{17,113},{33,65},{49,81},{2... | collective-permute-start | bytes 258056 | tf_op jit(solution)/shard_map/ppermute | solution.py:598
  79.0 25.8 %all-to-all-start.2 = ((bf16[16,16,2688]{2,1,0:T(8,128)(2,1)}), bf16[16,16,2688]{2,1,0:T(8,128)(2,1)S(1)}, u32[]{:S(2)}, u32[]{:S(2)}) async-start(bf16[16,16,2688]{2,1,0:T(8,128)(2,1)} %shard_map.127), calls=%async_computation.2 | async-start | bytes 2752512 | tf_op jit(solution)/shard_map/all_to_all | solution.py:601
  86.1 25.7 %copy-start.2 = (s32[2,3]{1,0:T(2,128)S(1)}, s32[2,3]{1,0:T(2,128)}, u32[]{:S(2)}) copy-start(s32[2,3]{1,0:T(2,128)} %seq_ref.5) | copy-start | bytes 76
  86.1 18.7 %collective-permute-start.9 = (bf16[768,512]{1,0:T(8,128)(2,1)}, bf16[768,512]{1,0:T(8,128)(2,1)S(1)}, u32[]{:S(2)}, u32[]{:S(2)}) collective-permute-start(bf16[768,512]{1,0:T(8,128)(2,1)} %slice.11), channel_id=1, source_target_pairs={{0,96},{16,112},{32,64},{48,80},{1,97},{17,113},{33,65},{49,81},{2... | collective-permute-start | bytes 2359304 | tf_op jit(solution)/shard_map/ppermute | solution.py:598
  87.4 8.3 %collective-permute-start.8 = (bf16[16,2688]{1,0:T(8,128)(2,1)S(1)}, bf16[16,2688]{1,0:T(8,128)(2,1)S(1)}, u32[]{:S(2)}, u32[]{:S(2)}) collective-permute-start(bf16[16,2688]{1,0:T(8,128)(2,1)S(1)} %shard_map.126), channel_id=1, source_target_pairs={{64,32},{80,48},{96,0},{112,16},{65,33},{81,49},{97,1},{113,17},{6... | collective-permute-start | bytes 258056 | tf_op jit(solution)/shard_map/ppermute | solution.py:598
  95.8 21.1 %collective-permute-start.11 = (bf16[512,512]{1,0:T(8,128)(2,1)S(1)}, bf16[512,512]{1,0:T(8,128)(2,1)}, u32[]{:S(2)}, u32[]{:S(2)}) collective-permute-start(bf16[512,512]{1,0:T(8,128)(2,1)S(1)} %bitcast.50), channel_id=1, source_target_pairs={{64,32},{80,48},{96,0},{112,16},{65,33},{81,49},{97,1},{113,17},{6... | collective-permute-start | bytes 1572872 | tf_op jit(solution)/shard_map/ppermute | solution.py:598
  104.9 22.3 %all-to-all-start.3 = ((bf16[16,16,2048]{2,1,0:T(8,128)(2,1)}), bf16[16,16,2048]{2,1,0:T(8,128)(2,1)}, u32[]{:S(2)}, u32[]{:S(2)}) async-start(bf16[16,16,2048]{2,1,0:T(8,128)(2,1)} %shard_map.128), calls=%async_computation.3 | async-start | bytes 2097152 | tf_op jit(solution)/shard_map/all_to_all | solution.py:601
  116.9 1.6 collective-permute-start.12
  118.5 5.6 %collective-permute-start.13 = (bf16[128,512]{1,0:T(8,128)(2,1)S(1)}, bf16[128,512]{1,0:T(8,128)(2,1)S(1)}, u32[]{:S(2)}, u32[]{:S(2)}) collective-permute-start(bf16[128,512]{1,0:T(8,128)(2,1)S(1)} %add_convert_fusion.5), channel_id=1, source_target_pairs={{0,32},{16,48},{32,0},{48,16},{1,33},{17,49},{33,1},{49,17},{2,34}... | collective-permute-start | bytes 393224 | tf_op jit(solution)/shard_map/ppermute | solution.py:679
  124.1 1.3 collective-permute-start.14
  157.1 24.7 %all-to-all-start.5 = ((bf16[16,16,2688]{2,1,0:T(8,128)(2,1)}), bf16[16,16,2688]{2,1,0:T(8,128)(2,1)S(1)}, u32[]{:S(2)}, u32[]{:S(2)}) async-start(bf16[16,16,2688]{2,1,0:T(8,128)(2,1)} %shard_map.132), calls=%async_computation.5 | async-start | bytes 2752512 | tf_op jit(solution)/shard_map/all_to_all | solution.py:601
  160.8 62.0 %collective-permute-start.18 = (bf16[512,2048]{1,0:T(8,128)(2,1)}, bf16[512,2048]{1,0:T(8,128)(2,1)}, u32[]{:S(2)}, u32[]{:S(2)}) collective-permute-start(bf16[512,2048]{1,0:T(8,128)(2,1)} %bitcast.41), channel_id=1, source_target_pairs={{0,96},{16,112},{32,64},{48,80},{1,97},{17,113},{33,65},{49,81},{2... | collective-permute-start | bytes 6291464 | tf_op jit(solution)/shard_map/ppermute | solution.py:598
  190.9 1.6 collective-permute-start.15
  192.5 5.6 %collective-permute-start.16 = (bf16[128,512]{1,0:T(8,128)(2,1)S(1)}, bf16[128,512]{1,0:T(8,128)(2,1)S(1)}, u32[]{:S(2)}, u32[]{:S(2)}) collective-permute-start(bf16[128,512]{1,0:T(8,128)(2,1)S(1)} %add_convert_fusion.4), channel_id=1, source_target_pairs={{0,32},{16,48},{32,0},{48,16},{1,33},{17,49},{33,1},{49,17},{2,34}... | collective-permute-start | bytes 393224 | tf_op jit(solution)/shard_map/ppermute | solution.py:679
  198.1 1.3 collective-permute-start.17
  201.0 22.1 %all-to-all-start.6 = ((bf16[16,16,2048]{2,1,0:T(8,128)(2,1)}), bf16[16,16,2048]{2,1,0:T(8,128)(2,1)S(1)}, u32[]{:S(2)}, u32[]{:S(2)}) async-start(bf16[16,16,2048]{2,1,0:T(8,128)(2,1)} %get-tuple-element.96), calls=%async_computation.6 | async-start | bytes 2097152 | tf_op jit(solution)/shard_map/all_to_all | solution.py:601
  204.7 17.3 %collective-permute-start.19 = (bf16[512,512]{1,0:T(8,128)(2,1)}, bf16[512,512]{1,0:T(8,128)(2,1)S(1)}, u32[]{:S(2)}, u32[]{:S(2)}) collective-permute-start(bf16[512,512]{1,0:T(8,128)(2,1)} %bitcast.48), channel_id=1, source_target_pairs={{0,96},{16,112},{32,64},{48,80},{1,97},{17,113},{33,65},{49,81},{2... | collective-permute-start | bytes 1572872 | tf_op jit(solution)/shard_map/ppermute | solution.py:598
  247.6 17.0 %copy-start.4 = (s32[1,32]{1,0:T(1,128)S(1)}, s32[1,32]{1,0:T(1,128)}, u32[]{:S(2)}) copy-start(s32[1,32]{1,0:T(1,128)} %owners_ref.1) | copy-start | bytes 388
  255.9 1.6 collective-permute-start.20
  257.5 5.6 %collective-permute-start.21 = (bf16[128,512]{1,0:T(8,128)(2,1)S(1)}, bf16[128,512]{1,0:T(8,128)(2,1)S(1)}, u32[]{:S(2)}, u32[]{:S(2)}) collective-permute-start(bf16[128,512]{1,0:T(8,128)(2,1)S(1)} %add_convert_fusion.3), channel_id=1, source_target_pairs={{0,32},{16,48},{32,0},{48,16},{1,33},{17,49},{33,1},{49,17},{2,34}... | collective-permute-start | bytes 393224 | tf_op jit(solution)/shard_map/ppermute | solution.py:679
  263.2 1.3 collective-permute-start.22
  290.9 5.6 %collective-permute-start.23 = (bf16[16,1280]{1,0:T(8,128)(2,1)S(1)}, bf16[16,1280]{1,0:T(8,128)(2,1)S(1)}, u32[]{:S(2)}, u32[]{:S(2)}) collective-permute-start(bf16[16,1280]{1,0:T(8,128)(2,1)S(1)} %get-tuple-element.107), channel_id=1, source_target_pairs={{0,64},{64,0},{1,65},{65,1},{2,66},{66,2},{3,67},{67,3},{4,68},{68... | collective-permute-start | bytes 122888 | tf_op jit(solution)/shard_map/ppermute | solution.py:867
  (7 other events, 65.9 us)

commit v3 on v2

--- a/solution.py
+++ b/solution.py
@@ -421,11 +421,12 @@
     out_ref[...] = out.astype(BF)
 
 
-def backward_kernel(
-    seq_ref, qkv_ref, grads_ref, wq0_ref, wq1_ref, wkv0_ref, wkv1_ref, out_ref,
-    qkv, grads, chunks, bias, scores, weight_grads, weights, score_grads, scaled_q, scaled_kv,
-    sems, in_sems,
-):
+def backward_kernel(pieces, seq_ref, qkv_ref, grads_ref, *refs):
+    wq0_refs, (wq1_ref, wkv0_ref, wkv1_ref, out_ref, *refs) = refs[:pieces], refs[pieces:]
+    (
+        qkv, grads, chunks, bias, scores, weight_grads, weights, score_grads, scaled_q, scaled_kv,
+        sems, in_sems,
+    ) = refs
     tokens, q_cols = grads.shape
     groups = q_cols // (GROUP_HEADS * HEAD_SIZE)
     pltpu.make_async_copy(qkv_ref.at[:, q_cols:], qkv.at[:, q_cols:], in_sems.at[0]).start()
@@ -442,7 +443,7 @@
         start_group(qkv_ref, qkv, in_sems, 1, group)
         start_group(grads_ref, grads, in_sems, 1 + groups, group)
     by_section(
-        lambda: start_joined([wq0_ref], wkv0_ref, chunks, sems),
+        lambda: start_joined(wq0_refs, wkv0_ref, chunks, sems),
         lambda: start_joined([wq1_ref], wkv1_ref, chunks, sems),
     )
     scale_lanes = qkv[:, q_cols + 2 * kv_cols :].astype(F32)
@@ -718,29 +719,32 @@
         (own_parts, received_x, gain_x, wq, wout)
     )
     own_parts = scatter(own_parts, "dp")
-    wq_b = swap(wq_s, from_second)
-    cuts = (5 * q_cols // 16, 5 * q_cols // 8)
+    quarter, cuts = q_cols // 4, (5 * q_cols // 16, 5 * q_cols // 8)
+    wq_b0 = swap(wq_s[:, :quarter], from_second)
     wout_a0 = swap(wout_s[: cuts[0]], from_first)
-    wout_a1, wout_a2 = wout_s[cuts[0] : cuts[1]], wout_s[cuts[1] :]
     other_parts = other_rows_parts(gather(received_x, "mp"))
-    own_parts, other_parts, wout_a0, wout_a1, wout_a2 = lax.optimization_barrier(
-        (own_parts, other_parts, wout_a0, wout_a1, wout_a2)
-    )
-    wout_a1 = swap(wout_a1, from_first)
+    own_parts, other_parts, wout_a0, wq_b0, wout_s, wq_s = lax.optimization_barrier(
+        (own_parts, other_parts, wout_a0, wq_b0, wout, wq)
+    )
+    wout_a1 = swap(wout_s[cuts[0] : cuts[1]], from_first)
+    wq_b1 = swap(wq_s[:, quarter:], from_second)
+    wout_a2 = wout_s[cuts[1] :]
     own = first_sum(own_parts)
-    mine_all = gather(other_x, "mp")
-    other_parts, own, mine_all, wout_a1 = lax.optimization_barrier(
-        (scatter(other_parts, "dp"), own, mine_all, wout_a1)
+    other_parts, own, other_x, wout_a2 = lax.optimization_barrier(
+        (scatter(other_parts, "dp"), own, other_x, wout_a2)
     )
     other = first_sum(other_parts)
     received = swap(other, from_first)
     received_grad, wkv_s = lax.optimization_barrier((swap(other, from_second), wkv))
     wkv_b = swap(wkv_s, from_second)
-    copies, wout_a2 = lax.optimization_barrier((chosen_copies(own, received, joined), wout_a2))
+    copies, wout_a1, wout_a2 = lax.optimization_barrier(
+        (chosen_copies(own, received, joined), wout_a1, wout_a2)
+    )
     wout_a2 = swap(wout_a2, from_first)
+    mine_all = gather(other_x, "mp")
     grad_copies = chosen_copies(received_grad, own, q_cols)
-    qkv_first, grad_copies, wout_a2, wq_b, wq_s, wkv_s = lax.optimization_barrier(
-        (spread(copies), grad_copies, wout_a2, wq_b, wq, wkv)
+    qkv_first, grad_copies, mine_all, wq_b1, wq_s, wkv_s = lax.optimization_barrier(
+        (spread(copies), grad_copies, mine_all, wq_b1, wq, wkv)
     )
     wout_a = (wout_a0, wout_a1, wout_a2)
     wq_a, wkv_a = swap(wq_s, from_first), swap(wkv_s, from_first)
@@ -774,8 +778,8 @@
         return (resident.astype(F32) + added).astype(BF)
 
     out, wkv_b = lax.optimization_barrier((layer_forward(qkv_first, (wout, wout_a)), wkv_b))
-    sums, pieces = sum_over_mp(out, wq_b, wkv_b, wq, wkv)
-    joined_last = loaded(True, pieces[:2], pieces[2:])
+    sums, pieces = sum_over_mp(out, wq_b0, wq_b1, wkv_b, wq, wkv)
+    joined_last = loaded(True, pieces[:3], pieces[3:])
     parts = pl.pallas_call(
         project_kernel,
         out_shape=pltpu.HBM((dp_count, share, joined), BF),
@@ -794,9 +798,9 @@
 
     def layer_backward(qkv, head_grads, wqs, wkvs, later=()):
         through = pl.pallas_call(
-            backward_kernel,
+            functools.partial(backward_kernel, len(wqs[0])),
             out_shape=shape_of((tokens, width), BF),
-            in_specs=[SMEM, ANY, ANY] + [HBM] * 4,
+            in_specs=[SMEM, ANY, ANY] + [HBM] * (3 + len(wqs[0])),
             out_specs=VMEM,
             scratch_shapes=[
                 vmem(tokens, joined),
@@ -814,13 +818,13 @@
             ],
             compiler_params=params(32),
             cost_estimate=cost(12 * tokens * tokens * q_cols, 6 << 20),
-        )(seq_lengths, qkv, head_grads, *in_hbm(*wqs, *wkvs))
+        )(seq_lengths, qkv, head_grads, *in_hbm(*wqs[0], *wqs[1], *wkvs))
         return sum_over_mp(through, *later)
 
     sums, pieces = layer_backward(
         qkv_last,
         *in_hbm(head_grad_last),
-        (wq_b, wq),
+        ((wq_b0, wq_b1), (wq,)),
         (wkv_b, wkv),
         later=(wout, *wout_a),
     )
@@ -835,7 +839,7 @@
     )(mine_all, own_all, *sums, gain_x, gain, loaded(False, pieces[:1], pieces[1:]))
     parts, wq_a, wkv_a = lax.optimization_barrier((scatter(parts, "dp"), wq_a, wkv_a))
     head_grad_first = spread(summed_copies(plain_sum, parts))
-    sums, _ = layer_backward(qkv_first, head_grad_first, (wq, wq_a), (wkv, wkv_a))
+    sums, _ = layer_backward(qkv_first, head_grad_first, ((wq,), (wq_a,)), (wkv, wkv_a))
 
     hidden_cols = merger_weight.shape[0]
     outgoing, input_grad = pl.pallas_call(

time: 299 us -> 304 us (1.017)
  starting transfers between devices: 65.1 us -> 74.4 us
  waiting for transfers between devices: 91.3 us -> 82.3 us
  local copies, waits for them, and re-layouts: 7.09 us -> 13.6 us
    ppermute x11 -> x12, waiting for transfers between devices: 44.4 us -> 29.7 us  [swap(): return lax.ppermute(array, ('section', 'mp'), pairs)]
    ppermute x11 -> x12, starting transfers between devices: 25.9 us -> 37.6 us  [swap(): return lax.ppermute(array, ('section', 'mp'), pairs)]
    all_to_all x6, waiting for transfers between devices: 20 us -> 26.5 us  [scatter(): return lax.all_to_all(array, axis, split_axis=0, concat_axis=0, tiled=True)]
    slice x2 -> x5, local copies, waits for them, and re-layouts: 4.31 us -> 9.04 us  [the longest x1 2.68 us: local(): wq_b1 = swap(wq_s[:, quarter:], from_second)]
    all_to_all x6, starting transfers between devices: 36.4 us -> 33.2 us  [scatter(): return lax.all_to_all(array, axis, split_axis=0, concat_axis=0, tiled=True)]
  transfers between devices with their start and end apart: 30 -> 31, of which waited for: 19 -> 18; matrix products, arithmetic and copies ran while one was open for 2% -> 4% of each run, Pallas kernels for 10% -> 10%
where the time goes in v3:
time: 304 us; the launch traced here: 302 us
  blocking collectives  83.9 us (28%)
  waiting for transfers between devices  82.3 us (27%)
  starting transfers between devices  74.4 us (24%)
  Pallas kernels  45 us (15%)
  local copies, waits for them, and re-layouts  13.6 us (4%)
    all_to_all x3, blocking collectives, scatter(): return lax.all_to_all(array, axis, split_axis=0, concat_axis=0, tiled=True)  72.4 us
    ppermute x12, starting transfers between devices, swap(): return lax.ppermute(array, ('section', 'mp'), pairs)  37.6 us
    all_to_all x6, starting transfers between devices, scatter(): return lax.all_to_all(array, axis, split_axis=0, concat_axis=0, tiled=True)  33.2 us
    ppermute x12, waiting for transfers between devices, swap(): return lax.ppermute(array, ('section', 'mp'), pairs)  29.7 us
    all_to_all x6, waiting for transfers between devices, scatter(): return lax.all_to_all(array, axis, split_axis=0, concat_axis=0, tiled=True)  26.5 us
    ppermute x12, waiting for transfers between devices, beside(): lax.ppermute(array, 'mp', [(i, i ^ distance) for i in range(mp_count)])  20.7 us
    pallas_call x2, Pallas kernels, layer_backward(): pl.pallas_call(functools.partial(backward_kernel, len(wqs[0])), out_shape...  17.4 us
    all_gather x2, blocking collectives, gather(): return lax.all_gather(array, axis, axis=0, tiled=True)  11.6 us
  transfers between devices with their start and end apart: 31, of which 18 were waited for; matrix products, arithmetic and copies ran while one was open for 4% of the time, Pallas kernels for 10%

profile of v3, /device:TPU:6, one launch (start us, length us, event | category | flops | bytes accessed | tf_op | source)
XLA Modules:
  0.0 302.3 jit_solution(10175884511133185616)
XLA Ops:
  3.9 2.8 collective-permute-start.3
  11.9 8.1 %all-to-all-start = ((bf16[16,16,2688]{2,1,0:T(8,128)(2,1)}), bf16[16,16,2688]{2,1,0:T(8,128)(2,1)S(1)}, u32[]{:S(2)}, u32[]{:S(2)}) async-start(bf16[16,16,2688]{2,1,0:T(8,128)(2,1)} %get-tuple-element.59), calls=%async_computation | async-start | bytes 2752512 | tf_op jit(solution)/shard_map/all_to_all | solution.py:602
  23.5 6.7 %collective-permute-start.6 = (bf16[512,512]{1,0:T(8,128)(2,1)S(1)}, bf16[512,512]{1,0:T(8,128)(2,1)S(1)}, u32[]{:S(2)}, u32[]{:S(2)}) collective-permute-start(bf16[512,512]{1,0:T(8,128)(2,1)S(1)} %slice.16), channel_id=1, source_target_pairs={{64,32},{80,48},{96,0},{112,16},{65,33},{81,49},{97,1},{113,17},{6... | collective-permute-start | bytes 1572872 | tf_op jit(solution)/shard_map/ppermute | solution.py:599
  30.2 5.8 %all_gather.6.x_ref = bf16[256,512]{1,0:T(8,128)(2,1)S(1)} all-gather(bf16[64,512]{1,0:T(8,128)(2,1)S(1)} %collective-permute-done.3), channel_id=1, replica_groups=mesh['section'=2,'mp'=4,'dp'=16] {'mp'}, dimensions={0}, use_global_device_ids=true | all-gather | bytes 327680 | tf_op jit(solution)/shard_map/all_gather | solution.py:608
  36.0 3.3 %shard_map.124 = bf16[16,16,2688]{2,1,0:T(8,128)(2,1)} custom-call(bf16[256,512]{1,0:T(8,128)(2,1)S(1)} %all_gather.6.x_ref, f32[1,512]{1,0:T(1,128)S(1)} %bitcast.25, bf16[512,2048]{1,0:T(8,128)(2,1)} %bitcast.31, bf16[512,512]{1,0:T(8,128)(2,1)} %bitcast.45, bf16[2048,512]{1,0:T(8,128)(2,1)} %bitcast.39), custom_call_target="tpu_custom_call" | custom-call | flops 704643072 | bytes 6291456 | tf_op jit(solution)/shard_map/pallas_call | solution.py:623
  41.6 6.9 %all-to-all-start.1 = ((bf16[16,16,2688]{2,1,0:T(8,128)(2,1)}), bf16[16,16,2688]{2,1,0:T(8,128)(2,1)S(1)}, u32[]{:S(2)}, u32[]{:S(2)}) async-start(bf16[16,16,2688]{2,1,0:T(8,128)(2,1)} %shard_map.124), calls=%async_computation.1 | async-start | bytes 2752512 | tf_op jit(solution)/shard_map/all_to_all | solution.py:602
  51.8 2.7 slice.19
  54.5 7.7 %collective-permute-start.10 = (bf16[512,1536]{1,0:T(8,128)(2,1)}, bf16[512,1536]{1,0:T(8,128)(2,1)}, u32[]{:S(2)}, u32[]{:S(2)}) collective-permute-start(bf16[512,1536]{1,0:T(8,128)(2,1)} %slice.19), channel_id=1, source_target_pairs={{64,32},{80,48},{96,0},{112,16},{65,33},{81,49},{97,1},{113,17},{6... | collective-permute-start | bytes 4718600 | tf_op jit(solution)/shard_map/ppermute | solution.py:599
  62.2 2.2 slice.17
  64.8 4.6 %all-to-all-done.1.parts_ref = bf16[16,16,2688]{2,1,0:T(8,128)(2,1)S(1)} async-done(((bf16[16,16,2688]{2,1,0:T(8,128)(2,1)}), bf16[16,16,2688]{2,1,0:T(8,128)(2,1)S(1)}, u32[]{:S(2)}, u32[]{:S(2)}) %all-to-all-start.1) | async-done | bytes 1376288 | tf_op jit(solution)/shard_map/all_to_all | solution.py:602
  71.1 6.3 %collective-permute-done.7.second_ref = bf16[16,2688]{1,0:T(8,128)(2,1)S(1)} collective-permute-done((bf16[16,2688]{1,0:T(8,128)(2,1)S(1)}, bf16[16,2688]{1,0:T(8,128)(2,1)S(1)}, u32[]{:S(2)}, u32[]{:S(2)}) %collective-permute-start.7) | collective-permute-done | bytes 86048 | tf_op jit(solution)/shard_map/ppermute | solution.py:599
  78.6 3.8 %all-to-all-start.2 = ((bf16[16,16,2688]{2,1,0:T(8,128)(2,1)}), bf16[16,16,2688]{2,1,0:T(8,128)(2,1)S(1)}, u32[]{:S(2)}, u32[]{:S(2)}) async-start(bf16[16,16,2688]{2,1,0:T(8,128)(2,1)} %shard_map.127), calls=%async_computation.2 | async-start | bytes 2752512 | tf_op jit(solution)/shard_map/all_to_all | solution.py:602
  83.8 5.8 %collective-permute-start.9 = (bf16[16,2688]{1,0:T(8,128)(2,1)S(1)}, bf16[16,2688]{1,0:T(8,128)(2,1)S(1)}, u32[]{:S(2)}, u32[]{:S(2)}) collective-permute-start(bf16[16,2688]{1,0:T(8,128)(2,1)S(1)} %shard_map.126), channel_id=1, source_target_pairs={{64,32},{80,48},{96,0},{112,16},{65,33},{81,49},{97,1},{113,17},{6... | collective-permute-start | bytes 258056 | tf_op jit(solution)/shard_map/ppermute | solution.py:599
  89.6 6.0 %collective-permute-done.9.first_ref = bf16[16,2688]{1,0:T(8,128)(2,1)S(1)} collective-permute-done((bf16[16,2688]{1,0:T(8,128)(2,1)S(1)}, bf16[16,2688]{1,0:T(8,128)(2,1)S(1)}, u32[]{:S(2)}, u32[]{:S(2)}) %collective-permute-start.9) | collective-permute-done | bytes 86048 | tf_op jit(solution)/shard_map/ppermute | solution.py:599
  95.6 6.4 %collective-permute-start.12 = (bf16[512,512]{1,0:T(8,128)(2,1)S(1)}, bf16[512,512]{1,0:T(8,128)(2,1)}, u32[]{:S(2)}, u32[]{:S(2)}) collective-permute-start(bf16[512,512]{1,0:T(8,128)(2,1)S(1)} %bitcast.50), channel_id=1, source_target_pairs={{64,32},{80,48},{96,0},{112,16},{65,33},{81,49},{97,1},{113,17},{6... | collective-permute-start | bytes 1572872 | tf_op jit(solution)/shard_map/ppermute | solution.py:599
  102.0 5.8 %all_gather.7.r1_ref.r0_ref = bf16[256,512]{1,0:T(8,128)(2,1)S(1)} all-gather(bf16[64,512]{1,0:T(8,128)(2,1)S(1)} %get-tuple-element.71), channel_id=1, replica_groups=mesh['section'=2,'mp'=4,'dp'=16] {'mp'}, dimensions={0}, use_global_device_ids=true | all-gather | bytes 327680 | tf_op jit(solution)/shard_map/all_gather | solution.py:608
  108.9 7.0 %all-to-all-start.3 = ((bf16[16,16,2048]{2,1,0:T(8,128)(2,1)}), bf16[16,16,2048]{2,1,0:T(8,128)(2,1)}, u32[]{:S(2)}, u32[]{:S(2)}) async-start(bf16[16,16,2048]{2,1,0:T(8,128)(2,1)} %shard_map.128), calls=%async_computation.3 | async-start | bytes 2097152 | tf_op jit(solution)/shard_map/all_to_all | solution.py:602
  116.9 5.0 %shard_map.129 = bf16[256,512]{1,0:T(8,128)(2,1)S(1)} custom-call(s32[2,3]{1,0:T(2,128)S(1)} %copy-done.2, bf16[256,2688]{1,0:T(8,128)(2,1)S(1)} %bitcast.19, bf16[2048,512]{1,0:T(8,128)(2,1)} %bitcast.42, bf16[640,512]{1,0:T(8,128)(2,1)} %collective-permute-done.5.refs_0_.refs_1_, bf16[640,512]{1,0:T(8,128)(2,1)} %collective-permute-done.8.refs_1_.refs_2_, ...), custom_call_target="tpu_custom_call" | custom-call | flops 805306368 | bytes 4194304 | tf_op jit(solution)/shard_map/pallas_call | solution.py:754
  125.8 3.3 %collective-permute-done.14.across_ref = bf16[128,512]{1,0:T(8,128)(2,1)S(1)} collective-permute-done((bf16[128,512]{1,0:T(8,128)(2,1)S(1)}, bf16[128,512]{1,0:T(8,128)(2,1)S(1)}, u32[]{:S(2)}, u32[]{:S(2)}) %collective-permute-start.14) | collective-permute-done | bytes 131104 | tf_op jit(solution)/shard_map/ppermute | solution.py:680
  134.1 26.3 %all_to_all.45.parts_ref = bf16[16,16,2688]{2,1,0:T(8,128)(2,1)S(1)} all-to-all(bf16[16,16,2688]{2,1,0:T(8,128)(2,1)} %shard_map.131), channel_id=1, replica_groups=mesh['section'=2,'mp'=4,'dp'=16] {'dp'}, dimensions={0} | all-to-all | bytes 2752512 | tf_op jit(solution)/shard_map/all_to_all | solution.py:602
  162.1 3.7 %all-to-all-start.5 = ((bf16[16,16,2688]{2,1,0:T(8,128)(2,1)}), bf16[16,16,2688]{2,1,0:T(8,128)(2,1)S(1)}, u32[]{:S(2)}, u32[]{:S(2)}) async-start(bf16[16,16,2688]{2,1,0:T(8,128)(2,1)} %shard_map.132), calls=%async_computation.5 | async-start | bytes 2752512 | tf_op jit(solution)/shard_map/all_to_all | solution.py:602
  167.2 19.6 %all-to-all-done.5 = bf16[16,16,2688]{2,1,0:T(8,128)(2,1)S(1)} async-done(((bf16[16,16,2688]{2,1,0:T(8,128)(2,1)}), bf16[16,16,2688]{2,1,0:T(8,128)(2,1)S(1)}, u32[]{:S(2)}, u32[]{:S(2)}) %all-to-all-start.5) | async-done | bytes 1376288 | tf_op jit(solution)/shard_map/all_to_all | solution.py:602
  186.8 9.1 %shard_map.133 = bf16[256,512]{1,0:T(8,128)(2,1)S(1)} custom-call(s32[2,3]{1,0:T(2,128)S(1)} %copy-done.2, bf16[256,2688]{1,0:T(8,128)(2,1)S(1)} %bitcast.21, bf16[256,2048]{1,0:T(8,128)(2,1)} %bitcast.6.grads_ref, bf16[512,512]{1,0:T(8,128)(2,1)} %copy-done.7, bf16[512,1536]{1,0:T(8,128)(2,1)} %collective-permute-done.10.refs_1_, ...), custom_call_target="tpu_custom_call" | custom-call | flops 1610612736 | bytes 6291456 | tf_op jit(solution)/shard_map/pallas_call | solution.py:800
  199.7 3.5 %collective-permute-done.17.across_ref = bf16[128,512]{1,0:T(8,128)(2,1)S(1)} collective-permute-done((bf16[128,512]{1,0:T(8,128)(2,1)S(1)}, bf16[128,512]{1,0:T(8,128)(2,1)S(1)}, u32[]{:S(2)}, u32[]{:S(2)}) %collective-permute-start.17) | collective-permute-done | bytes 131104 | tf_op jit(solution)/shard_map/ppermute | solution.py:680
  206.1 3.7 %all-to-all-start.6 = ((bf16[16,16,2048]{2,1,0:T(8,128)(2,1)}), bf16[16,16,2048]{2,1,0:T(8,128)(2,1)S(1)}, u32[]{:S(2)}, u32[]{:S(2)}) async-start(bf16[16,16,2048]{2,1,0:T(8,128)(2,1)} %get-tuple-element.102), calls=%async_computation.6 | async-start | bytes 2097152 | tf_op jit(solution)/shard_map/all_to_all | solution.py:602
  211.1 16.0 %collective-permute-done.20.refs_3_ = bf16[512,512]{1,0:T(8,128)(2,1)S(1)} collective-permute-done((bf16[512,512]{1,0:T(8,128)(2,1)}, bf16[512,512]{1,0:T(8,128)(2,1)S(1)}, u32[]{:S(2)}, u32[]{:S(2)}) %collective-permute-start.20) | collective-permute-done | bytes 524320 | tf_op jit(solution)/shard_map/ppermute | solution.py:599
  229.6 23.0 %all_to_all.46 = bf16[16,16,2048]{2,1,0:T(8,128)(2,1)S(1)} all-to-all(bf16[16,16,2048]{2,1,0:T(8,128)(2,1)} %shard_map.136), channel_id=1, replica_groups=mesh['section'=2,'mp'=4,'dp'=16] {'dp'}, dimensions={0} | all-to-all | bytes 2097152 | tf_op jit(solution)/shard_map/all_to_all | solution.py:602
  252.6 8.3 %shard_map.137 = bf16[256,512]{1,0:T(8,128)(2,1)S(1)} custom-call(s32[2,3]{1,0:T(2,128)S(1)} %copy-done.2, bf16[256,2688]{1,0:T(8,128)(2,1)S(1)} %bitcast.20, bf16[256,2048]{1,0:T(8,128)(2,1)S(1)} %bitcast.22, bf16[512,2048]{1,0:T(8,128)(2,1)} %bitcast.36, bf16[512,2048]{1,0:T(8,128)(2,1)} %collective-permute-done.19.refs_1_, bf16[512,512]{1,0:T(8,128)(2,1)} %bitcast.49, ...), custom_call_target="tpu_custom_call" | custom-call | flops 1610612736 | bytes 6291456 | tf_op jit(solution)/shard_map/pallas_call | solution.py:800
  262.7 5.5 %collective-permute-done.22.across_ref = bf16[128,512]{1,0:T(8,128)(2,1)S(1)} collective-permute-done((bf16[128,512]{1,0:T(8,128)(2,1)S(1)}, bf16[128,512]{1,0:T(8,128)(2,1)S(1)}, u32[]{:S(2)}, u32[]{:S(2)}) %collective-permute-start.22) | collective-permute-done | bytes 131104 | tf_op jit(solution)/shard_map/ppermute | solution.py:680
  269.5 3.1 %shard_map.138 = (bf16[16,2,16,1280]{3,2,1,0:T(8,128)(2,1)S(1)}, bf16[64,512]{1,0:T(8,128)(2,1)}) custom-call(s32[1,32]{1,0:T(1,128)S(1)} %copy-done.3, s32[1,32]{1,0:T(1,128)S(1)} %copy-done.4, bf16[256,512]{1,0:T(8,128)(2,1)S(1)} %get-tuple-element.101.last_ref, bf16[256,512]{1,0:T(8,128)(2,1)S(1)} %add_convert_fusion.pair_ref, ...), custom_call_target="tpu_custom_call" | custom-call | tf_op jit(solution)/shard_map/pallas_call | solution.py:845
  272.6 23.1 %all_to_all.47.parts_ref = bf16[16,2,16,1280]{3,2,1,0:T(8,128)(2,1)S(1)} all-to-all(bf16[16,2,16,1280]{3,2,1,0:T(8,128)(2,1)S(1)} %get-tuple-element.111), channel_id=1, replica_groups=mesh['section'=2,'mp'=4,'dp'=16] {'dp'}, dimensions={0} | all-to-all | bytes 2621440 | tf_op jit(solution)/shard_map/all_to_all | solution.py:602
  296.0 5.5 %collective-permute-done.24 = bf16[16,1280]{1,0:T(8,128)(2,1)S(1)} collective-permute-done((bf16[16,1280]{1,0:T(8,128)(2,1)S(1)}, bf16[16,1280]{1,0:T(8,128)(2,1)S(1)}, u32[]{:S(2)}, u32[]{:S(2)}) %collective-permute-start.24) | collective-permute-done | bytes 40992 | tf_op jit(solution)/shard_map/ppermute | solution.py:871
  (88 shorter events, 50.7 us)
Async XLA Ops:
  1.5 8.7 %collective-permute-start = (bf16[64,512]{1,0:T(8,128)(2,1)S(1)}, bf16[64,512]{1,0:T(8,128)(2,1)S(1)}, u32[]{:S(2)}, u32[]{:S(2)}) collective-permute-start(bf16[64,512]{1,0:T(8,128)(2,1)S(1)} %get-tuple-element.115.mine_ref), channel_id=1, source_target_pairs={{0,16},{16,0},{32,48},{48,32},{1,17},{17,1},{33,49},{49,33},{2,18}... | collective-permute-start | bytes 196616 | tf_op jit(solution)/shard_map/ppermute | solution.py:680
  1.6 8.6 %collective-permute-start.1 = (bf16[64,512]{1,0:T(8,128)(2,1)S(1)}, bf16[64,512]{1,0:T(8,128)(2,1)S(1)}, u32[]{:S(2)}, u32[]{:S(2)}) collective-permute-start(bf16[64,512]{1,0:T(8,128)(2,1)S(1)} %get-tuple-element.115.mine_ref), channel_id=1, source_target_pairs={{0,32},{16,48},{32,0},{48,16},{1,33},{17,49},{33,1},{49,17},{2,34}... | collective-permute-start | bytes 196616 | tf_op jit(solution)/shard_map/ppermute | solution.py:680
  2.5 7.7 %collective-permute-start.2 = (bf16[64,512]{1,0:T(8,128)(2,1)S(1)}, bf16[64,512]{1,0:T(8,128)(2,1)S(1)}, u32[]{:S(2)}, u32[]{:S(2)}) collective-permute-start(bf16[64,512]{1,0:T(8,128)(2,1)S(1)} %get-tuple-element.115.mine_ref), channel_id=1, source_target_pairs={{0,48},{16,32},{32,16},{48,0},{1,49},{17,33},{33,17},{49,1},{2,50}... | collective-permute-start | bytes 196616 | tf_op jit(solution)/shard_map/ppermute | solution.py:680
  3.5 8.4 %collective-permute-start.4 = (f32[1,512]{1,0:T(1,128)}, f32[1,512]{1,0:T(1,128)S(1)}, u32[]{:S(2)}, u32[]{:S(2)}) collective-permute-start(f32[1,512]{1,0:T(1,128)} %bitcast.23), channel_id=1, source_target_pairs={{0,96},{16,112},{32,64},{48,80},{64,32},{80,48},{96,0},{112,16},{1... | collective-permute-start | bytes 6152 | tf_op jit(solution)/shard_map/ppermute | solution.py:599
  3.9 8.0 %collective-permute-start.3 = (bf16[64,512]{1,0:T(8,128)(2,1)S(1)}, bf16[64,512]{1,0:T(8,128)(2,1)S(1)}, u32[]{:S(2)}, u32[]{:S(2)}) collective-permute-start(bf16[64,512]{1,0:T(8,128)(2,1)S(1)} %get-tuple-element.71), channel_id=1, source_target_pairs={{0,96},{16,112},{32,64},{48,80},{64,32},{80,48},{96,0},{112,16},{1... | collective-permute-start | bytes 196616 | tf_op jit(solution)/shard_map/ppermute | solution.py:599
  11.9 29.7 %all-to-all-start = ((bf16[16,16,2688]{2,1,0:T(8,128)(2,1)}), bf16[16,16,2688]{2,1,0:T(8,128)(2,1)S(1)}, u32[]{:S(2)}, u32[]{:S(2)}) async-start(bf16[16,16,2688]{2,1,0:T(8,128)(2,1)} %get-tuple-element.59), calls=%async_computation | async-start | bytes 2752512 | tf_op jit(solution)/shard_map/all_to_all | solution.py:602
  21.1 20.4 %collective-permute-start.5 = (bf16[640,512]{1,0:T(8,128)(2,1)S(1)}, bf16[640,512]{1,0:T(8,128)(2,1)}, u32[]{:S(2)}, u32[]{:S(2)}) collective-permute-start(bf16[640,512]{1,0:T(8,128)(2,1)S(1)} %slice.15), channel_id=1, source_target_pairs={{0,96},{16,112},{32,64},{48,80},{1,97},{17,113},{33,65},{49,81},{2... | collective-permute-start | bytes 1966088 | tf_op jit(solution)/shard_map/ppermute | solution.py:599
  23.5 17.2 %collective-permute-start.6 = (bf16[512,512]{1,0:T(8,128)(2,1)S(1)}, bf16[512,512]{1,0:T(8,128)(2,1)S(1)}, u32[]{:S(2)}, u32[]{:S(2)}) collective-permute-start(bf16[512,512]{1,0:T(8,128)(2,1)S(1)} %slice.16), channel_id=1, source_target_pairs={{64,32},{80,48},{96,0},{112,16},{65,33},{81,49},{97,1},{113,17},{6... | collective-permute-start | bytes 1572872 | tf_op jit(solution)/shard_map/ppermute | solution.py:599
  41.6 27.7 %all-to-all-start.1 = ((bf16[16,16,2688]{2,1,0:T(8,128)(2,1)}), bf16[16,16,2688]{2,1,0:T(8,128)(2,1)S(1)}, u32[]{:S(2)}, u32[]{:S(2)}) async-start(bf16[16,16,2688]{2,1,0:T(8,128)(2,1)} %shard_map.124), calls=%async_computation.1 | async-start | bytes 2752512 | tf_op jit(solution)/shard_map/all_to_all | solution.py:602
  50.5 28.1 %collective-permute-start.8 = (bf16[640,512]{1,0:T(8,128)(2,1)}, bf16[640,512]{1,0:T(8,128)(2,1)}, u32[]{:S(2)}, u32[]{:S(2)}) collective-permute-start(bf16[640,512]{1,0:T(8,128)(2,1)} %slice.18), channel_id=1, source_target_pairs={{0,96},{16,112},{32,64},{48,80},{1,97},{17,113},{33,65},{49,81},{2... | collective-permute-start | bytes 1966088 | tf_op jit(solution)/shard_map/ppermute | solution.py:599
  54.5 54.4 %collective-permute-start.10 = (bf16[512,1536]{1,0:T(8,128)(2,1)}, bf16[512,1536]{1,0:T(8,128)(2,1)}, u32[]{:S(2)}, u32[]{:S(2)}) collective-permute-start(bf16[512,1536]{1,0:T(8,128)(2,1)} %slice.19), channel_id=1, source_target_pairs={{64,32},{80,48},{96,0},{112,16},{65,33},{81,49},{97,1},{113,17},{6... | collective-permute-start | bytes 4718600 | tf_op jit(solution)/shard_map/ppermute | solution.py:599
  69.8 7.6 %collective-permute-start.7 = (bf16[16,2688]{1,0:T(8,128)(2,1)S(1)}, bf16[16,2688]{1,0:T(8,128)(2,1)S(1)}, u32[]{:S(2)}, u32[]{:S(2)}) collective-permute-start(bf16[16,2688]{1,0:T(8,128)(2,1)S(1)} %shard_map.126), channel_id=1, source_target_pairs={{0,96},{16,112},{32,64},{48,80},{1,97},{17,113},{33,65},{49,81},{2... | collective-permute-start | bytes 258056 | tf_op jit(solution)/shard_map/ppermute | solution.py:599
  78.6 17.0 %copy-start.5 = (bf16[64,8,2,256]{3,1,2,0:T(8,128)(2,1)S(1)}, bf16[64,8,2,256]{3,1,2,0:T(8,128)(2,1)}, u32[]{:S(2)}) copy-start(bf16[64,8,2,256]{3,1,2,0:T(8,128)(2,1)} %copy.13) | copy-start | bytes 1572868
  78.6 30.3 %all-to-all-start.2 = ((bf16[16,16,2688]{2,1,0:T(8,128)(2,1)}), bf16[16,16,2688]{2,1,0:T(8,128)(2,1)S(1)}, u32[]{:S(2)}, u32[]{:S(2)}) async-start(bf16[16,16,2688]{2,1,0:T(8,128)(2,1)} %shard_map.127), calls=%async_computation.2 | async-start | bytes 2752512 | tf_op jit(solution)/shard_map/all_to_all | solution.py:602
  82.5 33.4 %collective-permute-start.11 = (bf16[768,512]{1,0:T(8,128)(2,1)}, bf16[768,512]{1,0:T(8,128)(2,1)S(1)}, u32[]{:S(2)}, u32[]{:S(2)}) collective-permute-start(bf16[768,512]{1,0:T(8,128)(2,1)} %slice.17), channel_id=1, source_target_pairs={{0,96},{16,112},{32,64},{48,80},{1,97},{17,113},{33,65},{49,81},{2... | collective-permute-start | bytes 2359304 | tf_op jit(solution)/shard_map/ppermute | solution.py:599
  83.8 11.8 %collective-permute-start.9 = (bf16[16,2688]{1,0:T(8,128)(2,1)S(1)}, bf16[16,2688]{1,0:T(8,128)(2,1)S(1)}, u32[]{:S(2)}, u32[]{:S(2)}) collective-permute-start(bf16[16,2688]{1,0:T(8,128)(2,1)S(1)} %shard_map.126), channel_id=1, source_target_pairs={{64,32},{80,48},{96,0},{112,16},{65,33},{81,49},{97,1},{113,17},{6... | collective-permute-start | bytes 258056 | tf_op jit(solution)/shard_map/ppermute | solution.py:599
  95.6 26.3 %collective-permute-start.12 = (bf16[512,512]{1,0:T(8,128)(2,1)S(1)}, bf16[512,512]{1,0:T(8,128)(2,1)}, u32[]{:S(2)}, u32[]{:S(2)}) collective-permute-start(bf16[512,512]{1,0:T(8,128)(2,1)S(1)} %bitcast.50), channel_id=1, source_target_pairs={{64,32},{80,48},{96,0},{112,16},{65,33},{81,49},{97,1},{113,17},{6... | collective-permute-start | bytes 1572872 | tf_op jit(solution)/shard_map/ppermute | solution.py:599
  108.9 25.2 %all-to-all-start.3 = ((bf16[16,16,2048]{2,1,0:T(8,128)(2,1)}), bf16[16,16,2048]{2,1,0:T(8,128)(2,1)}, u32[]{:S(2)}, u32[]{:S(2)}) async-start(bf16[16,16,2048]{2,1,0:T(8,128)(2,1)} %shard_map.128), calls=%async_computation.3 | async-start | bytes 2097152 | tf_op jit(solution)/shard_map/all_to_all | solution.py:602
  121.9 1.6 collective-permute-start.13
  123.5 5.6 %collective-permute-start.14 = (bf16[128,512]{1,0:T(8,128)(2,1)S(1)}, bf16[128,512]{1,0:T(8,128)(2,1)S(1)}, u32[]{:S(2)}, u32[]{:S(2)}) collective-permute-start(bf16[128,512]{1,0:T(8,128)(2,1)S(1)} %add_convert_fusion.5), channel_id=1, source_target_pairs={{0,32},{16,48},{32,0},{48,16},{1,33},{17,49},{33,1},{49,17},{2,34}... | collective-permute-start | bytes 393224 | tf_op jit(solution)/shard_map/ppermute | solution.py:680
  129.1 1.3 collective-permute-start.15
  162.1 24.7 %all-to-all-start.5 = ((bf16[16,16,2688]{2,1,0:T(8,128)(2,1)}), bf16[16,16,2688]{2,1,0:T(8,128)(2,1)S(1)}, u32[]{:S(2)}, u32[]{:S(2)}) async-start(bf16[16,16,2688]{2,1,0:T(8,128)(2,1)} %shard_map.132), calls=%async_computation.5 | async-start | bytes 2752512 | tf_op jit(solution)/shard_map/all_to_all | solution.py:602
  165.9 62.0 %collective-permute-start.19 = (bf16[512,2048]{1,0:T(8,128)(2,1)}, bf16[512,2048]{1,0:T(8,128)(2,1)}, u32[]{:S(2)}, u32[]{:S(2)}) collective-permute-start(bf16[512,2048]{1,0:T(8,128)(2,1)} %bitcast.34), channel_id=1, source_target_pairs={{0,96},{16,112},{32,64},{48,80},{1,97},{17,113},{33,65},{49,81},{2... | collective-permute-start | bytes 6291464 | tf_op jit(solution)/shard_map/ppermute | solution.py:599
  195.9 1.6 collective-permute-start.16
  197.6 5.6 %collective-permute-start.17 = (bf16[128,512]{1,0:T(8,128)(2,1)S(1)}, bf16[128,512]{1,0:T(8,128)(2,1)S(1)}, u32[]{:S(2)}, u32[]{:S(2)}) collective-permute-start(bf16[128,512]{1,0:T(8,128)(2,1)S(1)} %add_convert_fusion.4), channel_id=1, source_target_pairs={{0,32},{16,48},{32,0},{48,16},{1,33},{17,49},{33,1},{49,17},{2,34}... | collective-permute-start | bytes 393224 | tf_op jit(solution)/shard_map/ppermute | solution.py:680
  203.2 1.3 collective-permute-start.18
  206.1 22.1 %all-to-all-start.6 = ((bf16[16,16,2048]{2,1,0:T(8,128)(2,1)}), bf16[16,16,2048]{2,1,0:T(8,128)(2,1)S(1)}, u32[]{:S(2)}, u32[]{:S(2)}) async-start(bf16[16,16,2048]{2,1,0:T(8,128)(2,1)} %get-tuple-element.102), calls=%async_computation.6 | async-start | bytes 2097152 | tf_op jit(solution)/shard_map/all_to_all | solution.py:602
  209.8 17.3 %collective-permute-start.20 = (bf16[512,512]{1,0:T(8,128)(2,1)}, bf16[512,512]{1,0:T(8,128)(2,1)S(1)}, u32[]{:S(2)}, u32[]{:S(2)}) collective-permute-start(bf16[512,512]{1,0:T(8,128)(2,1)} %bitcast.48), channel_id=1, source_target_pairs={{0,96},{16,112},{32,64},{48,80},{1,97},{17,113},{33,65},{49,81},{2... | collective-permute-start | bytes 1572872 | tf_op jit(solution)/shard_map/ppermute | solution.py:599
  260.9 1.6 collective-permute-start.21
  262.6 5.6 %collective-permute-start.22 = (bf16[128,512]{1,0:T(8,128)(2,1)S(1)}, bf16[128,512]{1,0:T(8,128)(2,1)S(1)}, u32[]{:S(2)}, u32[]{:S(2)}) collective-permute-start(bf16[128,512]{1,0:T(8,128)(2,1)S(1)} %add_convert_fusion.3), channel_id=1, source_target_pairs={{0,32},{16,48},{32,0},{48,16},{1,33},{17,49},{33,1},{49,17},{2,34}... | collective-permute-start | bytes 393224 | tf_op jit(solution)/shard_map/ppermute | solution.py:680
  268.2 1.3 collective-permute-start.23
  295.9 5.6 %collective-permute-start.24 = (bf16[16,1280]{1,0:T(8,128)(2,1)S(1)}, bf16[16,1280]{1,0:T(8,128)(2,1)S(1)}, u32[]{:S(2)}, u32[]{:S(2)}) collective-permute-start(bf16[16,1280]{1,0:T(8,128)(2,1)S(1)} %get-tuple-element.113), channel_id=1, source_target_pairs={{0,64},{64,0},{1,65},{65,1},{2,66},{66,2},{3,67},{67,3},{4,68},{68... | collective-permute-start | bytes 122888 | tf_op jit(solution)/shard_map/ppermute | solution.py:871
  (9 other events, 70.0 us)

commit v4 on v2

--- a/solution.py
+++ b/solution.py
@@ -729,18 +729,20 @@
     wout_a1 = swap(wout_a1, from_first)
     own = first_sum(own_parts)
     mine_all = gather(other_x, "mp")
-    other_parts, own, mine_all, wout_a1 = lax.optimization_barrier(
-        (scatter(other_parts, "dp"), own, mine_all, wout_a1)
+    other_parts, own, mine_all = lax.optimization_barrier(
+        (scatter(other_parts, "dp"), own, mine_all)
     )
     other = first_sum(other_parts)
     received = swap(other, from_first)
     received_grad, wkv_s = lax.optimization_barrier((swap(other, from_second), wkv))
     wkv_b = swap(wkv_s, from_second)
-    copies, wout_a2 = lax.optimization_barrier((chosen_copies(own, received, joined), wout_a2))
+    copies, wout_a1, wout_a2 = lax.optimization_barrier(
+        (chosen_copies(own, received, joined), wout_a1, wout_a2)
+    )
     wout_a2 = swap(wout_a2, from_first)
     grad_copies = chosen_copies(received_grad, own, q_cols)
-    qkv_first, grad_copies, wout_a2, wq_b, wq_s, wkv_s = lax.optimization_barrier(
-        (spread(copies), grad_copies, wout_a2, wq_b, wq, wkv)
+    qkv_first, grad_copies, wq_b, wq_s, wkv_s = lax.optimization_barrier(
+        (spread(copies), grad_copies, wq_b, wq, wkv)
     )
     wout_a = (wout_a0, wout_a1, wout_a2)
     wq_a, wkv_a = swap(wq_s, from_first), swap(wkv_s, from_first)

time: 299 us -> 298 us (level)
  starting transfers between devices: 65.1 us -> 61.8 us
    all_to_all x6, waiting for transfers between devices: 20 us -> 29.6 us  [scatter(): return lax.all_to_all(array, axis, split_axis=0, concat_axis=0, tiled=True)]
    ppermute x11, waiting for transfers between devices: 44.4 us -> 36.5 us  [swap(): return lax.ppermute(array, ('section', 'mp'), pairs)]
    all_to_all x6, starting transfers between devices: 36.4 us -> 33.1 us  [scatter(): return lax.all_to_all(array, axis, split_axis=0, concat_axis=0, tiled=True)]
  transfers between devices with their start and end apart: 30 -> 30, of which waited for: 19 -> 18; matrix products, arithmetic and copies ran while one was open for 2% -> 2% of each run, Pallas kernels for 10% -> 10%
where the time goes in v4:
time: 298 us; the launch traced here: 297 us
  waiting for transfers between devices  92.9 us (31%)
  blocking collectives  85.9 us (29%)
  starting transfers between devices  61.8 us (21%)
  Pallas kernels  44.9 us (15%)
  local copies, waits for them, and re-layouts  7.96 us (3%)
    all_to_all x3, blocking collectives, scatter(): return lax.all_to_all(array, axis, split_axis=0, concat_axis=0, tiled=True)  74.3 us
    ppermute x11, waiting for transfers between devices, swap(): return lax.ppermute(array, ('section', 'mp'), pairs)  36.5 us
    all_to_all x6, starting transfers between devices, scatter(): return lax.all_to_all(array, axis, split_axis=0, concat_axis=0, tiled=True)  33.1 us
    all_to_all x6, waiting for transfers between devices, scatter(): return lax.all_to_all(array, axis, split_axis=0, concat_axis=0, tiled=True)  29.6 us
    ppermute x11, starting transfers between devices, swap(): return lax.ppermute(array, ('section', 'mp'), pairs)  25.9 us
    ppermute x12, waiting for transfers between devices, beside(): lax.ppermute(array, 'mp', [(i, i ^ distance) for i in range(mp_count)])  21.4 us
    pallas_call x2, Pallas kernels, layer_backward(): pl.pallas_call(backward_kernel, out_shape=shape_of((tokens, width), BF),...  17.4 us
    all_gather x2, blocking collectives, gather(): return lax.all_gather(array, axis, axis=0, tiled=True)  11.6 us
  transfers between devices with their start and end apart: 30, of which 18 were waited for; matrix products, arithmetic and copies ran while one was open for 2% of the time, Pallas kernels for 10%

profile of v4, /device:TPU:6, one launch (start us, length us, event | category | flops | bytes accessed | tf_op | source)
XLA Modules:
  0.0 296.6 jit_solution(7447622527635844496)
XLA Ops:
  3.9 2.8 collective-permute-start.3
  11.9 8.1 %all-to-all-start = ((bf16[16,16,2688]{2,1,0:T(8,128)(2,1)}), bf16[16,16,2688]{2,1,0:T(8,128)(2,1)S(1)}, u32[]{:S(2)}, u32[]{:S(2)}) async-start(bf16[16,16,2688]{2,1,0:T(8,128)(2,1)} %get-tuple-element.55), calls=%async_computation | async-start | bytes 2752512 | tf_op jit(solution)/shard_map/all_to_all | solution.py:601
  20.0 2.2 fusion.9
  23.5 2.1 slice.11
  25.5 5.8 %all_gather.6.x_ref = bf16[256,512]{1,0:T(8,128)(2,1)S(1)} all-gather(bf16[64,512]{1,0:T(8,128)(2,1)S(1)} %collective-permute-done.3), channel_id=1, replica_groups=mesh['section'=2,'mp'=4,'dp'=16] {'mp'}, dimensions={0}, use_global_device_ids=true | all-gather | bytes 327680 | tf_op jit(solution)/shard_map/all_gather | solution.py:607
  31.3 3.3 %shard_map.124 = bf16[16,16,2688]{2,1,0:T(8,128)(2,1)} custom-call(bf16[256,512]{1,0:T(8,128)(2,1)S(1)} %all_gather.6.x_ref, f32[1,512]{1,0:T(1,128)S(1)} %bitcast.27, bf16[512,2048]{1,0:T(8,128)(2,1)} %bitcast.38, bf16[512,512]{1,0:T(8,128)(2,1)} %bitcast.45, bf16[2048,512]{1,0:T(8,128)(2,1)} %bitcast.34), custom_call_target="tpu_custom_call" | custom-call | flops 704643072 | bytes 6291456 | tf_op jit(solution)/shard_map/pallas_call | solution.py:622
  34.6 6.9 %collective-permute-done.5.refs_0_.refs_1_ = bf16[640,512]{1,0:T(8,128)(2,1)} collective-permute-done((bf16[640,512]{1,0:T(8,128)(2,1)S(1)}, bf16[640,512]{1,0:T(8,128)(2,1)}, u32[]{:S(2)}, u32[]{:S(2)}) %collective-permute-start.5) | collective-permute-done | bytes 655392 | tf_op jit(solution)/shard_map/ppermute | solution.py:598
  41.6 6.9 %all-to-all-start.1 = ((bf16[16,16,2688]{2,1,0:T(8,128)(2,1)}), bf16[16,16,2688]{2,1,0:T(8,128)(2,1)S(1)}, u32[]{:S(2)}, u32[]{:S(2)}) async-start(bf16[16,16,2688]{2,1,0:T(8,128)(2,1)} %shard_map.124), calls=%async_computation.1 | async-start | bytes 2752512 | tf_op jit(solution)/shard_map/all_to_all | solution.py:601
  48.5 2.7 collective-permute-start.9
  52.4 5.8 %all-gather = bf16[1,256,512]{2,1,0:T(8,128)(2,1)S(1)} all-gather(bf16[1,64,512]{2,1,0:T(8,128)(2,1)S(1)} %get-tuple-element.108), channel_id=2, replica_groups=mesh['section'=2,'mp'=4,'dp'=16] {'mp'}, dimensions={1}, use_global_device_ids=true | all-gather | bytes 327680 | tf_op jit(solution)/shard_map/all_gather | solution.py:607
  58.6 9.6 %all-to-all-done.1.parts_ref = bf16[16,16,2688]{2,1,0:T(8,128)(2,1)S(1)} async-done(((bf16[16,16,2688]{2,1,0:T(8,128)(2,1)}), bf16[16,16,2688]{2,1,0:T(8,128)(2,1)S(1)}, u32[]{:S(2)}, u32[]{:S(2)}) %all-to-all-start.1) | async-done | bytes 1376288 | tf_op jit(solution)/shard_map/all_to_all | solution.py:601
  69.9 6.3 %collective-permute-done.6.second_ref = bf16[16,2688]{1,0:T(8,128)(2,1)S(1)} collective-permute-done((bf16[16,2688]{1,0:T(8,128)(2,1)S(1)}, bf16[16,2688]{1,0:T(8,128)(2,1)S(1)}, u32[]{:S(2)}, u32[]{:S(2)}) %collective-permute-start.6) | collective-permute-done | bytes 86048 | tf_op jit(solution)/shard_map/ppermute | solution.py:598
  77.5 3.8 %all-to-all-start.2 = ((bf16[16,16,2688]{2,1,0:T(8,128)(2,1)}), bf16[16,16,2688]{2,1,0:T(8,128)(2,1)S(1)}, u32[]{:S(2)}, u32[]{:S(2)}) async-start(bf16[16,16,2688]{2,1,0:T(8,128)(2,1)} %shard_map.127), calls=%async_computation.2 | async-start | bytes 2752512 | tf_op jit(solution)/shard_map/all_to_all | solution.py:601
  82.6 5.8 %collective-permute-start.8 = (bf16[16,2688]{1,0:T(8,128)(2,1)S(1)}, bf16[16,2688]{1,0:T(8,128)(2,1)S(1)}, u32[]{:S(2)}, u32[]{:S(2)}) collective-permute-start(bf16[16,2688]{1,0:T(8,128)(2,1)S(1)} %shard_map.126), channel_id=1, source_target_pairs={{64,32},{80,48},{96,0},{112,16},{65,33},{81,49},{97,1},{113,17},{6... | collective-permute-start | bytes 258056 | tf_op jit(solution)/shard_map/ppermute | solution.py:598
  88.5 7.3 %collective-permute-done.8.first_ref = bf16[16,2688]{1,0:T(8,128)(2,1)S(1)} collective-permute-done((bf16[16,2688]{1,0:T(8,128)(2,1)S(1)}, bf16[16,2688]{1,0:T(8,128)(2,1)S(1)}, u32[]{:S(2)}, u32[]{:S(2)}) %collective-permute-start.8) | collective-permute-done | bytes 86048 | tf_op jit(solution)/shard_map/ppermute | solution.py:598
  95.8 6.4 %collective-permute-start.11 = (bf16[512,512]{1,0:T(8,128)(2,1)S(1)}, bf16[512,512]{1,0:T(8,128)(2,1)}, u32[]{:S(2)}, u32[]{:S(2)}) collective-permute-start(bf16[512,512]{1,0:T(8,128)(2,1)S(1)} %bitcast.50), channel_id=1, source_target_pairs={{64,32},{80,48},{96,0},{112,16},{65,33},{81,49},{97,1},{113,17},{6... | collective-permute-start | bytes 1572872 | tf_op jit(solution)/shard_map/ppermute | solution.py:598
  103.3 7.0 %all-to-all-start.3 = ((bf16[16,16,2048]{2,1,0:T(8,128)(2,1)}), bf16[16,16,2048]{2,1,0:T(8,128)(2,1)}, u32[]{:S(2)}, u32[]{:S(2)}) async-start(bf16[16,16,2048]{2,1,0:T(8,128)(2,1)} %shard_map.128), calls=%async_computation.3 | async-start | bytes 2097152 | tf_op jit(solution)/shard_map/all_to_all | solution.py:601
  111.2 5.0 %shard_map.129 = bf16[256,512]{1,0:T(8,128)(2,1)S(1)} custom-call(s32[2,3]{1,0:T(2,128)S(1)} %copy-done.2, bf16[256,2688]{1,0:T(8,128)(2,1)S(1)} %bitcast.19, bf16[2048,512]{1,0:T(8,128)(2,1)} %bitcast.35, bf16[640,512]{1,0:T(8,128)(2,1)} %collective-permute-done.5.refs_0_.refs_1_, bf16[640,512]{1,0:T(8,128)(2,1)} %collective-permute-done.7.refs_1_.refs_2_, ...), custom_call_target="tpu_custom_call" | custom-call | flops 805306368 | bytes 4194304 | tf_op jit(solution)/shard_map/pallas_call | solution.py:752
  119.7 3.8 %collective-permute-done.13.across_ref = bf16[128,512]{1,0:T(8,128)(2,1)S(1)} collective-permute-done((bf16[128,512]{1,0:T(8,128)(2,1)S(1)}, bf16[128,512]{1,0:T(8,128)(2,1)S(1)}, u32[]{:S(2)}, u32[]{:S(2)}) %collective-permute-start.13) | collective-permute-done | bytes 131104 | tf_op jit(solution)/shard_map/ppermute | solution.py:679
  126.5 28.2 %all_to_all.45.parts_ref = bf16[16,16,2688]{2,1,0:T(8,128)(2,1)S(1)} all-to-all(bf16[16,16,2688]{2,1,0:T(8,128)(2,1)} %shard_map.131), channel_id=1, replica_groups=mesh['section'=2,'mp'=4,'dp'=16] {'dp'}, dimensions={0} | all-to-all | bytes 2752512 | tf_op jit(solution)/shard_map/all_to_all | solution.py:601
  156.4 3.7 %all-to-all-start.5 = ((bf16[16,16,2688]{2,1,0:T(8,128)(2,1)}), bf16[16,16,2688]{2,1,0:T(8,128)(2,1)S(1)}, u32[]{:S(2)}, u32[]{:S(2)}) async-start(bf16[16,16,2688]{2,1,0:T(8,128)(2,1)} %shard_map.132), calls=%async_computation.5 | async-start | bytes 2752512 | tf_op jit(solution)/shard_map/all_to_all | solution.py:601
  161.4 19.6 %all-to-all-done.5 = bf16[16,16,2688]{2,1,0:T(8,128)(2,1)S(1)} async-done(((bf16[16,16,2688]{2,1,0:T(8,128)(2,1)}), bf16[16,16,2688]{2,1,0:T(8,128)(2,1)S(1)}, u32[]{:S(2)}, u32[]{:S(2)}) %all-to-all-start.5) | async-done | bytes 1376288 | tf_op jit(solution)/shard_map/all_to_all | solution.py:601
  181.1 9.1 %shard_map.133 = bf16[256,512]{1,0:T(8,128)(2,1)S(1)} custom-call(s32[2,3]{1,0:T(2,128)S(1)} %copy-done.2, bf16[256,2688]{1,0:T(8,128)(2,1)S(1)} %bitcast.21, bf16[256,2048]{1,0:T(8,128)(2,1)} %bitcast.7.grads_ref, bf16[512,2048]{1,0:T(8,128)(2,1)} %collective-permute-done.9.refs_0_.wq0_ref, bf16[512,2048]{1,0:T(8,128)(2,1)} %bitcast.42, ...), custom_call_target="tpu_custom_call" | custom-call | flops 1610612736 | bytes 6291456 | tf_op jit(solution)/shard_map/pallas_call | solution.py:798
  193.7 3.7 %collective-permute-done.16.across_ref = bf16[128,512]{1,0:T(8,128)(2,1)S(1)} collective-permute-done((bf16[128,512]{1,0:T(8,128)(2,1)S(1)}, bf16[128,512]{1,0:T(8,128)(2,1)S(1)}, u32[]{:S(2)}, u32[]{:S(2)}) %collective-permute-start.16) | collective-permute-done | bytes 131104 | tf_op jit(solution)/shard_map/ppermute | solution.py:679
  200.4 3.7 %all-to-all-start.6 = ((bf16[16,16,2048]{2,1,0:T(8,128)(2,1)}), bf16[16,16,2048]{2,1,0:T(8,128)(2,1)S(1)}, u32[]{:S(2)}, u32[]{:S(2)}) async-start(bf16[16,16,2048]{2,1,0:T(8,128)(2,1)} %get-tuple-element.94), calls=%async_computation.6 | async-start | bytes 2097152 | tf_op jit(solution)/shard_map/all_to_all | solution.py:601
  205.3 16.0 %collective-permute-done.19.wkv1_ref = bf16[512,512]{1,0:T(8,128)(2,1)S(1)} collective-permute-done((bf16[512,512]{1,0:T(8,128)(2,1)}, bf16[512,512]{1,0:T(8,128)(2,1)S(1)}, u32[]{:S(2)}, u32[]{:S(2)}) %collective-permute-start.19) | collective-permute-done | bytes 524320 | tf_op jit(solution)/shard_map/ppermute | solution.py:598
  223.9 23.0 %all_to_all.46 = bf16[16,16,2048]{2,1,0:T(8,128)(2,1)S(1)} all-to-all(bf16[16,16,2048]{2,1,0:T(8,128)(2,1)} %shard_map.136), channel_id=1, replica_groups=mesh['section'=2,'mp'=4,'dp'=16] {'dp'}, dimensions={0} | all-to-all | bytes 2097152 | tf_op jit(solution)/shard_map/all_to_all | solution.py:601
  246.9 8.3 %shard_map.137 = bf16[256,512]{1,0:T(8,128)(2,1)S(1)} custom-call(s32[2,3]{1,0:T(2,128)S(1)} %copy-done.2, bf16[256,2688]{1,0:T(8,128)(2,1)S(1)} %bitcast.20, bf16[256,2048]{1,0:T(8,128)(2,1)S(1)} %bitcast.22, bf16[512,2048]{1,0:T(8,128)(2,1)} %bitcast.43, bf16[512,2048]{1,0:T(8,128)(2,1)} %collective-permute-done.18.wq1_ref, bf16[512,512]{1,0:T(8,128)(2,1)} %bitcast.49, ...), custom_call_target="tpu_custom_call" | custom-call | flops 1610612736 | bytes 6291456 | tf_op jit(solution)/shard_map/pallas_call | solution.py:798
  257.0 5.5 %collective-permute-done.21.across_ref = bf16[128,512]{1,0:T(8,128)(2,1)S(1)} collective-permute-done((bf16[128,512]{1,0:T(8,128)(2,1)S(1)}, bf16[128,512]{1,0:T(8,128)(2,1)S(1)}, u32[]{:S(2)}, u32[]{:S(2)}) %collective-permute-start.21) | collective-permute-done | bytes 131104 | tf_op jit(solution)/shard_map/ppermute | solution.py:679
  263.9 3.1 %shard_map.138 = (bf16[16,2,16,1280]{3,2,1,0:T(8,128)(2,1)S(1)}, bf16[64,512]{1,0:T(8,128)(2,1)}) custom-call(s32[1,32]{1,0:T(1,128)S(1)} %copy-done.3, s32[1,32]{1,0:T(1,128)S(1)} %copy-done.4, bf16[256,512]{1,0:T(8,128)(2,1)S(1)} %get-tuple-element.93.last_ref, bf16[256,512]{1,0:T(8,128)(2,1)S(1)} %add_convert_fusion.pair_ref, ...), custom_call_target="tpu_custom_call" | custom-call | tf_op jit(solution)/shard_map/pallas_call | solution.py:843
  266.9 23.2 %all_to_all.47.parts_ref = bf16[16,2,16,1280]{3,2,1,0:T(8,128)(2,1)S(1)} all-to-all(bf16[16,2,16,1280]{3,2,1,0:T(8,128)(2,1)S(1)} %get-tuple-element.103), channel_id=1, replica_groups=mesh['section'=2,'mp'=4,'dp'=16] {'dp'}, dimensions={0} | all-to-all | bytes 2621440 | tf_op jit(solution)/shard_map/all_to_all | solution.py:601
  290.3 5.5 %collective-permute-done.23 = bf16[16,1280]{1,0:T(8,128)(2,1)S(1)} collective-permute-done((bf16[16,1280]{1,0:T(8,128)(2,1)S(1)}, bf16[16,1280]{1,0:T(8,128)(2,1)S(1)}, u32[]{:S(2)}, u32[]{:S(2)}) %collective-permute-start.23) | collective-permute-done | bytes 40992 | tf_op jit(solution)/shard_map/ppermute | solution.py:869
  (81 shorter events, 41.5 us)
Async XLA Ops:
  1.5 8.7 %collective-permute-start = (bf16[64,512]{1,0:T(8,128)(2,1)S(1)}, bf16[64,512]{1,0:T(8,128)(2,1)S(1)}, u32[]{:S(2)}, u32[]{:S(2)}) collective-permute-start(bf16[64,512]{1,0:T(8,128)(2,1)S(1)} %get-tuple-element.109.mine_ref), channel_id=1, source_target_pairs={{0,16},{16,0},{32,48},{48,32},{1,17},{17,1},{33,49},{49,33},{2,18}... | collective-permute-start | bytes 196616 | tf_op jit(solution)/shard_map/ppermute | solution.py:679
  1.6 8.6 %collective-permute-start.1 = (bf16[64,512]{1,0:T(8,128)(2,1)S(1)}, bf16[64,512]{1,0:T(8,128)(2,1)S(1)}, u32[]{:S(2)}, u32[]{:S(2)}) collective-permute-start(bf16[64,512]{1,0:T(8,128)(2,1)S(1)} %get-tuple-element.109.mine_ref), channel_id=1, source_target_pairs={{0,32},{16,48},{32,0},{48,16},{1,33},{17,49},{33,1},{49,17},{2,34}... | collective-permute-start | bytes 196616 | tf_op jit(solution)/shard_map/ppermute | solution.py:679
  2.5 7.7 %collective-permute-start.2 = (bf16[64,512]{1,0:T(8,128)(2,1)S(1)}, bf16[64,512]{1,0:T(8,128)(2,1)S(1)}, u32[]{:S(2)}, u32[]{:S(2)}) collective-permute-start(bf16[64,512]{1,0:T(8,128)(2,1)S(1)} %get-tuple-element.109.mine_ref), channel_id=1, source_target_pairs={{0,48},{16,32},{32,16},{48,0},{1,49},{17,33},{33,17},{49,1},{2,50}... | collective-permute-start | bytes 196616 | tf_op jit(solution)/shard_map/ppermute | solution.py:679
  3.5 8.4 %collective-permute-start.4 = (f32[1,512]{1,0:T(1,128)}, f32[1,512]{1,0:T(1,128)S(1)}, u32[]{:S(2)}, u32[]{:S(2)}) collective-permute-start(f32[1,512]{1,0:T(1,128)} %bitcast.25), channel_id=1, source_target_pairs={{0,96},{16,112},{32,64},{48,80},{64,32},{80,48},{96,0},{112,16},{1... | collective-permute-start | bytes 6152 | tf_op jit(solution)/shard_map/ppermute | solution.py:598
  3.9 8.0 %collective-permute-start.3 = (bf16[64,512]{1,0:T(8,128)(2,1)S(1)}, bf16[64,512]{1,0:T(8,128)(2,1)S(1)}, u32[]{:S(2)}, u32[]{:S(2)}) collective-permute-start(bf16[64,512]{1,0:T(8,128)(2,1)S(1)} %bitcast.52), channel_id=1, source_target_pairs={{0,96},{16,112},{32,64},{48,80},{64,32},{80,48},{96,0},{112,16},{1... | collective-permute-start | bytes 196616 | tf_op jit(solution)/shard_map/ppermute | solution.py:598
  11.9 29.7 %all-to-all-start = ((bf16[16,16,2688]{2,1,0:T(8,128)(2,1)}), bf16[16,16,2688]{2,1,0:T(8,128)(2,1)S(1)}, u32[]{:S(2)}, u32[]{:S(2)}) async-start(bf16[16,16,2688]{2,1,0:T(8,128)(2,1)} %get-tuple-element.55), calls=%async_computation | async-start | bytes 2752512 | tf_op jit(solution)/shard_map/all_to_all | solution.py:601
  22.2 19.3 %collective-permute-start.5 = (bf16[640,512]{1,0:T(8,128)(2,1)S(1)}, bf16[640,512]{1,0:T(8,128)(2,1)}, u32[]{:S(2)}, u32[]{:S(2)}) collective-permute-start(bf16[640,512]{1,0:T(8,128)(2,1)S(1)} %get-tuple-element.107), channel_id=1, source_target_pairs={{0,96},{16,112},{32,64},{48,80},{1,97},{17,113},{33,65},{49,81},{2... | collective-permute-start | bytes 1966088 | tf_op jit(solution)/shard_map/ppermute | solution.py:598
  41.6 26.6 %all-to-all-start.1 = ((bf16[16,16,2688]{2,1,0:T(8,128)(2,1)}), bf16[16,16,2688]{2,1,0:T(8,128)(2,1)S(1)}, u32[]{:S(2)}, u32[]{:S(2)}) async-start(bf16[16,16,2688]{2,1,0:T(8,128)(2,1)} %shard_map.124), calls=%async_computation.1 | async-start | bytes 2752512 | tf_op jit(solution)/shard_map/all_to_all | solution.py:601
  48.5 54.8 %collective-permute-start.9 = (bf16[512,2048]{1,0:T(8,128)(2,1)}, bf16[512,2048]{1,0:T(8,128)(2,1)}, u32[]{:S(2)}, u32[]{:S(2)}) collective-permute-start(bf16[512,2048]{1,0:T(8,128)(2,1)} %bitcast.39), channel_id=1, source_target_pairs={{64,32},{80,48},{96,0},{112,16},{65,33},{81,49},{97,1},{113,17},{6... | collective-permute-start | bytes 6291464 | tf_op jit(solution)/shard_map/ppermute | solution.py:598
  51.1 26.3 %collective-permute-start.7 = (bf16[640,512]{1,0:T(8,128)(2,1)}, bf16[640,512]{1,0:T(8,128)(2,1)}, u32[]{:S(2)}, u32[]{:S(2)}) collective-permute-start(bf16[640,512]{1,0:T(8,128)(2,1)} %get-tuple-element.64), channel_id=1, source_target_pairs={{0,96},{16,112},{32,64},{48,80},{1,97},{17,113},{33,65},{49,81},{2... | collective-permute-start | bytes 1966088 | tf_op jit(solution)/shard_map/ppermute | solution.py:598
  68.6 7.6 %collective-permute-start.6 = (bf16[16,2688]{1,0:T(8,128)(2,1)S(1)}, bf16[16,2688]{1,0:T(8,128)(2,1)S(1)}, u32[]{:S(2)}, u32[]{:S(2)}) collective-permute-start(bf16[16,2688]{1,0:T(8,128)(2,1)S(1)} %shard_map.126), channel_id=1, source_target_pairs={{0,96},{16,112},{32,64},{48,80},{1,97},{17,113},{33,65},{49,81},{2... | collective-permute-start | bytes 258056 | tf_op jit(solution)/shard_map/ppermute | solution.py:598
  77.5 18.3 %copy-start.5 = (bf16[64,8,2,256]{3,1,2,0:T(8,128)(2,1)S(1)}, bf16[64,8,2,256]{3,1,2,0:T(8,128)(2,1)}, u32[]{:S(2)}) copy-start(bf16[64,8,2,256]{3,1,2,0:T(8,128)(2,1)} %copy.13) | copy-start | bytes 1572868
  77.5 25.8 %all-to-all-start.2 = ((bf16[16,16,2688]{2,1,0:T(8,128)(2,1)}), bf16[16,16,2688]{2,1,0:T(8,128)(2,1)S(1)}, u32[]{:S(2)}, u32[]{:S(2)}) async-start(bf16[16,16,2688]{2,1,0:T(8,128)(2,1)} %shard_map.127), calls=%async_computation.2 | async-start | bytes 2752512 | tf_op jit(solution)/shard_map/all_to_all | solution.py:601
  81.3 29.8 %copy-start.2 = (s32[2,3]{1,0:T(2,128)S(1)}, s32[2,3]{1,0:T(2,128)}, u32[]{:S(2)}) copy-start(s32[2,3]{1,0:T(2,128)} %seq_ref.5) | copy-start | bytes 76
  81.3 28.9 %collective-permute-start.10 = (bf16[768,512]{1,0:T(8,128)(2,1)}, bf16[768,512]{1,0:T(8,128)(2,1)S(1)}, u32[]{:S(2)}, u32[]{:S(2)}) collective-permute-start(bf16[768,512]{1,0:T(8,128)(2,1)} %slice.11), channel_id=1, source_target_pairs={{0,96},{16,112},{32,64},{48,80},{1,97},{17,113},{33,65},{49,81},{2... | collective-permute-start | bytes 2359304 | tf_op jit(solution)/shard_map/ppermute | solution.py:598
  82.6 13.1 %collective-permute-start.8 = (bf16[16,2688]{1,0:T(8,128)(2,1)S(1)}, bf16[16,2688]{1,0:T(8,128)(2,1)S(1)}, u32[]{:S(2)}, u32[]{:S(2)}) collective-permute-start(bf16[16,2688]{1,0:T(8,128)(2,1)S(1)} %shard_map.126), channel_id=1, source_target_pairs={{64,32},{80,48},{96,0},{112,16},{65,33},{81,49},{97,1},{113,17},{6... | collective-permute-start | bytes 258056 | tf_op jit(solution)/shard_map/ppermute | solution.py:598
  95.8 20.4 %collective-permute-start.11 = (bf16[512,512]{1,0:T(8,128)(2,1)S(1)}, bf16[512,512]{1,0:T(8,128)(2,1)}, u32[]{:S(2)}, u32[]{:S(2)}) collective-permute-start(bf16[512,512]{1,0:T(8,128)(2,1)S(1)} %bitcast.50), channel_id=1, source_target_pairs={{64,32},{80,48},{96,0},{112,16},{65,33},{81,49},{97,1},{113,17},{6... | collective-permute-start | bytes 1572872 | tf_op jit(solution)/shard_map/ppermute | solution.py:598
  103.3 23.2 %all-to-all-start.3 = ((bf16[16,16,2048]{2,1,0:T(8,128)(2,1)}), bf16[16,16,2048]{2,1,0:T(8,128)(2,1)}, u32[]{:S(2)}, u32[]{:S(2)}) async-start(bf16[16,16,2048]{2,1,0:T(8,128)(2,1)} %shard_map.128), calls=%async_computation.3 | async-start | bytes 2097152 | tf_op jit(solution)/shard_map/all_to_all | solution.py:601
  116.2 1.6 collective-permute-start.12
  117.8 5.6 %collective-permute-start.13 = (bf16[128,512]{1,0:T(8,128)(2,1)S(1)}, bf16[128,512]{1,0:T(8,128)(2,1)S(1)}, u32[]{:S(2)}, u32[]{:S(2)}) collective-permute-start(bf16[128,512]{1,0:T(8,128)(2,1)S(1)} %add_convert_fusion.5), channel_id=1, source_target_pairs={{0,32},{16,48},{32,0},{48,16},{1,33},{17,49},{33,1},{49,17},{2,34}... | collective-permute-start | bytes 393224 | tf_op jit(solution)/shard_map/ppermute | solution.py:679
  123.4 1.3 collective-permute-start.14
  156.4 24.7 %all-to-all-start.5 = ((bf16[16,16,2688]{2,1,0:T(8,128)(2,1)}), bf16[16,16,2688]{2,1,0:T(8,128)(2,1)S(1)}, u32[]{:S(2)}, u32[]{:S(2)}) async-start(bf16[16,16,2688]{2,1,0:T(8,128)(2,1)} %shard_map.132), calls=%async_computation.5 | async-start | bytes 2752512 | tf_op jit(solution)/shard_map/all_to_all | solution.py:601
  160.1 62.0 %collective-permute-start.18 = (bf16[512,2048]{1,0:T(8,128)(2,1)}, bf16[512,2048]{1,0:T(8,128)(2,1)}, u32[]{:S(2)}, u32[]{:S(2)}) collective-permute-start(bf16[512,2048]{1,0:T(8,128)(2,1)} %bitcast.41), channel_id=1, source_target_pairs={{0,96},{16,112},{32,64},{48,80},{1,97},{17,113},{33,65},{49,81},{2... | collective-permute-start | bytes 6291464 | tf_op jit(solution)/shard_map/ppermute | solution.py:598
  190.2 1.6 collective-permute-start.15
  191.8 5.6 %collective-permute-start.16 = (bf16[128,512]{1,0:T(8,128)(2,1)S(1)}, bf16[128,512]{1,0:T(8,128)(2,1)S(1)}, u32[]{:S(2)}, u32[]{:S(2)}) collective-permute-start(bf16[128,512]{1,0:T(8,128)(2,1)S(1)} %add_convert_fusion.4), channel_id=1, source_target_pairs={{0,32},{16,48},{32,0},{48,16},{1,33},{17,49},{33,1},{49,17},{2,34}... | collective-permute-start | bytes 393224 | tf_op jit(solution)/shard_map/ppermute | solution.py:679
  197.4 1.3 collective-permute-start.17
  200.4 22.1 %all-to-all-start.6 = ((bf16[16,16,2048]{2,1,0:T(8,128)(2,1)}), bf16[16,16,2048]{2,1,0:T(8,128)(2,1)S(1)}, u32[]{:S(2)}, u32[]{:S(2)}) async-start(bf16[16,16,2048]{2,1,0:T(8,128)(2,1)} %get-tuple-element.94), calls=%async_computation.6 | async-start | bytes 2097152 | tf_op jit(solution)/shard_map/all_to_all | solution.py:601
  204.0 17.3 %collective-permute-start.19 = (bf16[512,512]{1,0:T(8,128)(2,1)}, bf16[512,512]{1,0:T(8,128)(2,1)S(1)}, u32[]{:S(2)}, u32[]{:S(2)}) collective-permute-start(bf16[512,512]{1,0:T(8,128)(2,1)} %bitcast.48), channel_id=1, source_target_pairs={{0,96},{16,112},{32,64},{48,80},{1,97},{17,113},{33,65},{49,81},{2... | collective-permute-start | bytes 1572872 | tf_op jit(solution)/shard_map/ppermute | solution.py:598
  255.2 1.6 collective-permute-start.20
  256.9 5.6 %collective-permute-start.21 = (bf16[128,512]{1,0:T(8,128)(2,1)S(1)}, bf16[128,512]{1,0:T(8,128)(2,1)S(1)}, u32[]{:S(2)}, u32[]{:S(2)}) collective-permute-start(bf16[128,512]{1,0:T(8,128)(2,1)S(1)} %add_convert_fusion.3), channel_id=1, source_target_pairs={{0,32},{16,48},{32,0},{48,16},{1,33},{17,49},{33,1},{49,17},{2,34}... | collective-permute-start | bytes 393224 | tf_op jit(solution)/shard_map/ppermute | solution.py:679
  262.5 1.3 collective-permute-start.22
  290.2 5.6 %collective-permute-start.23 = (bf16[16,1280]{1,0:T(8,128)(2,1)S(1)}, bf16[16,1280]{1,0:T(8,128)(2,1)S(1)}, u32[]{:S(2)}, u32[]{:S(2)}) collective-permute-start(bf16[16,1280]{1,0:T(8,128)(2,1)S(1)} %get-tuple-element.105), channel_id=1, source_target_pairs={{0,64},{64,0},{1,65},{65,1},{2,66},{66,2},{3,67},{67,3},{4,68},{68... | collective-permute-start | bytes 122888 | tf_op jit(solution)/shard_map/ppermute | solution.py:869
  (7 other events, 60.0 us)

commit v5 on v4

--- a/solution.py
+++ b/solution.py
@@ -513,7 +513,7 @@
             places[owner * CAP + slot] = -1
         return carry
 
-    lax.fori_loop(0, owner_count, clear, 0)
+    lax.fori_loop(0, owner_count, clear, 0, unroll=8)
 
     def place(block, carry):
         owner = owners_ref[0, block]
@@ -526,7 +526,7 @@
 
         return carry
 
-    lax.fori_loop(0, marks_ref.shape[1], place, 0)
+    lax.fori_loop(0, marks_ref.shape[1], place, 0, unroll=4)
 
     def send(owner, carry):
         pieces = []
@@ -539,7 +539,7 @@
         ).astype(BF)
         return carry
 
-    lax.fori_loop(0, owner_count, send, 0)
+    lax.fori_loop(0, owner_count, send, 0, unroll=4)
 
 
 def merger_sum_kernel(parts_ref, own_ref, other_ref):

time: 298 us -> 297 us (level)
  no operation moved by 1% of the time
where the time goes in v5:
time: 297 us; the launch traced here: 296 us
  waiting for transfers between devices  92.9 us (31%)
  blocking collectives  85.9 us (29%)
  starting transfers between devices  61.8 us (21%)
  Pallas kernels  44.3 us (15%)
  local copies, waits for them, and re-layouts  7.96 us (3%)
    all_to_all x3, blocking collectives, scatter(): return lax.all_to_all(array, axis, split_axis=0, concat_axis=0, tiled=True)  74.3 us
    ppermute x11, waiting for transfers between devices, swap(): return lax.ppermute(array, ('section', 'mp'), pairs)  36.5 us
    all_to_all x6, starting transfers between devices, scatter(): return lax.all_to_all(array, axis, split_axis=0, concat_axis=0, tiled=True)  33.1 us
    all_to_all x6, waiting for transfers between devices, scatter(): return lax.all_to_all(array, axis, split_axis=0, concat_axis=0, tiled=True)  29.6 us
    ppermute x11, starting transfers between devices, swap(): return lax.ppermute(array, ('section', 'mp'), pairs)  25.9 us
    ppermute x12, waiting for transfers between devices, beside(): lax.ppermute(array, 'mp', [(i, i ^ distance) for i in range(mp_count)])  21.4 us
    pallas_call x2, Pallas kernels, layer_backward(): pl.pallas_call(backward_kernel, out_shape=shape_of((tokens, width), BF),...  17.4 us
    all_gather x2, blocking collectives, gather(): return lax.all_gather(array, axis, axis=0, tiled=True)  11.6 us
  transfers between devices with their start and end apart: 30, of which 18 were waited for; matrix products, arithmetic and copies ran while one was open for 2% of the time, Pallas kernels for 10%

profile of v5, /device:TPU:6, one launch (start us, length us, event | category | flops | bytes accessed | tf_op | source)
XLA Modules:
  0.0 296.0 jit_solution(9382282409859039171)
XLA Ops:
  3.9 2.8 collective-permute-start.3
  11.9 8.1 %all-to-all-start = ((bf16[16,16,2688]{2,1,0:T(8,128)(2,1)}), bf16[16,16,2688]{2,1,0:T(8,128)(2,1)S(1)}, u32[]{:S(2)}, u32[]{:S(2)}) async-start(bf16[16,16,2688]{2,1,0:T(8,128)(2,1)} %get-tuple-element.55), calls=%async_computation | async-start | bytes 2752512 | tf_op jit(solution)/shard_map/all_to_all | solution.py:601
  20.0 2.2 fusion.9
  23.5 2.1 slice.11
  25.5 5.8 %all_gather.6.x_ref = bf16[256,512]{1,0:T(8,128)(2,1)S(1)} all-gather(bf16[64,512]{1,0:T(8,128)(2,1)S(1)} %collective-permute-done.3), channel_id=1, replica_groups=mesh['section'=2,'mp'=4,'dp'=16] {'mp'}, dimensions={0}, use_global_device_ids=true | all-gather | bytes 327680 | tf_op jit(solution)/shard_map/all_gather | solution.py:607
  31.3 3.3 %shard_map.124 = bf16[16,16,2688]{2,1,0:T(8,128)(2,1)} custom-call(bf16[256,512]{1,0:T(8,128)(2,1)S(1)} %all_gather.6.x_ref, f32[1,512]{1,0:T(1,128)S(1)} %bitcast.27, bf16[512,2048]{1,0:T(8,128)(2,1)} %bitcast.38, bf16[512,512]{1,0:T(8,128)(2,1)} %bitcast.45, bf16[2048,512]{1,0:T(8,128)(2,1)} %bitcast.34), custom_call_target="tpu_custom_call" | custom-call | flops 704643072 | bytes 6291456 | tf_op jit(solution)/shard_map/pallas_call | solution.py:622
  34.6 6.9 %collective-permute-done.5.refs_0_.refs_1_ = bf16[640,512]{1,0:T(8,128)(2,1)} collective-permute-done((bf16[640,512]{1,0:T(8,128)(2,1)S(1)}, bf16[640,512]{1,0:T(8,128)(2,1)}, u32[]{:S(2)}, u32[]{:S(2)}) %collective-permute-start.5) | collective-permute-done | bytes 655392 | tf_op jit(solution)/shard_map/ppermute | solution.py:598
  41.6 6.9 %all-to-all-start.1 = ((bf16[16,16,2688]{2,1,0:T(8,128)(2,1)}), bf16[16,16,2688]{2,1,0:T(8,128)(2,1)S(1)}, u32[]{:S(2)}, u32[]{:S(2)}) async-start(bf16[16,16,2688]{2,1,0:T(8,128)(2,1)} %shard_map.124), calls=%async_computation.1 | async-start | bytes 2752512 | tf_op jit(solution)/shard_map/all_to_all | solution.py:601
  48.5 2.7 collective-permute-start.9
  52.4 5.8 %all-gather = bf16[1,256,512]{2,1,0:T(8,128)(2,1)S(1)} all-gather(bf16[1,64,512]{2,1,0:T(8,128)(2,1)S(1)} %get-tuple-element.108), channel_id=2, replica_groups=mesh['section'=2,'mp'=4,'dp'=16] {'mp'}, dimensions={1}, use_global_device_ids=true | all-gather | bytes 327680 | tf_op jit(solution)/shard_map/all_gather | solution.py:607
  58.6 9.6 %all-to-all-done.1.parts_ref = bf16[16,16,2688]{2,1,0:T(8,128)(2,1)S(1)} async-done(((bf16[16,16,2688]{2,1,0:T(8,128)(2,1)}), bf16[16,16,2688]{2,1,0:T(8,128)(2,1)S(1)}, u32[]{:S(2)}, u32[]{:S(2)}) %all-to-all-start.1) | async-done | bytes 1376288 | tf_op jit(solution)/shard_map/all_to_all | solution.py:601
  69.9 6.3 %collective-permute-done.6.second_ref = bf16[16,2688]{1,0:T(8,128)(2,1)S(1)} collective-permute-done((bf16[16,2688]{1,0:T(8,128)(2,1)S(1)}, bf16[16,2688]{1,0:T(8,128)(2,1)S(1)}, u32[]{:S(2)}, u32[]{:S(2)}) %collective-permute-start.6) | collective-permute-done | bytes 86048 | tf_op jit(solution)/shard_map/ppermute | solution.py:598
  77.5 3.8 %all-to-all-start.2 = ((bf16[16,16,2688]{2,1,0:T(8,128)(2,1)}), bf16[16,16,2688]{2,1,0:T(8,128)(2,1)S(1)}, u32[]{:S(2)}, u32[]{:S(2)}) async-start(bf16[16,16,2688]{2,1,0:T(8,128)(2,1)} %shard_map.127), calls=%async_computation.2 | async-start | bytes 2752512 | tf_op jit(solution)/shard_map/all_to_all | solution.py:601
  82.6 5.8 %collective-permute-start.8 = (bf16[16,2688]{1,0:T(8,128)(2,1)S(1)}, bf16[16,2688]{1,0:T(8,128)(2,1)S(1)}, u32[]{:S(2)}, u32[]{:S(2)}) collective-permute-start(bf16[16,2688]{1,0:T(8,128)(2,1)S(1)} %shard_map.126), channel_id=1, source_target_pairs={{64,32},{80,48},{96,0},{112,16},{65,33},{81,49},{97,1},{113,17},{6... | collective-permute-start | bytes 258056 | tf_op jit(solution)/shard_map/ppermute | solution.py:598
  88.5 7.3 %collective-permute-done.8.first_ref = bf16[16,2688]{1,0:T(8,128)(2,1)S(1)} collective-permute-done((bf16[16,2688]{1,0:T(8,128)(2,1)S(1)}, bf16[16,2688]{1,0:T(8,128)(2,1)S(1)}, u32[]{:S(2)}, u32[]{:S(2)}) %collective-permute-start.8) | collective-permute-done | bytes 86048 | tf_op jit(solution)/shard_map/ppermute | solution.py:598
  95.8 6.4 %collective-permute-start.11 = (bf16[512,512]{1,0:T(8,128)(2,1)S(1)}, bf16[512,512]{1,0:T(8,128)(2,1)}, u32[]{:S(2)}, u32[]{:S(2)}) collective-permute-start(bf16[512,512]{1,0:T(8,128)(2,1)S(1)} %bitcast.50), channel_id=1, source_target_pairs={{64,32},{80,48},{96,0},{112,16},{65,33},{81,49},{97,1},{113,17},{6... | collective-permute-start | bytes 1572872 | tf_op jit(solution)/shard_map/ppermute | solution.py:598
  103.3 7.0 %all-to-all-start.3 = ((bf16[16,16,2048]{2,1,0:T(8,128)(2,1)}), bf16[16,16,2048]{2,1,0:T(8,128)(2,1)}, u32[]{:S(2)}, u32[]{:S(2)}) async-start(bf16[16,16,2048]{2,1,0:T(8,128)(2,1)} %shard_map.128), calls=%async_computation.3 | async-start | bytes 2097152 | tf_op jit(solution)/shard_map/all_to_all | solution.py:601
  111.2 5.0 %shard_map.129 = bf16[256,512]{1,0:T(8,128)(2,1)S(1)} custom-call(s32[2,3]{1,0:T(2,128)S(1)} %copy-done.2, bf16[256,2688]{1,0:T(8,128)(2,1)S(1)} %bitcast.19, bf16[2048,512]{1,0:T(8,128)(2,1)} %bitcast.35, bf16[640,512]{1,0:T(8,128)(2,1)} %collective-permute-done.5.refs_0_.refs_1_, bf16[640,512]{1,0:T(8,128)(2,1)} %collective-permute-done.7.refs_1_.refs_2_, ...), custom_call_target="tpu_custom_call" | custom-call | flops 805306368 | bytes 4194304 | tf_op jit(solution)/shard_map/pallas_call | solution.py:752
  119.7 3.8 %collective-permute-done.13.across_ref = bf16[128,512]{1,0:T(8,128)(2,1)S(1)} collective-permute-done((bf16[128,512]{1,0:T(8,128)(2,1)S(1)}, bf16[128,512]{1,0:T(8,128)(2,1)S(1)}, u32[]{:S(2)}, u32[]{:S(2)}) %collective-permute-start.13) | collective-permute-done | bytes 131104 | tf_op jit(solution)/shard_map/ppermute | solution.py:679
  126.5 28.2 %all_to_all.45.parts_ref = bf16[16,16,2688]{2,1,0:T(8,128)(2,1)S(1)} all-to-all(bf16[16,16,2688]{2,1,0:T(8,128)(2,1)} %shard_map.131), channel_id=1, replica_groups=mesh['section'=2,'mp'=4,'dp'=16] {'dp'}, dimensions={0} | all-to-all | bytes 2752512 | tf_op jit(solution)/shard_map/all_to_all | solution.py:601
  156.4 3.7 %all-to-all-start.5 = ((bf16[16,16,2688]{2,1,0:T(8,128)(2,1)}), bf16[16,16,2688]{2,1,0:T(8,128)(2,1)S(1)}, u32[]{:S(2)}, u32[]{:S(2)}) async-start(bf16[16,16,2688]{2,1,0:T(8,128)(2,1)} %shard_map.132), calls=%async_computation.5 | async-start | bytes 2752512 | tf_op jit(solution)/shard_map/all_to_all | solution.py:601
  161.4 19.6 %all-to-all-done.5 = bf16[16,16,2688]{2,1,0:T(8,128)(2,1)S(1)} async-done(((bf16[16,16,2688]{2,1,0:T(8,128)(2,1)}), bf16[16,16,2688]{2,1,0:T(8,128)(2,1)S(1)}, u32[]{:S(2)}, u32[]{:S(2)}) %all-to-all-start.5) | async-done | bytes 1376288 | tf_op jit(solution)/shard_map/all_to_all | solution.py:601
  181.1 9.1 %shard_map.133 = bf16[256,512]{1,0:T(8,128)(2,1)S(1)} custom-call(s32[2,3]{1,0:T(2,128)S(1)} %copy-done.2, bf16[256,2688]{1,0:T(8,128)(2,1)S(1)} %bitcast.21, bf16[256,2048]{1,0:T(8,128)(2,1)} %bitcast.7.grads_ref, bf16[512,2048]{1,0:T(8,128)(2,1)} %collective-permute-done.9.refs_0_.wq0_ref, bf16[512,2048]{1,0:T(8,128)(2,1)} %bitcast.42, ...), custom_call_target="tpu_custom_call" | custom-call | flops 1610612736 | bytes 6291456 | tf_op jit(solution)/shard_map/pallas_call | solution.py:798
  193.7 3.7 %collective-permute-done.16.across_ref = bf16[128,512]{1,0:T(8,128)(2,1)S(1)} collective-permute-done((bf16[128,512]{1,0:T(8,128)(2,1)S(1)}, bf16[128,512]{1,0:T(8,128)(2,1)S(1)}, u32[]{:S(2)}, u32[]{:S(2)}) %collective-permute-start.16) | collective-permute-done | bytes 131104 | tf_op jit(solution)/shard_map/ppermute | solution.py:679
  200.4 3.7 %all-to-all-start.6 = ((bf16[16,16,2048]{2,1,0:T(8,128)(2,1)}), bf16[16,16,2048]{2,1,0:T(8,128)(2,1)S(1)}, u32[]{:S(2)}, u32[]{:S(2)}) async-start(bf16[16,16,2048]{2,1,0:T(8,128)(2,1)} %get-tuple-element.94), calls=%async_computation.6 | async-start | bytes 2097152 | tf_op jit(solution)/shard_map/all_to_all | solution.py:601
  205.3 16.0 %collective-permute-done.19.wkv1_ref = bf16[512,512]{1,0:T(8,128)(2,1)S(1)} collective-permute-done((bf16[512,512]{1,0:T(8,128)(2,1)}, bf16[512,512]{1,0:T(8,128)(2,1)S(1)}, u32[]{:S(2)}, u32[]{:S(2)}) %collective-permute-start.19) | collective-permute-done | bytes 524320 | tf_op jit(solution)/shard_map/ppermute | solution.py:598
  223.9 23.0 %all_to_all.46 = bf16[16,16,2048]{2,1,0:T(8,128)(2,1)S(1)} all-to-all(bf16[16,16,2048]{2,1,0:T(8,128)(2,1)} %shard_map.136), channel_id=1, replica_groups=mesh['section'=2,'mp'=4,'dp'=16] {'dp'}, dimensions={0} | all-to-all | bytes 2097152 | tf_op jit(solution)/shard_map/all_to_all | solution.py:601
  246.9 8.3 %shard_map.137 = bf16[256,512]{1,0:T(8,128)(2,1)S(1)} custom-call(s32[2,3]{1,0:T(2,128)S(1)} %copy-done.2, bf16[256,2688]{1,0:T(8,128)(2,1)S(1)} %bitcast.20, bf16[256,2048]{1,0:T(8,128)(2,1)S(1)} %bitcast.22, bf16[512,2048]{1,0:T(8,128)(2,1)} %bitcast.43, bf16[512,2048]{1,0:T(8,128)(2,1)} %collective-permute-done.18.wq1_ref, bf16[512,512]{1,0:T(8,128)(2,1)} %bitcast.49, ...), custom_call_target="tpu_custom_call" | custom-call | flops 1610612736 | bytes 6291456 | tf_op jit(solution)/shard_map/pallas_call | solution.py:798
  257.0 5.5 %collective-permute-done.21.across_ref = bf16[128,512]{1,0:T(8,128)(2,1)S(1)} collective-permute-done((bf16[128,512]{1,0:T(8,128)(2,1)S(1)}, bf16[128,512]{1,0:T(8,128)(2,1)S(1)}, u32[]{:S(2)}, u32[]{:S(2)}) %collective-permute-start.21) | collective-permute-done | bytes 131104 | tf_op jit(solution)/shard_map/ppermute | solution.py:679
  263.9 2.5 shard_map.138
  266.3 23.2 %all_to_all.47.parts_ref = bf16[16,2,16,1280]{3,2,1,0:T(8,128)(2,1)S(1)} all-to-all(bf16[16,2,16,1280]{3,2,1,0:T(8,128)(2,1)S(1)} %get-tuple-element.103), channel_id=1, replica_groups=mesh['section'=2,'mp'=4,'dp'=16] {'dp'}, dimensions={0} | all-to-all | bytes 2621440 | tf_op jit(solution)/shard_map/all_to_all | solution.py:601
  289.7 5.5 %collective-permute-done.23 = bf16[16,1280]{1,0:T(8,128)(2,1)S(1)} collective-permute-done((bf16[16,1280]{1,0:T(8,128)(2,1)S(1)}, bf16[16,1280]{1,0:T(8,128)(2,1)S(1)}, u32[]{:S(2)}, u32[]{:S(2)}) %collective-permute-start.23) | collective-permute-done | bytes 40992 | tf_op jit(solution)/shard_map/ppermute | solution.py:869
  (81 shorter events, 41.5 us)
Async XLA Ops:
  1.5 8.7 %collective-permute-start = (bf16[64,512]{1,0:T(8,128)(2,1)S(1)}, bf16[64,512]{1,0:T(8,128)(2,1)S(1)}, u32[]{:S(2)}, u32[]{:S(2)}) collective-permute-start(bf16[64,512]{1,0:T(8,128)(2,1)S(1)} %get-tuple-element.109.mine_ref), channel_id=1, source_target_pairs={{0,16},{16,0},{32,48},{48,32},{1,17},{17,1},{33,49},{49,33},{2,18}... | collective-permute-start | bytes 196616 | tf_op jit(solution)/shard_map/ppermute | solution.py:679
  1.6 8.6 %collective-permute-start.1 = (bf16[64,512]{1,0:T(8,128)(2,1)S(1)}, bf16[64,512]{1,0:T(8,128)(2,1)S(1)}, u32[]{:S(2)}, u32[]{:S(2)}) collective-permute-start(bf16[64,512]{1,0:T(8,128)(2,1)S(1)} %get-tuple-element.109.mine_ref), channel_id=1, source_target_pairs={{0,32},{16,48},{32,0},{48,16},{1,33},{17,49},{33,1},{49,17},{2,34}... | collective-permute-start | bytes 196616 | tf_op jit(solution)/shard_map/ppermute | solution.py:679
  2.5 7.7 %collective-permute-start.2 = (bf16[64,512]{1,0:T(8,128)(2,1)S(1)}, bf16[64,512]{1,0:T(8,128)(2,1)S(1)}, u32[]{:S(2)}, u32[]{:S(2)}) collective-permute-start(bf16[64,512]{1,0:T(8,128)(2,1)S(1)} %get-tuple-element.109.mine_ref), channel_id=1, source_target_pairs={{0,48},{16,32},{32,16},{48,0},{1,49},{17,33},{33,17},{49,1},{2,50}... | collective-permute-start | bytes 196616 | tf_op jit(solution)/shard_map/ppermute | solution.py:679
  3.5 8.4 %collective-permute-start.4 = (f32[1,512]{1,0:T(1,128)}, f32[1,512]{1,0:T(1,128)S(1)}, u32[]{:S(2)}, u32[]{:S(2)}) collective-permute-start(f32[1,512]{1,0:T(1,128)} %bitcast.25), channel_id=1, source_target_pairs={{0,96},{16,112},{32,64},{48,80},{64,32},{80,48},{96,0},{112,16},{1... | collective-permute-start | bytes 6152 | tf_op jit(solution)/shard_map/ppermute | solution.py:598
  3.9 8.0 %collective-permute-start.3 = (bf16[64,512]{1,0:T(8,128)(2,1)S(1)}, bf16[64,512]{1,0:T(8,128)(2,1)S(1)}, u32[]{:S(2)}, u32[]{:S(2)}) collective-permute-start(bf16[64,512]{1,0:T(8,128)(2,1)S(1)} %bitcast.52), channel_id=1, source_target_pairs={{0,96},{16,112},{32,64},{48,80},{64,32},{80,48},{96,0},{112,16},{1... | collective-permute-start | bytes 196616 | tf_op jit(solution)/shard_map/ppermute | solution.py:598
  11.9 29.7 %all-to-all-start = ((bf16[16,16,2688]{2,1,0:T(8,128)(2,1)}), bf16[16,16,2688]{2,1,0:T(8,128)(2,1)S(1)}, u32[]{:S(2)}, u32[]{:S(2)}) async-start(bf16[16,16,2688]{2,1,0:T(8,128)(2,1)} %get-tuple-element.55), calls=%async_computation | async-start | bytes 2752512 | tf_op jit(solution)/shard_map/all_to_all | solution.py:601
  22.2 19.3 %collective-permute-start.5 = (bf16[640,512]{1,0:T(8,128)(2,1)S(1)}, bf16[640,512]{1,0:T(8,128)(2,1)}, u32[]{:S(2)}, u32[]{:S(2)}) collective-permute-start(bf16[640,512]{1,0:T(8,128)(2,1)S(1)} %get-tuple-element.107), channel_id=1, source_target_pairs={{0,96},{16,112},{32,64},{48,80},{1,97},{17,113},{33,65},{49,81},{2... | collective-permute-start | bytes 1966088 | tf_op jit(solution)/shard_map/ppermute | solution.py:598
  41.6 26.6 %all-to-all-start.1 = ((bf16[16,16,2688]{2,1,0:T(8,128)(2,1)}), bf16[16,16,2688]{2,1,0:T(8,128)(2,1)S(1)}, u32[]{:S(2)}, u32[]{:S(2)}) async-start(bf16[16,16,2688]{2,1,0:T(8,128)(2,1)} %shard_map.124), calls=%async_computation.1 | async-start | bytes 2752512 | tf_op jit(solution)/shard_map/all_to_all | solution.py:601
  48.5 54.8 %collective-permute-start.9 = (bf16[512,2048]{1,0:T(8,128)(2,1)}, bf16[512,2048]{1,0:T(8,128)(2,1)}, u32[]{:S(2)}, u32[]{:S(2)}) collective-permute-start(bf16[512,2048]{1,0:T(8,128)(2,1)} %bitcast.39), channel_id=1, source_target_pairs={{64,32},{80,48},{96,0},{112,16},{65,33},{81,49},{97,1},{113,17},{6... | collective-permute-start | bytes 6291464 | tf_op jit(solution)/shard_map/ppermute | solution.py:598
  51.1 26.3 %collective-permute-start.7 = (bf16[640,512]{1,0:T(8,128)(2,1)}, bf16[640,512]{1,0:T(8,128)(2,1)}, u32[]{:S(2)}, u32[]{:S(2)}) collective-permute-start(bf16[640,512]{1,0:T(8,128)(2,1)} %get-tuple-element.64), channel_id=1, source_target_pairs={{0,96},{16,112},{32,64},{48,80},{1,97},{17,113},{33,65},{49,81},{2... | collective-permute-start | bytes 1966088 | tf_op jit(solution)/shard_map/ppermute | solution.py:598
  68.6 7.6 %collective-permute-start.6 = (bf16[16,2688]{1,0:T(8,128)(2,1)S(1)}, bf16[16,2688]{1,0:T(8,128)(2,1)S(1)}, u32[]{:S(2)}, u32[]{:S(2)}) collective-permute-start(bf16[16,2688]{1,0:T(8,128)(2,1)S(1)} %shard_map.126), channel_id=1, source_target_pairs={{0,96},{16,112},{32,64},{48,80},{1,97},{17,113},{33,65},{49,81},{2... | collective-permute-start | bytes 258056 | tf_op jit(solution)/shard_map/ppermute | solution.py:598
  77.5 18.3 %copy-start.5 = (bf16[64,8,2,256]{3,1,2,0:T(8,128)(2,1)S(1)}, bf16[64,8,2,256]{3,1,2,0:T(8,128)(2,1)}, u32[]{:S(2)}) copy-start(bf16[64,8,2,256]{3,1,2,0:T(8,128)(2,1)} %copy.13) | copy-start | bytes 1572868
  77.5 25.8 %all-to-all-start.2 = ((bf16[16,16,2688]{2,1,0:T(8,128)(2,1)}), bf16[16,16,2688]{2,1,0:T(8,128)(2,1)S(1)}, u32[]{:S(2)}, u32[]{:S(2)}) async-start(bf16[16,16,2688]{2,1,0:T(8,128)(2,1)} %shard_map.127), calls=%async_computation.2 | async-start | bytes 2752512 | tf_op jit(solution)/shard_map/all_to_all | solution.py:601
  81.3 29.8 %copy-start.2 = (s32[2,3]{1,0:T(2,128)S(1)}, s32[2,3]{1,0:T(2,128)}, u32[]{:S(2)}) copy-start(s32[2,3]{1,0:T(2,128)} %seq_ref.5) | copy-start | bytes 76
  81.3 28.9 %collective-permute-start.10 = (bf16[768,512]{1,0:T(8,128)(2,1)}, bf16[768,512]{1,0:T(8,128)(2,1)S(1)}, u32[]{:S(2)}, u32[]{:S(2)}) collective-permute-start(bf16[768,512]{1,0:T(8,128)(2,1)} %slice.11), channel_id=1, source_target_pairs={{0,96},{16,112},{32,64},{48,80},{1,97},{17,113},{33,65},{49,81},{2... | collective-permute-start | bytes 2359304 | tf_op jit(solution)/shard_map/ppermute | solution.py:598
  82.6 13.1 %collective-permute-start.8 = (bf16[16,2688]{1,0:T(8,128)(2,1)S(1)}, bf16[16,2688]{1,0:T(8,128)(2,1)S(1)}, u32[]{:S(2)}, u32[]{:S(2)}) collective-permute-start(bf16[16,2688]{1,0:T(8,128)(2,1)S(1)} %shard_map.126), channel_id=1, source_target_pairs={{64,32},{80,48},{96,0},{112,16},{65,33},{81,49},{97,1},{113,17},{6... | collective-permute-start | bytes 258056 | tf_op jit(solution)/shard_map/ppermute | solution.py:598
  95.8 20.4 %collective-permute-start.11 = (bf16[512,512]{1,0:T(8,128)(2,1)S(1)}, bf16[512,512]{1,0:T(8,128)(2,1)}, u32[]{:S(2)}, u32[]{:S(2)}) collective-permute-start(bf16[512,512]{1,0:T(8,128)(2,1)S(1)} %bitcast.50), channel_id=1, source_target_pairs={{64,32},{80,48},{96,0},{112,16},{65,33},{81,49},{97,1},{113,17},{6... | collective-permute-start | bytes 1572872 | tf_op jit(solution)/shard_map/ppermute | solution.py:598
  103.3 23.2 %all-to-all-start.3 = ((bf16[16,16,2048]{2,1,0:T(8,128)(2,1)}), bf16[16,16,2048]{2,1,0:T(8,128)(2,1)}, u32[]{:S(2)}, u32[]{:S(2)}) async-start(bf16[16,16,2048]{2,1,0:T(8,128)(2,1)} %shard_map.128), calls=%async_computation.3 | async-start | bytes 2097152 | tf_op jit(solution)/shard_map/all_to_all | solution.py:601
  116.2 1.6 collective-permute-start.12
  117.8 5.6 %collective-permute-start.13 = (bf16[128,512]{1,0:T(8,128)(2,1)S(1)}, bf16[128,512]{1,0:T(8,128)(2,1)S(1)}, u32[]{:S(2)}, u32[]{:S(2)}) collective-permute-start(bf16[128,512]{1,0:T(8,128)(2,1)S(1)} %add_convert_fusion.5), channel_id=1, source_target_pairs={{0,32},{16,48},{32,0},{48,16},{1,33},{17,49},{33,1},{49,17},{2,34}... | collective-permute-start | bytes 393224 | tf_op jit(solution)/shard_map/ppermute | solution.py:679
  123.4 1.3 collective-permute-start.14
  156.4 24.7 %all-to-all-start.5 = ((bf16[16,16,2688]{2,1,0:T(8,128)(2,1)}), bf16[16,16,2688]{2,1,0:T(8,128)(2,1)S(1)}, u32[]{:S(2)}, u32[]{:S(2)}) async-start(bf16[16,16,2688]{2,1,0:T(8,128)(2,1)} %shard_map.132), calls=%async_computation.5 | async-start | bytes 2752512 | tf_op jit(solution)/shard_map/all_to_all | solution.py:601
  160.1 62.0 %collective-permute-start.18 = (bf16[512,2048]{1,0:T(8,128)(2,1)}, bf16[512,2048]{1,0:T(8,128)(2,1)}, u32[]{:S(2)}, u32[]{:S(2)}) collective-permute-start(bf16[512,2048]{1,0:T(8,128)(2,1)} %bitcast.41), channel_id=1, source_target_pairs={{0,96},{16,112},{32,64},{48,80},{1,97},{17,113},{33,65},{49,81},{2... | collective-permute-start | bytes 6291464 | tf_op jit(solution)/shard_map/ppermute | solution.py:598
  190.2 1.6 collective-permute-start.15
  191.8 5.6 %collective-permute-start.16 = (bf16[128,512]{1,0:T(8,128)(2,1)S(1)}, bf16[128,512]{1,0:T(8,128)(2,1)S(1)}, u32[]{:S(2)}, u32[]{:S(2)}) collective-permute-start(bf16[128,512]{1,0:T(8,128)(2,1)S(1)} %add_convert_fusion.4), channel_id=1, source_target_pairs={{0,32},{16,48},{32,0},{48,16},{1,33},{17,49},{33,1},{49,17},{2,34}... | collective-permute-start | bytes 393224 | tf_op jit(solution)/shard_map/ppermute | solution.py:679
  197.4 1.3 collective-permute-start.17
  200.4 22.1 %all-to-all-start.6 = ((bf16[16,16,2048]{2,1,0:T(8,128)(2,1)}), bf16[16,16,2048]{2,1,0:T(8,128)(2,1)S(1)}, u32[]{:S(2)}, u32[]{:S(2)}) async-start(bf16[16,16,2048]{2,1,0:T(8,128)(2,1)} %get-tuple-element.94), calls=%async_computation.6 | async-start | bytes 2097152 | tf_op jit(solution)/shard_map/all_to_all | solution.py:601
  204.0 17.3 %collective-permute-start.19 = (bf16[512,512]{1,0:T(8,128)(2,1)}, bf16[512,512]{1,0:T(8,128)(2,1)S(1)}, u32[]{:S(2)}, u32[]{:S(2)}) collective-permute-start(bf16[512,512]{1,0:T(8,128)(2,1)} %bitcast.48), channel_id=1, source_target_pairs={{0,96},{16,112},{32,64},{48,80},{1,97},{17,113},{33,65},{49,81},{2... | collective-permute-start | bytes 1572872 | tf_op jit(solution)/shard_map/ppermute | solution.py:598
  255.2 1.6 collective-permute-start.20
  256.9 5.6 %collective-permute-start.21 = (bf16[128,512]{1,0:T(8,128)(2,1)S(1)}, bf16[128,512]{1,0:T(8,128)(2,1)S(1)}, u32[]{:S(2)}, u32[]{:S(2)}) collective-permute-start(bf16[128,512]{1,0:T(8,128)(2,1)S(1)} %add_convert_fusion.3), channel_id=1, source_target_pairs={{0,32},{16,48},{32,0},{48,16},{1,33},{17,49},{33,1},{49,17},{2,34}... | collective-permute-start | bytes 393224 | tf_op jit(solution)/shard_map/ppermute | solution.py:679
  262.5 1.3 collective-permute-start.22
  289.6 5.6 %collective-permute-start.23 = (bf16[16,1280]{1,0:T(8,128)(2,1)S(1)}, bf16[16,1280]{1,0:T(8,128)(2,1)S(1)}, u32[]{:S(2)}, u32[]{:S(2)}) collective-permute-start(bf16[16,1280]{1,0:T(8,128)(2,1)S(1)} %get-tuple-element.105), channel_id=1, source_target_pairs={{0,64},{64,0},{1,65},{65,1},{2,66},{66,2},{3,67},{67,3},{4,68},{68... | collective-permute-start | bytes 122888 | tf_op jit(solution)/shard_map/ppermute | solution.py:869
  (7 other events, 60.0 us)

commit v6 on v5

--- a/solution.py
+++ b/solution.py
@@ -835,8 +835,10 @@
         compiler_params=params(24),
         cost_estimate=cost(2 * tokens * width * q_cols, 4 << 20),
     )(mine_all, own_all, *sums, gain_x, gain, loaded(False, pieces[:1], pieces[1:]))
-    parts, wq_a, wkv_a = lax.optimization_barrier((scatter(parts, "dp"), wq_a, wkv_a))
-    head_grad_first = spread(summed_copies(plain_sum, parts))
+    parts, wq_a = lax.optimization_barrier((scatter(parts, "dp"), wq_a))
+    head_grad_first, wkv_a = lax.optimization_barrier(
+        (spread(summed_copies(plain_sum, parts)), wkv_a)
+    )
     sums, _ = layer_backward(qkv_first, head_grad_first, (wq, wq_a), (wkv, wkv_a))
 
     hidden_cols = merger_weight.shape[0]

time: 297 us -> 298 us (level)
  blocking collectives: 85.9 us -> 65.9 us
  waiting for transfers between devices: 92.9 us -> 110 us
  starting transfers between devices: 61.8 us -> 66 us
    all_to_all x3 -> x2, blocking collectives: 74.3 us -> 54.3 us  [scatter(): return lax.all_to_all(array, axis, split_axis=0, concat_axis=0, tiled=True)]
    all_to_all x6 -> x7, waiting for transfers between devices: 29.6 us -> 42.4 us  [scatter(): return lax.all_to_all(array, axis, split_axis=0, concat_axis=0, tiled=True)]
    ppermute x11, waiting for transfers between devices: 36.5 us -> 41.5 us  [swap(): return lax.ppermute(array, ('section', 'mp'), pairs)]
    all_to_all x6 -> x7, starting transfers between devices: 33.1 us -> 36.8 us  [scatter(): return lax.all_to_all(array, axis, split_axis=0, concat_axis=0, tiled=True)]
  transfers between devices with their start and end apart: 30 -> 31, of which waited for: 18 -> 20; matrix products, arithmetic and copies ran while one was open for 2% -> 2% of each run, Pallas kernels for 10% -> 10%
where the time goes in v6:
time: 298 us; the launch traced here: 297 us
  waiting for transfers between devices  110 us (37%)
  starting transfers between devices  66 us (22%)
  blocking collectives  65.9 us (22%)
  Pallas kernels  44.4 us (15%)
  local copies, waits for them, and re-layouts  7.16 us (2%)
    all_to_all x2, blocking collectives, scatter(): return lax.all_to_all(array, axis, split_axis=0, concat_axis=0, tiled=True)  54.3 us
    all_to_all x7, waiting for transfers between devices, scatter(): return lax.all_to_all(array, axis, split_axis=0, concat_axis=0, tiled=True)  42.4 us
    ppermute x11, waiting for transfers between devices, swap(): return lax.ppermute(array, ('section', 'mp'), pairs)  41.5 us
    all_to_all x7, starting transfers between devices, scatter(): return lax.all_to_all(array, axis, split_axis=0, concat_axis=0, tiled=True)  36.8 us
    ppermute x11, starting transfers between devices, swap(): return lax.ppermute(array, ('section', 'mp'), pairs)  26.1 us
    ppermute x12, waiting for transfers between devices, beside(): lax.ppermute(array, 'mp', [(i, i ^ distance) for i in range(mp_count)])  21.1 us
    pallas_call x2, Pallas kernels, layer_backward(): pl.pallas_call(backward_kernel, out_shape=shape_of((tokens, width), BF),...  17.4 us
    all_gather x2, blocking collectives, gather(): return lax.all_gather(array, axis, axis=0, tiled=True)  11.6 us
  transfers between devices with their start and end apart: 31, of which 20 were waited for; matrix products, arithmetic and copies ran while one was open for 2% of the time, Pallas kernels for 10%

profile of v6, /device:TPU:6, one launch (start us, length us, event | category | flops | bytes accessed | tf_op | source)
XLA Modules:
  0.0 297.0 jit_solution(12722464484740483910)
XLA Ops:
  3.9 2.8 collective-permute-start.3
  11.9 8.1 %all-to-all-start = ((bf16[16,16,2688]{2,1,0:T(8,128)(2,1)}), bf16[16,16,2688]{2,1,0:T(8,128)(2,1)S(1)}, u32[]{:S(2)}, u32[]{:S(2)}) async-start(bf16[16,16,2688]{2,1,0:T(8,128)(2,1)} %get-tuple-element.56), calls=%async_computation | async-start | bytes 2752512 | tf_op jit(solution)/shard_map/all_to_all | solution.py:601
  25.6 5.8 %all_gather.6.x_ref = bf16[256,512]{1,0:T(8,128)(2,1)S(1)} all-gather(bf16[64,512]{1,0:T(8,128)(2,1)S(1)} %collective-permute-done.3), channel_id=1, replica_groups=mesh['section'=2,'mp'=4,'dp'=16] {'mp'}, dimensions={0}, use_global_device_ids=true | all-gather | bytes 327680 | tf_op jit(solution)/shard_map/all_gather | solution.py:607
  31.4 3.3 %shard_map.124 = bf16[16,16,2688]{2,1,0:T(8,128)(2,1)} custom-call(bf16[256,512]{1,0:T(8,128)(2,1)S(1)} %all_gather.6.x_ref, f32[1,512]{1,0:T(1,128)S(1)} %bitcast.27, bf16[512,2048]{1,0:T(8,128)(2,1)} %bitcast.38, bf16[512,512]{1,0:T(8,128)(2,1)} %bitcast.45, bf16[2048,512]{1,0:T(8,128)(2,1)} %bitcast.34), custom_call_target="tpu_custom_call" | custom-call | flops 704643072 | bytes 6291456 | tf_op jit(solution)/shard_map/pallas_call | solution.py:622
  34.7 6.8 %collective-permute-done.5.refs_0_.refs_1_ = bf16[640,512]{1,0:T(8,128)(2,1)} collective-permute-done((bf16[640,512]{1,0:T(8,128)(2,1)S(1)}, bf16[640,512]{1,0:T(8,128)(2,1)}, u32[]{:S(2)}, u32[]{:S(2)}) %collective-permute-start.5) | collective-permute-done | bytes 655392 | tf_op jit(solution)/shard_map/ppermute | solution.py:598
  41.6 6.9 %all-to-all-start.1 = ((bf16[16,16,2688]{2,1,0:T(8,128)(2,1)}), bf16[16,16,2688]{2,1,0:T(8,128)(2,1)S(1)}, u32[]{:S(2)}, u32[]{:S(2)}) async-start(bf16[16,16,2688]{2,1,0:T(8,128)(2,1)} %shard_map.124), calls=%async_computation.1 | async-start | bytes 2752512 | tf_op jit(solution)/shard_map/all_to_all | solution.py:601
  48.5 2.7 collective-permute-start.9
  52.5 5.8 %all-gather = bf16[1,256,512]{2,1,0:T(8,128)(2,1)S(1)} all-gather(bf16[1,64,512]{2,1,0:T(8,128)(2,1)S(1)} %get-tuple-element.110), channel_id=2, replica_groups=mesh['section'=2,'mp'=4,'dp'=16] {'mp'}, dimensions={1}, use_global_device_ids=true | all-gather | bytes 327680 | tf_op jit(solution)/shard_map/all_gather | solution.py:607
  58.7 9.6 %all-to-all-done.1.parts_ref = bf16[16,16,2688]{2,1,0:T(8,128)(2,1)S(1)} async-done(((bf16[16,16,2688]{2,1,0:T(8,128)(2,1)}), bf16[16,16,2688]{2,1,0:T(8,128)(2,1)S(1)}, u32[]{:S(2)}, u32[]{:S(2)}) %all-to-all-start.1) | async-done | bytes 1376288 | tf_op jit(solution)/shard_map/all_to_all | solution.py:601
  70.0 6.3 %collective-permute-done.6.second_ref = bf16[16,2688]{1,0:T(8,128)(2,1)S(1)} collective-permute-done((bf16[16,2688]{1,0:T(8,128)(2,1)S(1)}, bf16[16,2688]{1,0:T(8,128)(2,1)S(1)}, u32[]{:S(2)}, u32[]{:S(2)}) %collective-permute-start.6) | collective-permute-done | bytes 86048 | tf_op jit(solution)/shard_map/ppermute | solution.py:598
  77.5 3.8 %all-to-all-start.2 = ((bf16[16,16,2688]{2,1,0:T(8,128)(2,1)}), bf16[16,16,2688]{2,1,0:T(8,128)(2,1)S(1)}, u32[]{:S(2)}, u32[]{:S(2)}) async-start(bf16[16,16,2688]{2,1,0:T(8,128)(2,1)} %shard_map.127), calls=%async_computation.2 | async-start | bytes 2752512 | tf_op jit(solution)/shard_map/all_to_all | solution.py:601
  82.7 5.8 %collective-permute-start.8 = (bf16[16,2688]{1,0:T(8,128)(2,1)S(1)}, bf16[16,2688]{1,0:T(8,128)(2,1)S(1)}, u32[]{:S(2)}, u32[]{:S(2)}) collective-permute-start(bf16[16,2688]{1,0:T(8,128)(2,1)S(1)} %shard_map.126), channel_id=1, source_target_pairs={{64,32},{80,48},{96,0},{112,16},{65,33},{81,49},{97,1},{113,17},{6... | collective-permute-start | bytes 258056 | tf_op jit(solution)/shard_map/ppermute | solution.py:598
  88.5 7.3 %collective-permute-done.8.first_ref = bf16[16,2688]{1,0:T(8,128)(2,1)S(1)} collective-permute-done((bf16[16,2688]{1,0:T(8,128)(2,1)S(1)}, bf16[16,2688]{1,0:T(8,128)(2,1)S(1)}, u32[]{:S(2)}, u32[]{:S(2)}) %collective-permute-start.8) | collective-permute-done | bytes 86048 | tf_op jit(solution)/shard_map/ppermute | solution.py:598
  95.8 6.4 %collective-permute-start.11 = (bf16[512,512]{1,0:T(8,128)(2,1)S(1)}, bf16[512,512]{1,0:T(8,128)(2,1)}, u32[]{:S(2)}, u32[]{:S(2)}) collective-permute-start(bf16[512,512]{1,0:T(8,128)(2,1)S(1)} %bitcast.50), channel_id=1, source_target_pairs={{64,32},{80,48},{96,0},{112,16},{65,33},{81,49},{97,1},{113,17},{6... | collective-permute-start | bytes 1572872 | tf_op jit(solution)/shard_map/ppermute | solution.py:598
  103.3 7.0 %all-to-all-start.3 = ((bf16[16,16,2048]{2,1,0:T(8,128)(2,1)}), bf16[16,16,2048]{2,1,0:T(8,128)(2,1)}, u32[]{:S(2)}, u32[]{:S(2)}) async-start(bf16[16,16,2048]{2,1,0:T(8,128)(2,1)} %shard_map.128), calls=%async_computation.3 | async-start | bytes 2097152 | tf_op jit(solution)/shard_map/all_to_all | solution.py:601
  111.2 5.0 %shard_map.129 = bf16[256,512]{1,0:T(8,128)(2,1)S(1)} custom-call(s32[2,3]{1,0:T(2,128)S(1)} %copy-done.2, bf16[256,2688]{1,0:T(8,128)(2,1)S(1)} %bitcast.19, bf16[2048,512]{1,0:T(8,128)(2,1)} %bitcast.35, bf16[640,512]{1,0:T(8,128)(2,1)} %collective-permute-done.5.refs_0_.refs_1_, bf16[640,512]{1,0:T(8,128)(2,1)} %collective-permute-done.7.refs_1_.refs_2_, ...), custom_call_target="tpu_custom_call" | custom-call | flops 805306368 | bytes 4194304 | tf_op jit(solution)/shard_map/pallas_call | solution.py:752
  119.7 3.8 %collective-permute-done.13.across_ref = bf16[128,512]{1,0:T(8,128)(2,1)S(1)} collective-permute-done((bf16[128,512]{1,0:T(8,128)(2,1)S(1)}, bf16[128,512]{1,0:T(8,128)(2,1)S(1)}, u32[]{:S(2)}, u32[]{:S(2)}) %collective-permute-start.13) | collective-permute-done | bytes 131104 | tf_op jit(solution)/shard_map/ppermute | solution.py:679
  126.6 28.1 %all_to_all.45.parts_ref = bf16[16,16,2688]{2,1,0:T(8,128)(2,1)S(1)} all-to-all(bf16[16,16,2688]{2,1,0:T(8,128)(2,1)} %shard_map.131), channel_id=1, replica_groups=mesh['section'=2,'mp'=4,'dp'=16] {'dp'}, dimensions={0} | all-to-all | bytes 2752512 | tf_op jit(solution)/shard_map/all_to_all | solution.py:601
  156.5 3.7 %all-to-all-start.5 = ((bf16[16,16,2688]{2,1,0:T(8,128)(2,1)}), bf16[16,16,2688]{2,1,0:T(8,128)(2,1)S(1)}, u32[]{:S(2)}, u32[]{:S(2)}) async-start(bf16[16,16,2688]{2,1,0:T(8,128)(2,1)} %shard_map.132), calls=%async_computation.5 | async-start | bytes 2752512 | tf_op jit(solution)/shard_map/all_to_all | solution.py:601
  161.5 19.6 %all-to-all-done.5 = bf16[16,16,2688]{2,1,0:T(8,128)(2,1)S(1)} async-done(((bf16[16,16,2688]{2,1,0:T(8,128)(2,1)}), bf16[16,16,2688]{2,1,0:T(8,128)(2,1)S(1)}, u32[]{:S(2)}, u32[]{:S(2)}) %all-to-all-start.5) | async-done | bytes 1376288 | tf_op jit(solution)/shard_map/all_to_all | solution.py:601
  181.1 9.1 %shard_map.133 = bf16[256,512]{1,0:T(8,128)(2,1)S(1)} custom-call(s32[2,3]{1,0:T(2,128)S(1)} %copy-done.2, bf16[256,2688]{1,0:T(8,128)(2,1)S(1)} %bitcast.21, bf16[256,2048]{1,0:T(8,128)(2,1)} %bitcast.7.grads_ref, bf16[512,2048]{1,0:T(8,128)(2,1)} %collective-permute-done.9.refs_0_.wq0_ref, bf16[512,2048]{1,0:T(8,128)(2,1)} %bitcast.42, ...), custom_call_target="tpu_custom_call" | custom-call | flops 1610612736 | bytes 6291456 | tf_op jit(solution)/shard_map/pallas_call | solution.py:798
  193.8 3.7 %collective-permute-done.16.across_ref = bf16[128,512]{1,0:T(8,128)(2,1)S(1)} collective-permute-done((bf16[128,512]{1,0:T(8,128)(2,1)S(1)}, bf16[128,512]{1,0:T(8,128)(2,1)S(1)}, u32[]{:S(2)}, u32[]{:S(2)}) %collective-permute-start.16) | collective-permute-done | bytes 131104 | tf_op jit(solution)/shard_map/ppermute | solution.py:679
  200.4 3.7 %all-to-all-start.6 = ((bf16[16,16,2048]{2,1,0:T(8,128)(2,1)}), bf16[16,16,2048]{2,1,0:T(8,128)(2,1)S(1)}, u32[]{:S(2)}, u32[]{:S(2)}) async-start(bf16[16,16,2048]{2,1,0:T(8,128)(2,1)} %get-tuple-element.95), calls=%async_computation.6 | async-start | bytes 2097152 | tf_op jit(solution)/shard_map/all_to_all | solution.py:601
  204.1 6.1 %collective-permute-done.18.wq1_ref = bf16[512,2048]{1,0:T(8,128)(2,1)} collective-permute-done((bf16[512,2048]{1,0:T(8,128)(2,1)}, bf16[512,2048]{1,0:T(8,128)(2,1)}, u32[]{:S(2)}, u32[]{:S(2)}) %collective-permute-start.18) | collective-permute-done | bytes 2097184 | tf_op jit(solution)/shard_map/ppermute | solution.py:598
  210.2 12.3 %all-to-all-done.6.parts_ref = bf16[16,16,2048]{2,1,0:T(8,128)(2,1)S(1)} async-done(((bf16[16,16,2048]{2,1,0:T(8,128)(2,1)}), bf16[16,16,2048]{2,1,0:T(8,128)(2,1)S(1)}, u32[]{:S(2)}, u32[]{:S(2)}) %all-to-all-start.6) | async-done | bytes 1048608 | tf_op jit(solution)/shard_map/all_to_all | solution.py:601
  224.0 3.7 %all-to-all-start.7 = ((bf16[16,16,2048]{2,1,0:T(8,128)(2,1)}), bf16[16,16,2048]{2,1,0:T(8,128)(2,1)S(1)}, u32[]{:S(2)}, u32[]{:S(2)}) async-start(bf16[16,16,2048]{2,1,0:T(8,128)(2,1)} %shard_map.136), calls=%async_computation.7 | async-start | bytes 2097152 | tf_op jit(solution)/shard_map/all_to_all | solution.py:601
  229.1 14.9 %collective-permute-done.19.wkv1_ref = bf16[512,512]{1,0:T(8,128)(2,1)} collective-permute-done((bf16[512,512]{1,0:T(8,128)(2,1)}, bf16[512,512]{1,0:T(8,128)(2,1)}, u32[]{:S(2)}, u32[]{:S(2)}) %collective-permute-start.19) | collective-permute-done | bytes 524320 | tf_op jit(solution)/shard_map/ppermute | solution.py:598
  244.9 8.3 %shard_map.137 = bf16[256,512]{1,0:T(8,128)(2,1)S(1)} custom-call(s32[2,3]{1,0:T(2,128)S(1)} %copy-done.2, bf16[256,2688]{1,0:T(8,128)(2,1)S(1)} %bitcast.20, bf16[256,2048]{1,0:T(8,128)(2,1)S(1)} %bitcast.22, bf16[512,2048]{1,0:T(8,128)(2,1)} %bitcast.43, bf16[512,2048]{1,0:T(8,128)(2,1)} %collective-permute-done.18.wq1_ref, bf16[512,512]{1,0:T(8,128)(2,1)} %bitcast.49, ...), custom_call_target="tpu_custom_call" | custom-call | flops 1610612736 | bytes 6291456 | tf_op jit(solution)/shard_map/pallas_call | solution.py:798
  255.2 5.3 %collective-permute-done.21.across_ref = bf16[128,512]{1,0:T(8,128)(2,1)S(1)} collective-permute-done((bf16[128,512]{1,0:T(8,128)(2,1)S(1)}, bf16[128,512]{1,0:T(8,128)(2,1)S(1)}, u32[]{:S(2)}, u32[]{:S(2)}) %collective-permute-start.21) | collective-permute-done | bytes 131104 | tf_op jit(solution)/shard_map/ppermute | solution.py:679
  261.8 2.5 shard_map.138
  264.3 26.2 %all_to_all.46.parts_ref = bf16[16,2,16,1280]{3,2,1,0:T(8,128)(2,1)S(1)} all-to-all(bf16[16,2,16,1280]{3,2,1,0:T(8,128)(2,1)S(1)} %get-tuple-element.105), channel_id=1, replica_groups=mesh['section'=2,'mp'=4,'dp'=16] {'dp'}, dimensions={0} | all-to-all | bytes 2621440 | tf_op jit(solution)/shard_map/all_to_all | solution.py:601
  290.7 5.5 %collective-permute-done.23 = bf16[16,1280]{1,0:T(8,128)(2,1)S(1)} collective-permute-done((bf16[16,1280]{1,0:T(8,128)(2,1)S(1)}, bf16[16,1280]{1,0:T(8,128)(2,1)S(1)}, u32[]{:S(2)}, u32[]{:S(2)}) %collective-permute-start.23) | collective-permute-done | bytes 40992 | tf_op jit(solution)/shard_map/ppermute | solution.py:871
  (80 shorter events, 46.0 us)
Async XLA Ops:
  1.5 8.7 %collective-permute-start = (bf16[64,512]{1,0:T(8,128)(2,1)S(1)}, bf16[64,512]{1,0:T(8,128)(2,1)S(1)}, u32[]{:S(2)}, u32[]{:S(2)}) collective-permute-start(bf16[64,512]{1,0:T(8,128)(2,1)S(1)} %get-tuple-element.111.mine_ref), channel_id=1, source_target_pairs={{0,16},{16,0},{32,48},{48,32},{1,17},{17,1},{33,49},{49,33},{2,18}... | collective-permute-start | bytes 196616 | tf_op jit(solution)/shard_map/ppermute | solution.py:679
  1.6 8.6 %collective-permute-start.1 = (bf16[64,512]{1,0:T(8,128)(2,1)S(1)}, bf16[64,512]{1,0:T(8,128)(2,1)S(1)}, u32[]{:S(2)}, u32[]{:S(2)}) collective-permute-start(bf16[64,512]{1,0:T(8,128)(2,1)S(1)} %get-tuple-element.111.mine_ref), channel_id=1, source_target_pairs={{0,32},{16,48},{32,0},{48,16},{1,33},{17,49},{33,1},{49,17},{2,34}... | collective-permute-start | bytes 196616 | tf_op jit(solution)/shard_map/ppermute | solution.py:679
  2.5 7.7 %collective-permute-start.2 = (bf16[64,512]{1,0:T(8,128)(2,1)S(1)}, bf16[64,512]{1,0:T(8,128)(2,1)S(1)}, u32[]{:S(2)}, u32[]{:S(2)}) collective-permute-start(bf16[64,512]{1,0:T(8,128)(2,1)S(1)} %get-tuple-element.111.mine_ref), channel_id=1, source_target_pairs={{0,48},{16,32},{32,16},{48,0},{1,49},{17,33},{33,17},{49,1},{2,50}... | collective-permute-start | bytes 196616 | tf_op jit(solution)/shard_map/ppermute | solution.py:679
  3.5 8.4 %collective-permute-start.4 = (f32[1,512]{1,0:T(1,128)}, f32[1,512]{1,0:T(1,128)S(1)}, u32[]{:S(2)}, u32[]{:S(2)}) collective-permute-start(f32[1,512]{1,0:T(1,128)} %bitcast.25), channel_id=1, source_target_pairs={{0,96},{16,112},{32,64},{48,80},{64,32},{80,48},{96,0},{112,16},{1... | collective-permute-start | bytes 6152 | tf_op jit(solution)/shard_map/ppermute | solution.py:598
  3.9 8.0 %collective-permute-start.3 = (bf16[64,512]{1,0:T(8,128)(2,1)S(1)}, bf16[64,512]{1,0:T(8,128)(2,1)S(1)}, u32[]{:S(2)}, u32[]{:S(2)}) collective-permute-start(bf16[64,512]{1,0:T(8,128)(2,1)S(1)} %bitcast.52), channel_id=1, source_target_pairs={{0,96},{16,112},{32,64},{48,80},{64,32},{80,48},{96,0},{112,16},{1... | collective-permute-start | bytes 196616 | tf_op jit(solution)/shard_map/ppermute | solution.py:598
  11.9 29.7 %all-to-all-start = ((bf16[16,16,2688]{2,1,0:T(8,128)(2,1)}), bf16[16,16,2688]{2,1,0:T(8,128)(2,1)S(1)}, u32[]{:S(2)}, u32[]{:S(2)}) async-start(bf16[16,16,2688]{2,1,0:T(8,128)(2,1)} %get-tuple-element.56), calls=%async_computation | async-start | bytes 2752512 | tf_op jit(solution)/shard_map/all_to_all | solution.py:601
  22.2 19.3 %collective-permute-start.5 = (bf16[640,512]{1,0:T(8,128)(2,1)S(1)}, bf16[640,512]{1,0:T(8,128)(2,1)}, u32[]{:S(2)}, u32[]{:S(2)}) collective-permute-start(bf16[640,512]{1,0:T(8,128)(2,1)S(1)} %get-tuple-element.109), channel_id=1, source_target_pairs={{0,96},{16,112},{32,64},{48,80},{1,97},{17,113},{33,65},{49,81},{2... | collective-permute-start | bytes 1966088 | tf_op jit(solution)/shard_map/ppermute | solution.py:598
  41.6 26.6 %all-to-all-start.1 = ((bf16[16,16,2688]{2,1,0:T(8,128)(2,1)}), bf16[16,16,2688]{2,1,0:T(8,128)(2,1)S(1)}, u32[]{:S(2)}, u32[]{:S(2)}) async-start(bf16[16,16,2688]{2,1,0:T(8,128)(2,1)} %shard_map.124), calls=%async_computation.1 | async-start | bytes 2752512 | tf_op jit(solution)/shard_map/all_to_all | solution.py:601
  48.5 54.8 %collective-permute-start.9 = (bf16[512,2048]{1,0:T(8,128)(2,1)}, bf16[512,2048]{1,0:T(8,128)(2,1)}, u32[]{:S(2)}, u32[]{:S(2)}) collective-permute-start(bf16[512,2048]{1,0:T(8,128)(2,1)} %bitcast.39), channel_id=1, source_target_pairs={{64,32},{80,48},{96,0},{112,16},{65,33},{81,49},{97,1},{113,17},{6... | collective-permute-start | bytes 6291464 | tf_op jit(solution)/shard_map/ppermute | solution.py:598
  51.2 26.3 %collective-permute-start.7 = (bf16[640,512]{1,0:T(8,128)(2,1)}, bf16[640,512]{1,0:T(8,128)(2,1)}, u32[]{:S(2)}, u32[]{:S(2)}) collective-permute-start(bf16[640,512]{1,0:T(8,128)(2,1)} %get-tuple-element.65), channel_id=1, source_target_pairs={{0,96},{16,112},{32,64},{48,80},{1,97},{17,113},{33,65},{49,81},{2... | collective-permute-start | bytes 1966088 | tf_op jit(solution)/shard_map/ppermute | solution.py:598
  68.7 7.6 %collective-permute-start.6 = (bf16[16,2688]{1,0:T(8,128)(2,1)S(1)}, bf16[16,2688]{1,0:T(8,128)(2,1)S(1)}, u32[]{:S(2)}, u32[]{:S(2)}) collective-permute-start(bf16[16,2688]{1,0:T(8,128)(2,1)S(1)} %shard_map.126), channel_id=1, source_target_pairs={{0,96},{16,112},{32,64},{48,80},{1,97},{17,113},{33,65},{49,81},{2... | collective-permute-start | bytes 258056 | tf_op jit(solution)/shard_map/ppermute | solution.py:598
  77.5 25.8 %all-to-all-start.2 = ((bf16[16,16,2688]{2,1,0:T(8,128)(2,1)}), bf16[16,16,2688]{2,1,0:T(8,128)(2,1)S(1)}, u32[]{:S(2)}, u32[]{:S(2)}) async-start(bf16[16,16,2688]{2,1,0:T(8,128)(2,1)} %shard_map.127), calls=%async_computation.2 | async-start | bytes 2752512 | tf_op jit(solution)/shard_map/all_to_all | solution.py:601
  81.4 29.9 %copy-start.2 = (s32[2,3]{1,0:T(2,128)S(1)}, s32[2,3]{1,0:T(2,128)}, u32[]{:S(2)}) copy-start(s32[2,3]{1,0:T(2,128)} %seq_ref.5) | copy-start | bytes 76
  81.4 29.0 %collective-permute-start.10 = (bf16[768,512]{1,0:T(8,128)(2,1)}, bf16[768,512]{1,0:T(8,128)(2,1)S(1)}, u32[]{:S(2)}, u32[]{:S(2)}) collective-permute-start(bf16[768,512]{1,0:T(8,128)(2,1)} %slice.11), channel_id=1, source_target_pairs={{0,96},{16,112},{32,64},{48,80},{1,97},{17,113},{33,65},{49,81},{2... | collective-permute-start | bytes 2359304 | tf_op jit(solution)/shard_map/ppermute | solution.py:598
  82.7 13.1 %collective-permute-start.8 = (bf16[16,2688]{1,0:T(8,128)(2,1)S(1)}, bf16[16,2688]{1,0:T(8,128)(2,1)S(1)}, u32[]{:S(2)}, u32[]{:S(2)}) collective-permute-start(bf16[16,2688]{1,0:T(8,128)(2,1)S(1)} %shard_map.126), channel_id=1, source_target_pairs={{64,32},{80,48},{96,0},{112,16},{65,33},{81,49},{97,1},{113,17},{6... | collective-permute-start | bytes 258056 | tf_op jit(solution)/shard_map/ppermute | solution.py:598
  95.8 20.4 %collective-permute-start.11 = (bf16[512,512]{1,0:T(8,128)(2,1)S(1)}, bf16[512,512]{1,0:T(8,128)(2,1)}, u32[]{:S(2)}, u32[]{:S(2)}) collective-permute-start(bf16[512,512]{1,0:T(8,128)(2,1)S(1)} %bitcast.50), channel_id=1, source_target_pairs={{64,32},{80,48},{96,0},{112,16},{65,33},{81,49},{97,1},{113,17},{6... | collective-permute-start | bytes 1572872 | tf_op jit(solution)/shard_map/ppermute | solution.py:598
  103.3 23.2 %all-to-all-start.3 = ((bf16[16,16,2048]{2,1,0:T(8,128)(2,1)}), bf16[16,16,2048]{2,1,0:T(8,128)(2,1)}, u32[]{:S(2)}, u32[]{:S(2)}) async-start(bf16[16,16,2048]{2,1,0:T(8,128)(2,1)} %shard_map.128), calls=%async_computation.3 | async-start | bytes 2097152 | tf_op jit(solution)/shard_map/all_to_all | solution.py:601
  116.2 1.6 collective-permute-start.12
  117.9 5.6 %collective-permute-start.13 = (bf16[128,512]{1,0:T(8,128)(2,1)S(1)}, bf16[128,512]{1,0:T(8,128)(2,1)S(1)}, u32[]{:S(2)}, u32[]{:S(2)}) collective-permute-start(bf16[128,512]{1,0:T(8,128)(2,1)S(1)} %add_convert_fusion.5), channel_id=1, source_target_pairs={{0,32},{16,48},{32,0},{48,16},{1,33},{17,49},{33,1},{49,17},{2,34}... | collective-permute-start | bytes 393224 | tf_op jit(solution)/shard_map/ppermute | solution.py:679
  123.5 1.3 collective-permute-start.14
  156.5 24.7 %all-to-all-start.5 = ((bf16[16,16,2688]{2,1,0:T(8,128)(2,1)}), bf16[16,16,2688]{2,1,0:T(8,128)(2,1)S(1)}, u32[]{:S(2)}, u32[]{:S(2)}) async-start(bf16[16,16,2688]{2,1,0:T(8,128)(2,1)} %shard_map.132), calls=%async_computation.5 | async-start | bytes 2752512 | tf_op jit(solution)/shard_map/all_to_all | solution.py:601
  160.2 50.0 %collective-permute-start.18 = (bf16[512,2048]{1,0:T(8,128)(2,1)}, bf16[512,2048]{1,0:T(8,128)(2,1)}, u32[]{:S(2)}, u32[]{:S(2)}) collective-permute-start(bf16[512,2048]{1,0:T(8,128)(2,1)} %bitcast.41), channel_id=1, source_target_pairs={{0,96},{16,112},{32,64},{48,80},{1,97},{17,113},{33,65},{49,81},{2... | collective-permute-start | bytes 6291464 | tf_op jit(solution)/shard_map/ppermute | solution.py:598
  190.2 1.6 collective-permute-start.15
  191.9 5.6 %collective-permute-start.16 = (bf16[128,512]{1,0:T(8,128)(2,1)S(1)}, bf16[128,512]{1,0:T(8,128)(2,1)S(1)}, u32[]{:S(2)}, u32[]{:S(2)}) collective-permute-start(bf16[128,512]{1,0:T(8,128)(2,1)S(1)} %add_convert_fusion.4), channel_id=1, source_target_pairs={{0,32},{16,48},{32,0},{48,16},{1,33},{17,49},{33,1},{49,17},{2,34}... | collective-permute-start | bytes 393224 | tf_op jit(solution)/shard_map/ppermute | solution.py:679
  197.5 1.3 collective-permute-start.17
  200.4 22.1 %all-to-all-start.6 = ((bf16[16,16,2048]{2,1,0:T(8,128)(2,1)}), bf16[16,16,2048]{2,1,0:T(8,128)(2,1)S(1)}, u32[]{:S(2)}, u32[]{:S(2)}) async-start(bf16[16,16,2048]{2,1,0:T(8,128)(2,1)} %get-tuple-element.95), calls=%async_computation.6 | async-start | bytes 2097152 | tf_op jit(solution)/shard_map/all_to_all | solution.py:601
  224.0 20.9 %all-to-all-start.7 = ((bf16[16,16,2048]{2,1,0:T(8,128)(2,1)}), bf16[16,16,2048]{2,1,0:T(8,128)(2,1)S(1)}, u32[]{:S(2)}, u32[]{:S(2)}) async-start(bf16[16,16,2048]{2,1,0:T(8,128)(2,1)} %shard_map.136), calls=%async_computation.7 | async-start | bytes 2097152 | tf_op jit(solution)/shard_map/all_to_all | solution.py:601
  227.6 16.5 %collective-permute-start.19 = (bf16[512,512]{1,0:T(8,128)(2,1)}, bf16[512,512]{1,0:T(8,128)(2,1)}, u32[]{:S(2)}, u32[]{:S(2)}) collective-permute-start(bf16[512,512]{1,0:T(8,128)(2,1)} %bitcast.48), channel_id=1, source_target_pairs={{0,96},{16,112},{32,64},{48,80},{1,97},{17,113},{33,65},{49,81},{2... | collective-permute-start | bytes 1572872 | tf_op jit(solution)/shard_map/ppermute | solution.py:598
  253.2 1.6 collective-permute-start.20
  254.8 5.6 %collective-permute-start.21 = (bf16[128,512]{1,0:T(8,128)(2,1)S(1)}, bf16[128,512]{1,0:T(8,128)(2,1)S(1)}, u32[]{:S(2)}, u32[]{:S(2)}) collective-permute-start(bf16[128,512]{1,0:T(8,128)(2,1)S(1)} %add_convert_fusion.3), channel_id=1, source_target_pairs={{0,32},{16,48},{32,0},{48,16},{1,33},{17,49},{33,1},{49,17},{2,34}... | collective-permute-start | bytes 393224 | tf_op jit(solution)/shard_map/ppermute | solution.py:679
  260.4 1.3 collective-permute-start.22
  290.7 5.6 %collective-permute-start.23 = (bf16[16,1280]{1,0:T(8,128)(2,1)S(1)}, bf16[16,1280]{1,0:T(8,128)(2,1)S(1)}, u32[]{:S(2)}, u32[]{:S(2)}) collective-permute-start(bf16[16,1280]{1,0:T(8,128)(2,1)S(1)} %get-tuple-element.107), channel_id=1, source_target_pairs={{0,64},{64,0},{1,65},{65,1},{2,66},{66,2},{3,67},{67,3},{4,68},{68... | collective-permute-start | bytes 122888 | tf_op jit(solution)/shard_map/ppermute | solution.py:871
  (7 other events, 77.4 us)

commit v7 on v6

--- a/solution.py
+++ b/solution.py
@@ -347,7 +347,7 @@
             body(slice(at, at + QB), lanes, at + QB)
         return carry
 
-    lax.fori_loop(0, GROUP_HEADS, one_head, 0, unroll=4)
+    lax.fori_loop(0, GROUP_HEADS, one_head, 0, unroll=8)
 
 
 def clear_unreached(target, tokens):

time: 298 us -> 295 us (0.990)
  Pallas kernels: 44.4 us -> 40.8 us
where the time goes in v7:
time: 295 us; the launch traced here: 293 us
  waiting for transfers between devices  110 us (37%)
  starting transfers between devices  66 us (22%)
  blocking collectives  65.9 us (22%)
  Pallas kernels  40.8 us (14%)
  local copies, waits for them, and re-layouts  7.16 us (2%)
    all_to_all x2, blocking collectives, scatter(): return lax.all_to_all(array, axis, split_axis=0, concat_axis=0, tiled=True)  54.4 us
    ppermute x11, waiting for transfers between devices, swap(): return lax.ppermute(array, ('section', 'mp'), pairs)  42.9 us
    all_to_all x7, waiting for transfers between devices, scatter(): return lax.all_to_all(array, axis, split_axis=0, concat_axis=0, tiled=True)  41 us
    all_to_all x7, starting transfers between devices, scatter(): return lax.all_to_all(array, axis, split_axis=0, concat_axis=0, tiled=True)  36.8 us
    ppermute x11, starting transfers between devices, swap(): return lax.ppermute(array, ('section', 'mp'), pairs)  26.1 us
    ppermute x12, waiting for transfers between devices, beside(): lax.ppermute(array, 'mp', [(i, i ^ distance) for i in range(mp_count)])  21.1 us
    pallas_call x2, Pallas kernels, layer_backward(): pl.pallas_call(backward_kernel, out_shape=shape_of((tokens, width), BF),...  14.7 us
    all_gather x2, blocking collectives, gather(): return lax.all_gather(array, axis, axis=0, tiled=True)  11.6 us
  transfers between devices with their start and end apart: 31, of which 20 were waited for; matrix products, arithmetic and copies ran while one was open for 2% of the time, Pallas kernels for 10%

profile of v7, /device:TPU:6, one launch (start us, length us, event | category | flops | bytes accessed | tf_op | source)
XLA Modules:
  0.0 293.5 jit_solution(5711632719051851613)
XLA Ops:
  3.9 2.8 collective-permute-start.3
  11.9 8.1 %all-to-all-start = ((bf16[16,16,2688]{2,1,0:T(8,128)(2,1)}), bf16[16,16,2688]{2,1,0:T(8,128)(2,1)S(1)}, u32[]{:S(2)}, u32[]{:S(2)}) async-start(bf16[16,16,2688]{2,1,0:T(8,128)(2,1)} %get-tuple-element.56), calls=%async_computation | async-start | bytes 2752512 | tf_op jit(solution)/shard_map/all_to_all | solution.py:601
  25.6 5.8 %all_gather.6.x_ref = bf16[256,512]{1,0:T(8,128)(2,1)S(1)} all-gather(bf16[64,512]{1,0:T(8,128)(2,1)S(1)} %collective-permute-done.3), channel_id=1, replica_groups=mesh['section'=2,'mp'=4,'dp'=16] {'mp'}, dimensions={0}, use_global_device_ids=true | all-gather | bytes 327680 | tf_op jit(solution)/shard_map/all_gather | solution.py:607
  31.4 3.3 %shard_map.124 = bf16[16,16,2688]{2,1,0:T(8,128)(2,1)} custom-call(bf16[256,512]{1,0:T(8,128)(2,1)S(1)} %all_gather.6.x_ref, f32[1,512]{1,0:T(1,128)S(1)} %bitcast.27, bf16[512,2048]{1,0:T(8,128)(2,1)} %bitcast.38, bf16[512,512]{1,0:T(8,128)(2,1)} %bitcast.45, bf16[2048,512]{1,0:T(8,128)(2,1)} %bitcast.34), custom_call_target="tpu_custom_call" | custom-call | flops 704643072 | bytes 6291456 | tf_op jit(solution)/shard_map/pallas_call | solution.py:622
  34.7 6.8 %collective-permute-done.5.refs_0_.refs_1_ = bf16[640,512]{1,0:T(8,128)(2,1)} collective-permute-done((bf16[640,512]{1,0:T(8,128)(2,1)S(1)}, bf16[640,512]{1,0:T(8,128)(2,1)}, u32[]{:S(2)}, u32[]{:S(2)}) %collective-permute-start.5) | collective-permute-done | bytes 655392 | tf_op jit(solution)/shard_map/ppermute | solution.py:598
  41.6 6.9 %all-to-all-start.1 = ((bf16[16,16,2688]{2,1,0:T(8,128)(2,1)}), bf16[16,16,2688]{2,1,0:T(8,128)(2,1)S(1)}, u32[]{:S(2)}, u32[]{:S(2)}) async-start(bf16[16,16,2688]{2,1,0:T(8,128)(2,1)} %shard_map.124), calls=%async_computation.1 | async-start | bytes 2752512 | tf_op jit(solution)/shard_map/all_to_all | solution.py:601
  48.5 2.7 collective-permute-start.9
  52.5 5.8 %all-gather = bf16[1,256,512]{2,1,0:T(8,128)(2,1)S(1)} all-gather(bf16[1,64,512]{2,1,0:T(8,128)(2,1)S(1)} %get-tuple-element.110), channel_id=2, replica_groups=mesh['section'=2,'mp'=4,'dp'=16] {'mp'}, dimensions={1}, use_global_device_ids=true | all-gather | bytes 327680 | tf_op jit(solution)/shard_map/all_gather | solution.py:607
  58.7 9.6 %all-to-all-done.1.parts_ref = bf16[16,16,2688]{2,1,0:T(8,128)(2,1)S(1)} async-done(((bf16[16,16,2688]{2,1,0:T(8,128)(2,1)}), bf16[16,16,2688]{2,1,0:T(8,128)(2,1)S(1)}, u32[]{:S(2)}, u32[]{:S(2)}) %all-to-all-start.1) | async-done | bytes 1376288 | tf_op jit(solution)/shard_map/all_to_all | solution.py:601
  70.0 6.3 %collective-permute-done.6.second_ref = bf16[16,2688]{1,0:T(8,128)(2,1)S(1)} collective-permute-done((bf16[16,2688]{1,0:T(8,128)(2,1)S(1)}, bf16[16,2688]{1,0:T(8,128)(2,1)S(1)}, u32[]{:S(2)}, u32[]{:S(2)}) %collective-permute-start.6) | collective-permute-done | bytes 86048 | tf_op jit(solution)/shard_map/ppermute | solution.py:598
  77.5 3.8 %all-to-all-start.2 = ((bf16[16,16,2688]{2,1,0:T(8,128)(2,1)}), bf16[16,16,2688]{2,1,0:T(8,128)(2,1)S(1)}, u32[]{:S(2)}, u32[]{:S(2)}) async-start(bf16[16,16,2688]{2,1,0:T(8,128)(2,1)} %shard_map.127), calls=%async_computation.2 | async-start | bytes 2752512 | tf_op jit(solution)/shard_map/all_to_all | solution.py:601
  82.7 5.8 %collective-permute-start.8 = (bf16[16,2688]{1,0:T(8,128)(2,1)S(1)}, bf16[16,2688]{1,0:T(8,128)(2,1)S(1)}, u32[]{:S(2)}, u32[]{:S(2)}) collective-permute-start(bf16[16,2688]{1,0:T(8,128)(2,1)S(1)} %shard_map.126), channel_id=1, source_target_pairs={{64,32},{80,48},{96,0},{112,16},{65,33},{81,49},{97,1},{113,17},{6... | collective-permute-start | bytes 258056 | tf_op jit(solution)/shard_map/ppermute | solution.py:598
  88.5 7.3 %collective-permute-done.8.first_ref = bf16[16,2688]{1,0:T(8,128)(2,1)S(1)} collective-permute-done((bf16[16,2688]{1,0:T(8,128)(2,1)S(1)}, bf16[16,2688]{1,0:T(8,128)(2,1)S(1)}, u32[]{:S(2)}, u32[]{:S(2)}) %collective-permute-start.8) | collective-permute-done | bytes 86048 | tf_op jit(solution)/shard_map/ppermute | solution.py:598
  95.8 6.4 %collective-permute-start.11 = (bf16[512,512]{1,0:T(8,128)(2,1)S(1)}, bf16[512,512]{1,0:T(8,128)(2,1)}, u32[]{:S(2)}, u32[]{:S(2)}) collective-permute-start(bf16[512,512]{1,0:T(8,128)(2,1)S(1)} %bitcast.50), channel_id=1, source_target_pairs={{64,32},{80,48},{96,0},{112,16},{65,33},{81,49},{97,1},{113,17},{6... | collective-permute-start | bytes 1572872 | tf_op jit(solution)/shard_map/ppermute | solution.py:598
  103.3 7.0 %all-to-all-start.3 = ((bf16[16,16,2048]{2,1,0:T(8,128)(2,1)}), bf16[16,16,2048]{2,1,0:T(8,128)(2,1)}, u32[]{:S(2)}, u32[]{:S(2)}) async-start(bf16[16,16,2048]{2,1,0:T(8,128)(2,1)} %shard_map.128), calls=%async_computation.3 | async-start | bytes 2097152 | tf_op jit(solution)/shard_map/all_to_all | solution.py:601
  111.2 4.2 %shard_map.129 = bf16[256,512]{1,0:T(8,128)(2,1)S(1)} custom-call(s32[2,3]{1,0:T(2,128)S(1)} %copy-done.2, bf16[256,2688]{1,0:T(8,128)(2,1)S(1)} %bitcast.19, bf16[2048,512]{1,0:T(8,128)(2,1)} %bitcast.35, bf16[640,512]{1,0:T(8,128)(2,1)} %collective-permute-done.5.refs_0_.refs_1_, bf16[640,512]{1,0:T(8,128)(2,1)} %collective-permute-done.7.refs_1_.refs_2_, ...), custom_call_target="tpu_custom_call" | custom-call | flops 805306368 | bytes 4194304 | tf_op jit(solution)/shard_map/pallas_call | solution.py:752
  119.0 3.8 %collective-permute-done.13.across_ref = bf16[128,512]{1,0:T(8,128)(2,1)S(1)} collective-permute-done((bf16[128,512]{1,0:T(8,128)(2,1)S(1)}, bf16[128,512]{1,0:T(8,128)(2,1)S(1)}, u32[]{:S(2)}, u32[]{:S(2)}) %collective-permute-start.13) | collective-permute-done | bytes 131104 | tf_op jit(solution)/shard_map/ppermute | solution.py:679
  125.8 28.1 %all_to_all.45.parts_ref = bf16[16,16,2688]{2,1,0:T(8,128)(2,1)S(1)} all-to-all(bf16[16,16,2688]{2,1,0:T(8,128)(2,1)} %shard_map.131), channel_id=1, replica_groups=mesh['section'=2,'mp'=4,'dp'=16] {'dp'}, dimensions={0} | all-to-all | bytes 2752512 | tf_op jit(solution)/shard_map/all_to_all | solution.py:601
  155.7 3.7 %all-to-all-start.5 = ((bf16[16,16,2688]{2,1,0:T(8,128)(2,1)}), bf16[16,16,2688]{2,1,0:T(8,128)(2,1)S(1)}, u32[]{:S(2)}, u32[]{:S(2)}) async-start(bf16[16,16,2688]{2,1,0:T(8,128)(2,1)} %shard_map.132), calls=%async_computation.5 | async-start | bytes 2752512 | tf_op jit(solution)/shard_map/all_to_all | solution.py:601
  160.7 19.6 %all-to-all-done.5 = bf16[16,16,2688]{2,1,0:T(8,128)(2,1)S(1)} async-done(((bf16[16,16,2688]{2,1,0:T(8,128)(2,1)}), bf16[16,16,2688]{2,1,0:T(8,128)(2,1)S(1)}, u32[]{:S(2)}, u32[]{:S(2)}) %all-to-all-start.5) | async-done | bytes 1376288 | tf_op jit(solution)/shard_map/all_to_all | solution.py:601
  180.3 7.7 %shard_map.133 = bf16[256,512]{1,0:T(8,128)(2,1)S(1)} custom-call(s32[2,3]{1,0:T(2,128)S(1)} %copy-done.2, bf16[256,2688]{1,0:T(8,128)(2,1)S(1)} %bitcast.21, bf16[256,2048]{1,0:T(8,128)(2,1)} %bitcast.7.grads_ref, bf16[512,2048]{1,0:T(8,128)(2,1)} %collective-permute-done.9.refs_0_.wq0_ref, bf16[512,2048]{1,0:T(8,128)(2,1)} %bitcast.42, ...), custom_call_target="tpu_custom_call" | custom-call | flops 1610612736 | bytes 6291456 | tf_op jit(solution)/shard_map/pallas_call | solution.py:798
  191.6 3.7 %collective-permute-done.16.across_ref = bf16[128,512]{1,0:T(8,128)(2,1)S(1)} collective-permute-done((bf16[128,512]{1,0:T(8,128)(2,1)S(1)}, bf16[128,512]{1,0:T(8,128)(2,1)S(1)}, u32[]{:S(2)}, u32[]{:S(2)}) %collective-permute-start.16) | collective-permute-done | bytes 131104 | tf_op jit(solution)/shard_map/ppermute | solution.py:679
  198.2 3.7 %all-to-all-start.6 = ((bf16[16,16,2048]{2,1,0:T(8,128)(2,1)}), bf16[16,16,2048]{2,1,0:T(8,128)(2,1)S(1)}, u32[]{:S(2)}, u32[]{:S(2)}) async-start(bf16[16,16,2048]{2,1,0:T(8,128)(2,1)} %get-tuple-element.95), calls=%async_computation.6 | async-start | bytes 2097152 | tf_op jit(solution)/shard_map/all_to_all | solution.py:601
  201.9 7.5 %collective-permute-done.18.wq1_ref = bf16[512,2048]{1,0:T(8,128)(2,1)} collective-permute-done((bf16[512,2048]{1,0:T(8,128)(2,1)}, bf16[512,2048]{1,0:T(8,128)(2,1)}, u32[]{:S(2)}, u32[]{:S(2)}) %collective-permute-start.18) | collective-permute-done | bytes 2097184 | tf_op jit(solution)/shard_map/ppermute | solution.py:598
  209.4 10.9 %all-to-all-done.6.parts_ref = bf16[16,16,2048]{2,1,0:T(8,128)(2,1)S(1)} async-done(((bf16[16,16,2048]{2,1,0:T(8,128)(2,1)}), bf16[16,16,2048]{2,1,0:T(8,128)(2,1)S(1)}, u32[]{:S(2)}, u32[]{:S(2)}) %all-to-all-start.6) | async-done | bytes 1048608 | tf_op jit(solution)/shard_map/all_to_all | solution.py:601
  221.8 3.7 %all-to-all-start.7 = ((bf16[16,16,2048]{2,1,0:T(8,128)(2,1)}), bf16[16,16,2048]{2,1,0:T(8,128)(2,1)S(1)}, u32[]{:S(2)}, u32[]{:S(2)}) async-start(bf16[16,16,2048]{2,1,0:T(8,128)(2,1)} %shard_map.136), calls=%async_computation.7 | async-start | bytes 2097152 | tf_op jit(solution)/shard_map/all_to_all | solution.py:601
  226.9 14.9 %collective-permute-done.19.wkv1_ref = bf16[512,512]{1,0:T(8,128)(2,1)} collective-permute-done((bf16[512,512]{1,0:T(8,128)(2,1)}, bf16[512,512]{1,0:T(8,128)(2,1)}, u32[]{:S(2)}, u32[]{:S(2)}) %collective-permute-start.19) | collective-permute-done | bytes 524320 | tf_op jit(solution)/shard_map/ppermute | solution.py:598
  242.7 7.0 %shard_map.137 = bf16[256,512]{1,0:T(8,128)(2,1)S(1)} custom-call(s32[2,3]{1,0:T(2,128)S(1)} %copy-done.2, bf16[256,2688]{1,0:T(8,128)(2,1)S(1)} %bitcast.20, bf16[256,2048]{1,0:T(8,128)(2,1)S(1)} %bitcast.22, bf16[512,2048]{1,0:T(8,128)(2,1)} %bitcast.43, bf16[512,2048]{1,0:T(8,128)(2,1)} %collective-permute-done.18.wq1_ref, bf16[512,512]{1,0:T(8,128)(2,1)} %bitcast.49, ...), custom_call_target="tpu_custom_call" | custom-call | flops 1610612736 | bytes 6291456 | tf_op jit(solution)/shard_map/pallas_call | solution.py:798
  251.7 5.2 %collective-permute-done.21.across_ref = bf16[128,512]{1,0:T(8,128)(2,1)S(1)} collective-permute-done((bf16[128,512]{1,0:T(8,128)(2,1)S(1)}, bf16[128,512]{1,0:T(8,128)(2,1)S(1)}, u32[]{:S(2)}, u32[]{:S(2)}) %collective-permute-start.21) | collective-permute-done | bytes 131104 | tf_op jit(solution)/shard_map/ppermute | solution.py:679
  258.3 2.5 shard_map.138
  260.7 26.2 %all_to_all.46.parts_ref = bf16[16,2,16,1280]{3,2,1,0:T(8,128)(2,1)S(1)} all-to-all(bf16[16,2,16,1280]{3,2,1,0:T(8,128)(2,1)S(1)} %get-tuple-element.105), channel_id=1, replica_groups=mesh['section'=2,'mp'=4,'dp'=16] {'dp'}, dimensions={0} | all-to-all | bytes 2621440 | tf_op jit(solution)/shard_map/all_to_all | solution.py:601
  287.2 5.5 %collective-permute-done.23 = bf16[16,1280]{1,0:T(8,128)(2,1)S(1)} collective-permute-done((bf16[16,1280]{1,0:T(8,128)(2,1)S(1)}, bf16[16,1280]{1,0:T(8,128)(2,1)S(1)}, u32[]{:S(2)}, u32[]{:S(2)}) %collective-permute-start.23) | collective-permute-done | bytes 40992 | tf_op jit(solution)/shard_map/ppermute | solution.py:871
  (80 shorter events, 46.0 us)
Async XLA Ops:
  1.5 8.7 %collective-permute-start = (bf16[64,512]{1,0:T(8,128)(2,1)S(1)}, bf16[64,512]{1,0:T(8,128)(2,1)S(1)}, u32[]{:S(2)}, u32[]{:S(2)}) collective-permute-start(bf16[64,512]{1,0:T(8,128)(2,1)S(1)} %get-tuple-element.111.mine_ref), channel_id=1, source_target_pairs={{0,16},{16,0},{32,48},{48,32},{1,17},{17,1},{33,49},{49,33},{2,18}... | collective-permute-start | bytes 196616 | tf_op jit(solution)/shard_map/ppermute | solution.py:679
  1.6 8.6 %collective-permute-start.1 = (bf16[64,512]{1,0:T(8,128)(2,1)S(1)}, bf16[64,512]{1,0:T(8,128)(2,1)S(1)}, u32[]{:S(2)}, u32[]{:S(2)}) collective-permute-start(bf16[64,512]{1,0:T(8,128)(2,1)S(1)} %get-tuple-element.111.mine_ref), channel_id=1, source_target_pairs={{0,32},{16,48},{32,0},{48,16},{1,33},{17,49},{33,1},{49,17},{2,34}... | collective-permute-start | bytes 196616 | tf_op jit(solution)/shard_map/ppermute | solution.py:679
  2.5 7.7 %collective-permute-start.2 = (bf16[64,512]{1,0:T(8,128)(2,1)S(1)}, bf16[64,512]{1,0:T(8,128)(2,1)S(1)}, u32[]{:S(2)}, u32[]{:S(2)}) collective-permute-start(bf16[64,512]{1,0:T(8,128)(2,1)S(1)} %get-tuple-element.111.mine_ref), channel_id=1, source_target_pairs={{0,48},{16,32},{32,16},{48,0},{1,49},{17,33},{33,17},{49,1},{2,50}... | collective-permute-start | bytes 196616 | tf_op jit(solution)/shard_map/ppermute | solution.py:679
  3.5 8.4 %collective-permute-start.4 = (f32[1,512]{1,0:T(1,128)}, f32[1,512]{1,0:T(1,128)S(1)}, u32[]{:S(2)}, u32[]{:S(2)}) collective-permute-start(f32[1,512]{1,0:T(1,128)} %bitcast.25), channel_id=1, source_target_pairs={{0,96},{16,112},{32,64},{48,80},{64,32},{80,48},{96,0},{112,16},{1... | collective-permute-start | bytes 6152 | tf_op jit(solution)/shard_map/ppermute | solution.py:598
  3.9 8.0 %collective-permute-start.3 = (bf16[64,512]{1,0:T(8,128)(2,1)S(1)}, bf16[64,512]{1,0:T(8,128)(2,1)S(1)}, u32[]{:S(2)}, u32[]{:S(2)}) collective-permute-start(bf16[64,512]{1,0:T(8,128)(2,1)S(1)} %bitcast.52), channel_id=1, source_target_pairs={{0,96},{16,112},{32,64},{48,80},{64,32},{80,48},{96,0},{112,16},{1... | collective-permute-start | bytes 196616 | tf_op jit(solution)/shard_map/ppermute | solution.py:598
  11.9 29.7 %all-to-all-start = ((bf16[16,16,2688]{2,1,0:T(8,128)(2,1)}), bf16[16,16,2688]{2,1,0:T(8,128)(2,1)S(1)}, u32[]{:S(2)}, u32[]{:S(2)}) async-start(bf16[16,16,2688]{2,1,0:T(8,128)(2,1)} %get-tuple-element.56), calls=%async_computation | async-start | bytes 2752512 | tf_op jit(solution)/shard_map/all_to_all | solution.py:601
  22.2 19.3 %collective-permute-start.5 = (bf16[640,512]{1,0:T(8,128)(2,1)S(1)}, bf16[640,512]{1,0:T(8,128)(2,1)}, u32[]{:S(2)}, u32[]{:S(2)}) collective-permute-start(bf16[640,512]{1,0:T(8,128)(2,1)S(1)} %get-tuple-element.109), channel_id=1, source_target_pairs={{0,96},{16,112},{32,64},{48,80},{1,97},{17,113},{33,65},{49,81},{2... | collective-permute-start | bytes 1966088 | tf_op jit(solution)/shard_map/ppermute | solution.py:598
  41.6 26.6 %all-to-all-start.1 = ((bf16[16,16,2688]{2,1,0:T(8,128)(2,1)}), bf16[16,16,2688]{2,1,0:T(8,128)(2,1)S(1)}, u32[]{:S(2)}, u32[]{:S(2)}) async-start(bf16[16,16,2688]{2,1,0:T(8,128)(2,1)} %shard_map.124), calls=%async_computation.1 | async-start | bytes 2752512 | tf_op jit(solution)/shard_map/all_to_all | solution.py:601
  48.5 54.8 %collective-permute-start.9 = (bf16[512,2048]{1,0:T(8,128)(2,1)}, bf16[512,2048]{1,0:T(8,128)(2,1)}, u32[]{:S(2)}, u32[]{:S(2)}) collective-permute-start(bf16[512,2048]{1,0:T(8,128)(2,1)} %bitcast.39), channel_id=1, source_target_pairs={{64,32},{80,48},{96,0},{112,16},{65,33},{81,49},{97,1},{113,17},{6... | collective-permute-start | bytes 6291464 | tf_op jit(solution)/shard_map/ppermute | solution.py:598
  51.2 26.3 %collective-permute-start.7 = (bf16[640,512]{1,0:T(8,128)(2,1)}, bf16[640,512]{1,0:T(8,128)(2,1)}, u32[]{:S(2)}, u32[]{:S(2)}) collective-permute-start(bf16[640,512]{1,0:T(8,128)(2,1)} %get-tuple-element.65), channel_id=1, source_target_pairs={{0,96},{16,112},{32,64},{48,80},{1,97},{17,113},{33,65},{49,81},{2... | collective-permute-start | bytes 1966088 | tf_op jit(solution)/shard_map/ppermute | solution.py:598
  68.7 7.6 %collective-permute-start.6 = (bf16[16,2688]{1,0:T(8,128)(2,1)S(1)}, bf16[16,2688]{1,0:T(8,128)(2,1)S(1)}, u32[]{:S(2)}, u32[]{:S(2)}) collective-permute-start(bf16[16,2688]{1,0:T(8,128)(2,1)S(1)} %shard_map.126), channel_id=1, source_target_pairs={{0,96},{16,112},{32,64},{48,80},{1,97},{17,113},{33,65},{49,81},{2... | collective-permute-start | bytes 258056 | tf_op jit(solution)/shard_map/ppermute | solution.py:598
  77.5 25.8 %all-to-all-start.2 = ((bf16[16,16,2688]{2,1,0:T(8,128)(2,1)}), bf16[16,16,2688]{2,1,0:T(8,128)(2,1)S(1)}, u32[]{:S(2)}, u32[]{:S(2)}) async-start(bf16[16,16,2688]{2,1,0:T(8,128)(2,1)} %shard_map.127), calls=%async_computation.2 | async-start | bytes 2752512 | tf_op jit(solution)/shard_map/all_to_all | solution.py:601
  81.4 29.9 %copy-start.2 = (s32[2,3]{1,0:T(2,128)S(1)}, s32[2,3]{1,0:T(2,128)}, u32[]{:S(2)}) copy-start(s32[2,3]{1,0:T(2,128)} %seq_ref.5) | copy-start | bytes 76
  81.4 29.0 %collective-permute-start.10 = (bf16[768,512]{1,0:T(8,128)(2,1)}, bf16[768,512]{1,0:T(8,128)(2,1)S(1)}, u32[]{:S(2)}, u32[]{:S(2)}) collective-permute-start(bf16[768,512]{1,0:T(8,128)(2,1)} %slice.11), channel_id=1, source_target_pairs={{0,96},{16,112},{32,64},{48,80},{1,97},{17,113},{33,65},{49,81},{2... | collective-permute-start | bytes 2359304 | tf_op jit(solution)/shard_map/ppermute | solution.py:598
  82.7 13.1 %collective-permute-start.8 = (bf16[16,2688]{1,0:T(8,128)(2,1)S(1)}, bf16[16,2688]{1,0:T(8,128)(2,1)S(1)}, u32[]{:S(2)}, u32[]{:S(2)}) collective-permute-start(bf16[16,2688]{1,0:T(8,128)(2,1)S(1)} %shard_map.126), channel_id=1, source_target_pairs={{64,32},{80,48},{96,0},{112,16},{65,33},{81,49},{97,1},{113,17},{6... | collective-permute-start | bytes 258056 | tf_op jit(solution)/shard_map/ppermute | solution.py:598
  95.8 19.6 %collective-permute-start.11 = (bf16[512,512]{1,0:T(8,128)(2,1)S(1)}, bf16[512,512]{1,0:T(8,128)(2,1)}, u32[]{:S(2)}, u32[]{:S(2)}) collective-permute-start(bf16[512,512]{1,0:T(8,128)(2,1)S(1)} %bitcast.50), channel_id=1, source_target_pairs={{64,32},{80,48},{96,0},{112,16},{65,33},{81,49},{97,1},{113,17},{6... | collective-permute-start | bytes 1572872 | tf_op jit(solution)/shard_map/ppermute | solution.py:598
  103.3 22.4 %all-to-all-start.3 = ((bf16[16,16,2048]{2,1,0:T(8,128)(2,1)}), bf16[16,16,2048]{2,1,0:T(8,128)(2,1)}, u32[]{:S(2)}, u32[]{:S(2)}) async-start(bf16[16,16,2048]{2,1,0:T(8,128)(2,1)} %shard_map.128), calls=%async_computation.3 | async-start | bytes 2097152 | tf_op jit(solution)/shard_map/all_to_all | solution.py:601
  115.5 1.6 collective-permute-start.12
  117.1 5.6 %collective-permute-start.13 = (bf16[128,512]{1,0:T(8,128)(2,1)S(1)}, bf16[128,512]{1,0:T(8,128)(2,1)S(1)}, u32[]{:S(2)}, u32[]{:S(2)}) collective-permute-start(bf16[128,512]{1,0:T(8,128)(2,1)S(1)} %add_convert_fusion.5), channel_id=1, source_target_pairs={{0,32},{16,48},{32,0},{48,16},{1,33},{17,49},{33,1},{49,17},{2,34}... | collective-permute-start | bytes 393224 | tf_op jit(solution)/shard_map/ppermute | solution.py:679
  122.7 1.3 collective-permute-start.14
  155.7 24.7 %all-to-all-start.5 = ((bf16[16,16,2688]{2,1,0:T(8,128)(2,1)}), bf16[16,16,2688]{2,1,0:T(8,128)(2,1)S(1)}, u32[]{:S(2)}, u32[]{:S(2)}) async-start(bf16[16,16,2688]{2,1,0:T(8,128)(2,1)} %shard_map.132), calls=%async_computation.5 | async-start | bytes 2752512 | tf_op jit(solution)/shard_map/all_to_all | solution.py:601
  159.4 50.0 %collective-permute-start.18 = (bf16[512,2048]{1,0:T(8,128)(2,1)}, bf16[512,2048]{1,0:T(8,128)(2,1)}, u32[]{:S(2)}, u32[]{:S(2)}) collective-permute-start(bf16[512,2048]{1,0:T(8,128)(2,1)} %bitcast.41), channel_id=1, source_target_pairs={{0,96},{16,112},{32,64},{48,80},{1,97},{17,113},{33,65},{49,81},{2... | collective-permute-start | bytes 6291464 | tf_op jit(solution)/shard_map/ppermute | solution.py:598
  188.1 1.6 collective-permute-start.15
  189.7 5.6 %collective-permute-start.16 = (bf16[128,512]{1,0:T(8,128)(2,1)S(1)}, bf16[128,512]{1,0:T(8,128)(2,1)S(1)}, u32[]{:S(2)}, u32[]{:S(2)}) collective-permute-start(bf16[128,512]{1,0:T(8,128)(2,1)S(1)} %add_convert_fusion.4), channel_id=1, source_target_pairs={{0,32},{16,48},{32,0},{48,16},{1,33},{17,49},{33,1},{49,17},{2,34}... | collective-permute-start | bytes 393224 | tf_op jit(solution)/shard_map/ppermute | solution.py:679
  195.3 1.3 collective-permute-start.17
  198.2 22.1 %all-to-all-start.6 = ((bf16[16,16,2048]{2,1,0:T(8,128)(2,1)}), bf16[16,16,2048]{2,1,0:T(8,128)(2,1)S(1)}, u32[]{:S(2)}, u32[]{:S(2)}) async-start(bf16[16,16,2048]{2,1,0:T(8,128)(2,1)} %get-tuple-element.95), calls=%async_computation.6 | async-start | bytes 2097152 | tf_op jit(solution)/shard_map/all_to_all | solution.py:601
  221.8 20.9 %all-to-all-start.7 = ((bf16[16,16,2048]{2,1,0:T(8,128)(2,1)}), bf16[16,16,2048]{2,1,0:T(8,128)(2,1)S(1)}, u32[]{:S(2)}, u32[]{:S(2)}) async-start(bf16[16,16,2048]{2,1,0:T(8,128)(2,1)} %shard_map.136), calls=%async_computation.7 | async-start | bytes 2097152 | tf_op jit(solution)/shard_map/all_to_all | solution.py:601
  225.4 16.5 %collective-permute-start.19 = (bf16[512,512]{1,0:T(8,128)(2,1)}, bf16[512,512]{1,0:T(8,128)(2,1)}, u32[]{:S(2)}, u32[]{:S(2)}) collective-permute-start(bf16[512,512]{1,0:T(8,128)(2,1)} %bitcast.48), channel_id=1, source_target_pairs={{0,96},{16,112},{32,64},{48,80},{1,97},{17,113},{33,65},{49,81},{2... | collective-permute-start | bytes 1572872 | tf_op jit(solution)/shard_map/ppermute | solution.py:598
  249.6 1.6 collective-permute-start.20
  251.3 5.6 %collective-permute-start.21 = (bf16[128,512]{1,0:T(8,128)(2,1)S(1)}, bf16[128,512]{1,0:T(8,128)(2,1)S(1)}, u32[]{:S(2)}, u32[]{:S(2)}) collective-permute-start(bf16[128,512]{1,0:T(8,128)(2,1)S(1)} %add_convert_fusion.3), channel_id=1, source_target_pairs={{0,32},{16,48},{32,0},{48,16},{1,33},{17,49},{33,1},{49,17},{2,34}... | collective-permute-start | bytes 393224 | tf_op jit(solution)/shard_map/ppermute | solution.py:679
  256.9 1.3 collective-permute-start.22
  287.1 5.6 %collective-permute-start.23 = (bf16[16,1280]{1,0:T(8,128)(2,1)S(1)}, bf16[16,1280]{1,0:T(8,128)(2,1)S(1)}, u32[]{:S(2)}, u32[]{:S(2)}) collective-permute-start(bf16[16,1280]{1,0:T(8,128)(2,1)S(1)} %get-tuple-element.107), channel_id=1, source_target_pairs={{0,64},{64,0},{1,65},{65,1},{2,66},{66,2},{3,67},{67,3},{4,68},{68... | collective-permute-start | bytes 122888 | tf_op jit(solution)/shard_map/ppermute | solution.py:871
  (7 other events, 73.4 us)
